TPU v7x, 512 devices: a whole 4x8x8 slice. The times are simulated.
512 devices in a mesh: dp: 4 (over x), seq: 128 (over y, z, core).
Axes of the slice: x: 4, y: 8, z: 8, core: 2. Of those that a mesh axis runs over, the one named last changes fastest.
Arguments:
- feats: bfloat16 [262144, 512], P(('dp', 'seq')), parts along dimension 0, may hold values from -6 to 6
- order: int32 [262144], P(('dp', 'seq')), parts along dimension 0, may hold values from 0 to 65535, as said below
- norm_gain: float32 [512], replicated, may hold values from 0.5 to 2
- norm_bias: float32 [512], replicated, may hold values from -3 to 3
- qkv_weight: bfloat16 [512, 1536], replicated, may hold values from -12 to 12
- qkv_bias: float32 [1536], replicated, may hold values from -3 to 3
- proj_weight: bfloat16 [512, 512], replicated, may hold values from -1 to 1
- proj_bias: float32 [512], replicated, may hold values from -1.2 to 1.2
Outputs:
- update: bfloat16 [262144, 512], P(('dp', 'seq')), parts along dimension 0
There are 4 independent parts, one for each index of `dp`. A program takes and returns all parts, laid end to end along the dimension named above; an argument that names none is the same for every part. Nothing has to cross between parts.
Inputs may be any that keep to these rules, and one draw needn't show every extreme that they name: order is a permutation of the 65536 stored rows. Of the 512 sequence positions of one device of seq, at most 8 come from the stored rows of any one device, and that bound is met in every draw.
All inputs are finite; a program needn't handle non-finite values.
Results may differ from a plain program's by a relative error of at most 0.0065.
The roundings to bfloat16 on the way count: a program that leaves them out, or rounds other values in their place, can miss the bound.
Values may be sent and summed in bfloat16 or wider, within the bound.
No kernel may reach another device: no remote copies, remote signals or barrier semaphores. Data moves between devices by JAX's collectives and lax.ppermute only.
A program may use at most 64 MiB of HBM per device.

v0:
```python
import jax
import jax.numpy as jnp
from jax import lax
from jax.sharding import PartitionSpec as P

HEAD_DIM = 16


def with_halo(block, sides, width):
    for axis, dim in sides:
        count = lax.axis_size(axis)
        forward = [(i, i + 1) for i in range(count - 1)]
        forward.append((count - 1, 0))
        backward = [(target, source) for source, target in forward]
        low = lax.ppermute(
            lax.slice_in_dim(block, block.shape[dim] - width, None, axis=dim), axis, forward
        )
        high = lax.ppermute(lax.slice_in_dim(block, 0, width, axis=dim), axis, backward)
        block = jnp.concatenate([low, block, high], axis=dim)
    return block


def layer_norm(inputs, norm_gain, norm_bias):
    values = inputs.astype(jnp.float32)
    center = jnp.mean(values, axis=-1, keepdims=True)
    spread = jnp.mean(jnp.square(values - center), axis=-1, keepdims=True)
    return ((values - center) * lax.rsqrt(spread + 1e-05) * norm_gain + norm_bias).astype(
        jnp.bfloat16
    )


def attend(query_block, key_block, value_block):
    query_count = query_block.shape[0]
    key_count = key_block.shape[0]
    group_count = query_block.shape[1] // (4 * HEAD_DIM)

    def arrange(source_block, count):
        return source_block.reshape(count, group_count, 4, HEAD_DIM).transpose(1, 0, 2, 3)

    def one_group(operands):
        query_heads, key_heads, value_heads = operands
        scores = jnp.einsum(
            "qhd,khd->hqk", query_heads, key_heads, preferred_element_type=jnp.float32
        ) * HEAD_DIM ** (-0.5)
        highest = jnp.max(scores, axis=-1, keepdims=True)
        expanded = jnp.exp(scores - highest)
        weights = (expanded / jnp.sum(expanded, axis=-1, keepdims=True)).astype(jnp.bfloat16)
        mixed = jnp.einsum("hqk,khd->qhd", weights, value_heads, preferred_element_type=jnp.float32)
        return mixed.astype(jnp.bfloat16)

    outputs = lax.map(
        one_group,
        (
            arrange(query_block, query_count),
            arrange(key_block, key_count),
            arrange(value_block, key_count),
        ),
    )
    return outputs.transpose(1, 0, 2, 3).reshape(query_count, -1)


def per_device(feats, order, norm_gain, norm_bias, qkv_weight, qkv_bias, proj_weight, proj_bias):
    row_count, feature_width = feats.shape
    peer_count = lax.axis_size("seq")
    capacity = 2 * row_count // peer_count
    holder = order // row_count
    local_row = order % row_count
    matches = holder[:, None] == jnp.arange(peer_count, dtype=jnp.int32)[None, :]
    counts = jnp.sum(matches.astype(jnp.int32), axis=0)
    starts = jnp.cumsum(counts) - counts
    first_slot = jnp.sum(jnp.where(matches, starts[None, :], 0), axis=1)
    ranking = jnp.argsort(holder, stable=True)
    positions = jnp.arange(row_count, dtype=jnp.int32)
    slot_sorted = holder[ranking] * capacity + positions - first_slot[ranking]
    slot_of_row = jnp.zeros(row_count, jnp.int32).at[ranking].set(slot_sorted)
    wanted = jnp.full((peer_count * capacity,), row_count, jnp.int32).at[slot_of_row].set(local_row)
    asked = lax.all_to_all(
        wanted.reshape(peer_count, capacity), "seq", split_axis=0, concat_axis=0, tiled=True
    )
    present = asked < row_count
    picked = jnp.where(
        present[:, :, None], feats[jnp.minimum(asked, row_count - 1)], jnp.zeros((), jnp.bfloat16)
    )
    arrived = lax.all_to_all(picked, "seq", split_axis=0, concat_axis=0, tiled=True)
    seq_feats = arrived.reshape(peer_count * capacity, feature_width)[slot_of_row]
    normed = layer_norm(seq_feats, norm_gain, norm_bias)
    projected = (jnp.dot(normed, qkv_weight, preferred_element_type=jnp.float32) + qkv_bias).astype(
        jnp.bfloat16
    )
    half_width = feature_width // 2
    half_rows = row_count // 2
    far_pairs = jnp.concatenate(
        [
            projected[:, feature_width + half_width : 2 * feature_width],
            projected[:, 2 * feature_width + half_width :],
        ],
        axis=1,
    )
    extended = with_halo(far_pairs, (("seq", 0),), row_count)
    near = attend(
        projected[:, :half_width],
        projected[:, feature_width : feature_width + half_width],
        projected[:, 2 * feature_width : 2 * feature_width + half_width],
    )
    lower = extended[row_count - half_rows : row_count + half_rows]
    upper = extended[row_count + half_rows : row_count + 3 * half_rows]
    far_queries = projected[:, half_width:feature_width]
    far_first = attend(far_queries[:half_rows], lower[:, :half_width], lower[:, half_width:])
    far_second = attend(far_queries[half_rows:], upper[:, :half_width], upper[:, half_width:])
    attended = jnp.concatenate([near, jnp.concatenate([far_first, far_second], axis=0)], axis=1)
    update_seq = (
        jnp.dot(attended, proj_weight, preferred_element_type=jnp.float32) + proj_bias
    ).astype(jnp.bfloat16)
    outgoing = (
        jnp.zeros((peer_count * capacity, feature_width), jnp.bfloat16)
        .at[slot_of_row]
        .set(update_seq)
    )
    returned = lax.all_to_all(
        outgoing.reshape(peer_count, capacity, feature_width),
        "seq",
        split_axis=0,
        concat_axis=0,
        tiled=True,
    )
    return (
        jnp.zeros_like(feats)
        .at[asked.reshape(-1)]
        .set(returned.reshape(-1, feature_width), mode="drop")
    )


def solution(mesh):
    return jax.shard_map(
        per_device,
        mesh=mesh,
        in_specs=(P(("dp", "seq"), None), P(("dp", "seq")), P(), P(), P(), P(), P(), P()),
        out_specs=P(("dp", "seq"), None),
        check_vma=False,
    )
```

profile of v0, /device:TPU:1, one launch (start us, length us, event | category | flops | bytes accessed | tf_op | source)
XLA Modules:
  0.0 205.9 jit_solution(3877467625583534664)
XLA Ops:
  1.0 3.8 %sort.17 = (s32[512]{0:T(512)}, s32[512]{0:T(512)S(1)}) sort(s32[512]{0:T(512)S(1)} %get-tuple-element.139, s32[512]{0:T(512)S(1)} %iota.11), dimensions={0}, to_apply=%region_0.1 | sort | flops 4608 | bytes 8192 | tf_op jit(solution)/shard_map/jit(argsort)/sort | solution.py:72
  5.4 3.5 %gather_fusion = s32[512]{0:T(512)S(1)} fusion(s32[512]{0:T(512)S(1)} %get-tuple-element.139, s32[1024]{0:T(1024)S(1)} %pad_clamp_fusion.1), kind=kCustom, calls=%fused_computation | custom fusion | bytes 6144 | tf_op jit(solution)/shard_map/gather | solution.py:74
  8.9 3.5 %gather_fusion.1 = s32[512]{0:T(512)S(1)} fusion(s32[512]{0:T(512)S(1)} %select_reduce_fusion, s32[1024]{0:T(1024)S(1)} %pad_clamp_fusion.1), kind=kCustom, calls=%fused_computation.1 | custom fusion | bytes 6144 | tf_op jit(solution)/shard_map/gather | solution.py:74
  14.9 2.4 %scatter_custom_fusion.1 = s32[1024]{0:T(1024)S(1)} fusion(s32[512]{0:T(512)S(1)} %compare_select_fusion.2, s32[512]{0:T(512)S(1)} %get-tuple-element.138, s32[]{:T(128)} %constant.95.clone.1), kind=kCustom, calls=%fused_computation.150 | custom fusion | bytes 4100 | tf_op jit(solution)/shard_map/scatter | solution.py:76
  17.4 29.7 %all_to_all.19 = s32[128,1,8]{2,1,0:T(1,128)S(1)} all-to-all(s32[128,1,8]{2,1,0:T(1,128)S(1)} %bitcast.198), channel_id=1, replica_groups=mesh['dp'=4,'seq'=128] {'seq'}, dimensions={0} | all-to-all | bytes 8192 | tf_op jit(solution)/shard_map/all_to_all | solution.py:77
  48.9 4.0 %gather_fusion.2 = bf16[1024,512]{1,0:T(8,128)(2,1)S(1)} fusion(bf16[512,512]{1,0:T(8,128)(2,1)S(1)} %copy-done.1, s32[1024]{0:T(1024)S(1)} %broadcast_clamp_fusion), kind=kCustom, calls=%fused_computation.2 | custom fusion | bytes 2101248 | tf_op jit(solution)/shard_map/gather | solution.py:82
  54.0 5.7 %all-to-all-start.1 = ((bf16[128,8,512]{2,1,0:T(8,128)(2,1)}), bf16[128,8,512]{2,1,0:T(8,128)(2,1)S(1)}, u32[]{:S(2)}, u32[]{:S(2)}) async-start(bf16[128,8,512]{2,1,0:T(8,128)(2,1)} %bitcast_select_fusion), calls=%async_computation.1 | async-start | bytes 2097152 | tf_op jit(solution)/shard_map/all_to_all | solution.py:84
  59.8 30.4 %all-to-all-done.1 = bf16[128,8,512]{2,1,0:T(8,128)(2,1)S(1)} async-done(((bf16[128,8,512]{2,1,0:T(8,128)(2,1)}), bf16[128,8,512]{2,1,0:T(8,128)(2,1)S(1)}, u32[]{:S(2)}, u32[]{:S(2)}) %all-to-all-start.1) | async-done | bytes 1048608 | tf_op jit(solution)/shard_map/all_to_all | solution.py:84
  95.9 3.7 %collective-permute-start = (bf16[512,512]{1,0:T(8,128)(2,1)}, bf16[512,512]{1,0:T(8,128)(2,1)S(1)}, u32[]{:S(2)}, u32[]{:S(2)}) collective-permute-start(bf16[512,512]{1,0:T(8,128)(2,1)} %pad_maximum_fusion), channel_id=1, source_target_pairs={{0,1},{1,2},{2,3},{3,4},{4,5},{5,6},{6,7},{7,8},{8,9},{9,10},{10,1... | collective-permute-start | bytes 1572872 | tf_op jit(solution)/shard_map/ppermute | solution.py:15
  102.8 26.6 %while.30 = (s32[]{:T(128)}, bf16[4,512,4,16]{1,3,2,0:T(8,128)(2,1)}, bf16[4,512,4,16]{1,3,2,0:T(8,128)(2,1)}, bf16[4,512,4,16]{1,3,2,0:T(8,128)(2,1)S(1)}, bf16[4,512,4,16]{1,3,2,0:T(8,128)(2,1)S(1)}, /*index=5*/s32[]{:T(128)}) while((s32[]{:T(128)}, bf16[4,512,4,16]{1,3,2,0:T(8,128)(2,1)}, bf16[4,512,4,16]{1,3,2,0:T(8,128)(2,1)}, ...), condition=%wide.region_11.12_spmd, body=%wide.region_8.11_spmd.sunk | while | flops 72385024 | bytes 8669261 | solution.py:51
  102.8 3.4 %fusion.214 = (f32[4,512]{1,0:T(4,128)S(1)}, f32[4,512,512]{1,2,0:T(8,128)}) fusion(bf16[4,512,4,16]{1,3,2,0:T(8,128)(2,1)S(1)} %get-tuple-element.289, s32[]{:T(128)S(6)} %copy.89, bf16[4,512,4,16]{1,3,2,0:T(8,128)(2,1)S(1)} %get-tuple-element.288), kind=kOutput, calls=%fused_computation.158.clone.1 | convolution fusion | flops 36700672 | bytes 4334592 | tf_op jit(solution)/shard_map/while/body/eval_jaxpr/sub | solution.py:46
  106.2 3.2 %fusion.215 = bf16[4,512,4,16]{1,3,2,0:T(8,128)(2,1)} fusion(bf16[4,512,4,16]{1,3,2,0:T(8,128)(2,1)} %get-tuple-element.280, s32[]{:T(128)S(6)} %copy.89, f32[4,512,512]{1,2,0:T(8,128)} %get-tuple-element.225, f32[4,512]{1,0:T(4,128)S(1)} %get-tuple-element.226, bf16[4,512,4,16]{1,3,2,0:T(8,128)(2,1)} %get-tuple-element.287), kind=kOutput, calls=%fused_computation.17.clone.1 | convolution fusion | flops 35684352 | bytes 4334592 | tf_op jit(solution)/shard_map/while/body/eval_jaxpr/hqk,khd->qhd/dot_general | solution.py:48
  109.4 3.4 %fusion.214 = (f32[4,512]{1,0:T(4,128)S(1)}, f32[4,512,512]{1,2,0:T(8,128)}) fusion(bf16[4,512,4,16]{1,3,2,0:T(8,128)(2,1)S(1)} %get-tuple-element.289, s32[]{:T(128)S(6)} %copy.89, bf16[4,512,4,16]{1,3,2,0:T(8,128)(2,1)S(1)} %get-tuple-element.288), kind=kOutput, calls=%fused_computation.158.clone.1 | convolution fusion | flops 36700672 | bytes 4334592 | tf_op jit(solution)/shard_map/while/body/eval_jaxpr/sub | solution.py:46
  112.8 3.2 %fusion.215 = bf16[4,512,4,16]{1,3,2,0:T(8,128)(2,1)} fusion(bf16[4,512,4,16]{1,3,2,0:T(8,128)(2,1)} %get-tuple-element.280, s32[]{:T(128)S(6)} %copy.89, f32[4,512,512]{1,2,0:T(8,128)} %get-tuple-element.225, f32[4,512]{1,0:T(4,128)S(1)} %get-tuple-element.226, bf16[4,512,4,16]{1,3,2,0:T(8,128)(2,1)} %get-tuple-element.287), kind=kOutput, calls=%fused_computation.17.clone.1 | convolution fusion | flops 35684352 | bytes 4334592 | tf_op jit(solution)/shard_map/while/body/eval_jaxpr/hqk,khd->qhd/dot_general | solution.py:48
  116.1 3.4 %fusion.214 = (f32[4,512]{1,0:T(4,128)S(1)}, f32[4,512,512]{1,2,0:T(8,128)}) fusion(bf16[4,512,4,16]{1,3,2,0:T(8,128)(2,1)S(1)} %get-tuple-element.289, s32[]{:T(128)S(6)} %copy.89, bf16[4,512,4,16]{1,3,2,0:T(8,128)(2,1)S(1)} %get-tuple-element.288), kind=kOutput, calls=%fused_computation.158.clone.1 | convolution fusion | flops 36700672 | bytes 4334592 | tf_op jit(solution)/shard_map/while/body/eval_jaxpr/sub | solution.py:46
  119.5 3.2 %fusion.215 = bf16[4,512,4,16]{1,3,2,0:T(8,128)(2,1)} fusion(bf16[4,512,4,16]{1,3,2,0:T(8,128)(2,1)} %get-tuple-element.280, s32[]{:T(128)S(6)} %copy.89, f32[4,512,512]{1,2,0:T(8,128)} %get-tuple-element.225, f32[4,512]{1,0:T(4,128)S(1)} %get-tuple-element.226, bf16[4,512,4,16]{1,3,2,0:T(8,128)(2,1)} %get-tuple-element.287), kind=kOutput, calls=%fused_computation.17.clone.1 | convolution fusion | flops 35684352 | bytes 4334592 | tf_op jit(solution)/shard_map/while/body/eval_jaxpr/hqk,khd->qhd/dot_general | solution.py:48
  122.7 3.4 %fusion.214 = (f32[4,512]{1,0:T(4,128)S(1)}, f32[4,512,512]{1,2,0:T(8,128)}) fusion(bf16[4,512,4,16]{1,3,2,0:T(8,128)(2,1)S(1)} %get-tuple-element.289, s32[]{:T(128)S(6)} %copy.89, bf16[4,512,4,16]{1,3,2,0:T(8,128)(2,1)S(1)} %get-tuple-element.288), kind=kOutput, calls=%fused_computation.158.clone.1 | convolution fusion | flops 36700672 | bytes 4334592 | tf_op jit(solution)/shard_map/while/body/eval_jaxpr/sub | solution.py:46
  126.1 3.2 %fusion.215 = bf16[4,512,4,16]{1,3,2,0:T(8,128)(2,1)} fusion(bf16[4,512,4,16]{1,3,2,0:T(8,128)(2,1)} %get-tuple-element.280, s32[]{:T(128)S(6)} %copy.89, f32[4,512,512]{1,2,0:T(8,128)} %get-tuple-element.225, f32[4,512]{1,0:T(4,128)S(1)} %get-tuple-element.226, bf16[4,512,4,16]{1,3,2,0:T(8,128)(2,1)} %get-tuple-element.287), kind=kOutput, calls=%fused_computation.17.clone.1 | convolution fusion | flops 35684352 | bytes 4334592 | tf_op jit(solution)/shard_map/while/body/eval_jaxpr/hqk,khd->qhd/dot_general | solution.py:48
  134.1 13.5 %while.32 = (s32[]{:T(128)}, bf16[4,256,4,16]{1,3,2,0:T(8,128)(2,1)S(1)}, bf16[4,512,4,16]{1,3,2,0:T(8,128)(2,1)S(1)}, bf16[4,256,4,16]{1,3,2,0:T(8,128)(2,1)}, bf16[4,512,4,16]{1,3,2,0:T(8,128)(2,1)S(1)}, /*index=5*/s32[]{:T(128)}) while((s32[]{:T(128)}, bf16[4,256,4,16]{1,3,2,0:T(8,128)(2,1)S(1)}, bf16[4,512,4,16]{1,3,2,0:T(8,128)(2,1)S(1)}, ...), condition=%wide.region_19.20_spmd, body=%wide.region_16.19_spmd.sunk | while | flops 54020096 | bytes 306253 | solution.py:51
  148.1 7.4 %while.31 = (s32[]{:T(128)}, bf16[4,256,4,16]{1,3,2,0:T(8,128)(2,1)S(1)}, bf16[4,512,4,16]{1,3,2,0:T(8,128)(2,1)S(1)}, bf16[4,256,4,16]{1,3,2,0:T(8,128)(2,1)S(1...) while((s32[]{:T(128)}, bf16[4,256,4,16]{1,3,2,0:T(8,128)(2,1)S(1)}, ...), condition=%wide.region_15.16_spmd, body=%wide.region_12.15_spmd.sunk | while | flops 54020096 | bytes 306253 | solution.py:51
  156.0 3.5 %scatter_custom_fusion.2 = bf16[1024,512]{1,0:T(8,128)(2,1)} fusion(s32[512]{0:T(512)S(1)} %compare_select_fusion.2, bf16[512,512]{1,0:T(8,128)(2,1)S(1)} %fusion.139, bf16[]{:T(256)} %constant.94.clone.1), kind=kCustom, calls=%fused_computation.121 | custom fusion | bytes 1048578 | tf_op jit(solution)/shard_map/scatter | solution.py:117
  159.5 10.2 %all-to-all-start.2 = ((bf16[128,8,512]{2,1,0:T(8,128)(2,1)}), bf16[128,8,512]{2,1,0:T(8,128)(2,1)S(1)}, u32[]{:S(2)}, u32[]{:S(2)}) async-start(bf16[128,8,512]{2,1,0:T(8,128)(2,1)} %bitcast.189), calls=%async_computation.2 | async-start | bytes 2097152 | tf_op jit(solution)/shard_map/all_to_all | solution.py:119
  169.8 30.3 %all-to-all-done.2 = bf16[128,8,512]{2,1,0:T(8,128)(2,1)S(1)} async-done(((bf16[128,8,512]{2,1,0:T(8,128)(2,1)}), bf16[128,8,512]{2,1,0:T(8,128)(2,1)S(1)}, u32[]{:S(2)}, u32[]{:S(2)}) %all-to-all-start.2) | async-done | bytes 1048608 | tf_op jit(solution)/shard_map/all_to_all | solution.py:119
  200.1 5.8 %scatter_custom_fusion.3 = bf16[512,512]{1,0:T(8,128)(2,1)} fusion(s32[1024]{0:T(1024)S(1)} %bitcast.203, bf16[128,8,512]{2,1,0:T(8,128)(2,1)S(1)} %all-to-all-done.2, bf16[]{:T(256)} %constant.94.clone.1), kind=kCustom, calls=%fused_computation.108 | custom fusion | bytes 1572866 | tf_op jit(solution)/shard_map/scatter | solution.py:129
  (90 shorter events, 42.4 us)
Async XLA Ops:
  0.0 92.6 %copy-start = (bf16[512,1536]{1,0:T(8,128)(2,1)S(1)}, bf16[512,1536]{1,0:T(8,128)(2,1)}, u32[]{:S(2)}) copy-start(bf16[512,1536]{1,0:T(8,128)(2,1)} %param.18) | copy-start | bytes 4718596
  5.4 43.5 %copy-start.1 = (bf16[512,512]{1,0:T(8,128)(2,1)S(1)}, bf16[512,512]{1,0:T(8,128)(2,1)}, u32[]{:S(2)}) copy-start(bf16[512,512]{1,0:T(8,128)(2,1)} %param.14) | copy-start | bytes 1572868
  54.0 36.1 %all-to-all-start.1 = ((bf16[128,8,512]{2,1,0:T(8,128)(2,1)}), bf16[128,8,512]{2,1,0:T(8,128)(2,1)S(1)}, u32[]{:S(2)}, u32[]{:S(2)}) async-start(bf16[128,8,512]{2,1,0:T(8,128)(2,1)} %bitcast_select_fusion), calls=%async_computation.1 | async-start | bytes 2097152 | tf_op jit(solution)/shard_map/all_to_all | solution.py:84
  90.2 2.5 %copy-start.6 = (f32[1536]{0:T(1024)S(1)}, f32[1536]{0:T(1024)}, u32[]{:S(2)}) copy-start(f32[1536]{0:T(1024)} %param.19) | copy-start | bytes 18436
  90.2 2.5 %copy-start.7 = (f32[512]{0:T(512)S(1)}, f32[512]{0:T(512)}, u32[]{:S(2)}) copy-start(f32[512]{0:T(512)} %param.17) | copy-start | bytes 6148
  90.2 2.5 %copy-start.8 = (f32[512]{0:T(512)S(1)}, f32[512]{0:T(512)}, u32[]{:S(2)}) copy-start(f32[512]{0:T(512)} %param.16) | copy-start | bytes 6148
  93.8 1.2 copy-start.2
  95.9 36.0 %collective-permute-start = (bf16[512,512]{1,0:T(8,128)(2,1)}, bf16[512,512]{1,0:T(8,128)(2,1)S(1)}, u32[]{:S(2)}, u32[]{:S(2)}) collective-permute-start(bf16[512,512]{1,0:T(8,128)(2,1)} %pad_maximum_fusion), channel_id=1, source_target_pairs={{0,1},{1,2},{2,3},{3,4},{4,5},{5,6},{6,7},{7,8},{8,9},{9,10},{10,1... | collective-permute-start | bytes 1572872 | tf_op jit(solution)/shard_map/ppermute | solution.py:15
  99.5 33.1 %collective-permute-start.1 = (bf16[512,512]{1,0:T(8,128)(2,1)}, bf16[512,512]{1,0:T(8,128)(2,1)}, u32[]{:S(2)}, u32[]{:S(2)}) collective-permute-start(bf16[512,512]{1,0:T(8,128)(2,1)} %pad_maximum_fusion), channel_id=1, source_target_pairs={{1,0},{2,1},{3,2},{4,3},{5,4},{6,5},{7,6},{8,7},{9,8},{10,9},{11,1... | collective-permute-start | bytes 1572872 | tf_op jit(solution)/shard_map/ppermute | solution.py:18
  131.9 0.8 copy-start.3
  134.1 13.9 %copy-start.4 = (bf16[256,256]{0,1:T(8,128)(2,1)S(1)}, bf16[256,256]{0,1:T(8,128)(2,1)}, u32[]{:S(2)}) copy-start(bf16[256,256]{0,1:T(8,128)(2,1)} %copy.66) | copy-start | bytes 393220
  148.0 7.5 %copy-start.5 = (bf16[512,512]{1,0:T(8,128)(2,1)S(1)}, bf16[512,512]{1,0:T(8,128)(2,1)}, u32[]{:S(2)}) copy-start(bf16[512,512]{1,0:T(8,128)(2,1)} %param.20) | copy-start | bytes 1572868
  148.0 7.5 %copy-start.9 = (f32[512]{0:T(512)S(1)}, f32[512]{0:T(512)}, u32[]{:S(2)}) copy-start(f32[512]{0:T(512)} %param.21) | copy-start | bytes 6148
  148.1 7.5 %copy-start.10 = (bf16[4,512,4,16]{1,3,2,0:T(8,128)(2,1)S(1)}, bf16[4,512,4,16]{1,3,2,0:T(8,128)(2,1)}, u32[]{:S(2)}) copy-start(bf16[4,512,4,16]{1,3,2,0:T(8,128)(2,1)} %get-tuple-element.88) | copy-start | bytes 786436
  159.5 40.6 %all-to-all-start.2 = ((bf16[128,8,512]{2,1,0:T(8,128)(2,1)}), bf16[128,8,512]{2,1,0:T(8,128)(2,1)S(1)}, u32[]{:S(2)}, u32[]{:S(2)}) async-start(bf16[128,8,512]{2,1,0:T(8,128)(2,1)} %bitcast.189), calls=%async_computation.2 | async-start | bytes 2097152 | tf_op jit(solution)/shard_map/all_to_all | solution.py:119
where the time goes:
time: 207 us; the launch traced here: 206 us
  waiting for transfers between devices  60.7 us (29%)
  matrix products  49 us (24%)
  local copies, waits for them, and re-layouts  34.5 us (17%)
  blocking collectives  29.7 us (14%)
  starting transfers between devices  21.7 us (10%)
  other arithmetic  9.81 us (5%)
    all_to_all x1, waiting for transfers between devices, per_device(): lax.all_to_all(picked, 'seq', split_axis=0, concat_axis=0, tiled=True)  30.4 us
    all_to_all x1, waiting for transfers between devices, per_device(): lax.all_to_all(outgoing.reshape(peer_count, capacity, feature_width), 'se...  30.3 us
    all_to_all x1, blocking collectives, per_device(): lax.all_to_all(wanted.reshape(peer_count, capacity), 'seq', split_axis=0,...  29.7 us
    sub x12, matrix products, one_group(): expanded = jnp.exp(scores - highest)  23.8 us
    dot_general x12, matrix products, one_group(): jnp.einsum('hqk,khd->qhd', weights, value_heads, preferred_element_type=j...  23.7 us
    all_to_all x1, starting transfers between devices, per_device(): lax.all_to_all(outgoing.reshape(peer_count, capacity, feature_width), 'se...  10.2 us
    gather x2, local copies, waits for them, and re-layouts, per_device(): slot_sorted = holder[ranking] * capacity + positions - first_slot[ranking]  6.98 us
    scatter x1, local copies, waits for them, and re-layouts, per_device(): return jnp.zeros_like(feats).at[asked.reshape(-1)].set(returned.reshape(-...  5.79 us
  transfers between devices with their start and end apart: 4, of which 2 were waited for; matrix products, arithmetic and copies ran while one was open for 15% of the time, Pallas kernels for 0%

commit v1 on v0

v1 whole, which is shorter than its diff:
```python
import jax
import jax.numpy as jnp
from jax import lax
from jax.experimental import pallas as pl
from jax.experimental.pallas import tpu as pltpu
from jax.sharding import PartitionSpec as P

HEAD_DIM = 16
CAPACITY = 8
LANES = 128
GROUP = LANES // HEAD_DIM
SCALE = HEAD_DIM ** (-0.5) * 1.4426950408889634
SAFE = 100.0
BF16 = jnp.bfloat16
F32 = jnp.float32
NT = (((1,), (1,)), ((), ()))


def iota(shape, dim):
    return lax.broadcasted_iota(jnp.int32, shape, dim)


def dot(a, b):
    return jnp.dot(a, b, preferred_element_type=F32)


def dot_nt(a, b):
    return lax.dot_general(a, b, NT, preferred_element_type=F32)


def ranks(order_row, peers):
    rows = order_row.shape[1]
    holder = jnp.right_shift(order_row, rows.bit_length() - 1)
    mine = iota((peers, rows), 0) == holder
    mine_bf = jnp.where(mine, 1.0, 0.0).astype(BF16)
    before = jnp.where(iota((rows, rows), 0) < iota((rows, rows), 1), 1.0, 0.0).astype(BF16)
    rank = dot(mine_bf, before)
    rank_row = jnp.sum(jnp.where(mine, rank, 0.0), axis=0, keepdims=True).astype(jnp.int32)
    return holder, mine_bf, rank_row


def request_kernel(order_ref, wanted_ref):
    order_row = order_ref[...]
    peers = wanted_ref.shape[0]
    rows = order_row.shape[1]
    _, mine_bf, rank_row = ranks(order_row, peers)
    local = jnp.bitwise_and(order_row, rows - 1) + 1
    chosen = iota((LANES, rows), 0) == rank_row
    high = jnp.where(chosen, jnp.right_shift(local, 4).astype(F32), 0.0).astype(BF16)
    low = jnp.where(chosen, jnp.bitwise_and(local, 15).astype(F32), 0.0).astype(BF16)
    wanted_ref[...] = (dot_nt(mine_bf, high) * 16.0 + dot_nt(mine_bf, low)).astype(jnp.int32)


def column(row, count):
    return jnp.transpose(jnp.broadcast_to(row, (LANES, count)))


def prepare_kernel(
    feats_ref, order_ref, gain_ref, bias_ref, qkv_weight_ref, qkv_bias_ref, proj_weight_ref,
    proj_bias_ref, normed_ref, slot_row_ref, slot_col_ref, query_t_ref, value_t_ref, proj_t_ref,
    query_bias_ref, value_bias_ref, proj_bias_col_ref,
):
    rows, width = feats_ref.shape
    values = feats_ref[...].astype(F32)
    center = jnp.mean(values, axis=-1, keepdims=True)
    spread = jnp.mean(jnp.square(values - center), axis=-1, keepdims=True)
    normed_ref[...] = (
        (values - center) * lax.rsqrt(spread + 1e-05) * gain_ref[...] + bias_ref[...]
    ).astype(BF16)
    order_row = order_ref[...]
    peers = LANES
    holder, _, rank_row = ranks(order_row, peers)
    slot = holder * CAPACITY + rank_row
    slot_row_ref[...] = jnp.broadcast_to(slot, slot_row_ref.shape)
    slot_col_ref[...] = column(slot.astype(F32), rows).astype(jnp.int32)
    query_t_ref[...] = jnp.transpose(qkv_weight_ref[:, :width])
    value_t_ref[...] = jnp.transpose(qkv_weight_ref[:, 2 * width :])
    proj_t_ref[...] = jnp.transpose(proj_weight_ref[...])
    query_bias_ref[...] = column(qkv_bias_ref[:, :width], width)
    value_bias_ref[...] = column(qkv_bias_ref[:, 2 * width :], width)
    proj_bias_col_ref[...] = column(proj_bias_ref[...], width)


def pick_kernel(asked_ref, normed_ref, picked_ref):
    slots, _ = picked_ref.shape
    rows = normed_ref.shape[0]
    peers = asked_ref.shape[0]
    spread = jnp.broadcast_to(asked_ref[...], (peers, CAPACITY, LANES))
    own = iota((peers, CAPACITY, LANES), 1) == iota((peers, CAPACITY, LANES), 2)
    index = jnp.sum(jnp.where(own, spread, 0).reshape(slots, LANES).astype(F32), axis=1, keepdims=True)
    onehot = jnp.where(index.astype(jnp.int32) - 1 == iota((slots, rows), 1), 1.0, 0.0).astype(BF16)
    picked_ref[...] = dot(onehot, normed_ref[...]).astype(BF16)


def asked_row_kernel(asked_ref, row_ref):
    peers = asked_ref.shape[0]
    slots = row_ref.shape[1]
    flipped = jnp.transpose(asked_ref[...].astype(F32)).astype(jnp.int32)
    expand = jnp.where(
        jnp.right_shift(iota((peers, slots), 1), 3) == iota((peers, slots), 0), 1.0, 0.0
    ).astype(BF16)
    high = dot(jnp.right_shift(flipped, 4).astype(F32).astype(BF16), expand)
    low = dot(jnp.bitwise_and(flipped, 15).astype(F32).astype(BF16), expand)
    own = jnp.bitwise_and(iota((LANES, slots), 1), CAPACITY - 1) == iota((LANES, slots), 0)
    row = jnp.sum(jnp.where(own, high * 16.0 + low, 0.0), axis=0, keepdims=True)
    row_ref[...] = jnp.broadcast_to(row.astype(jnp.int32), row_ref.shape)


def arrange_kernel(arrived_ref, slot_col_ref, seq_ref):
    rows = seq_ref.shape[0]
    slots = arrived_ref.shape[0]
    onehot = jnp.where(slot_col_ref[:, :1] == iota((rows, slots), 1), 1.0, 0.0).astype(BF16)
    seq_ref[...] = dot(onehot, arrived_ref[...]).astype(BF16)


def largest_square(source, axis):
    squares = jnp.square(source.astype(F32)).astype(BF16)
    channels = source.shape[axis]
    if axis == 1:
        fold = jnp.where(
            jnp.right_shift(iota((channels, LANES), 0), 4) == iota((channels, LANES), 1), 1.0, 0.0
        ).astype(BF16)
        return jnp.max(dot(squares, fold))
    fold = jnp.where(
        jnp.right_shift(iota((LANES, channels), 1), 4) == iota((LANES, channels), 0), 1.0, 0.0
    ).astype(BF16)
    return jnp.max(dot(fold, squares))


def in_range(query_square, key_square):
    return query_square * key_square * (1.05 * SCALE * SCALE) < SAFE * SAFE


def attend(queries_ref, sides, out_ref, out_start, shifted):
    channels, rows = queries_ref.shape
    groups = channels // LANES

    def scores(group, masked):
        start = pl.multiple_of(group * LANES, LANES)
        return [dot(keys[:, pl.ds(start, LANES)], masked[:, a:b]) for keys, _, a, b in sides]

    def store(base, parts):
        mixed = [
            dot(values[pl.ds(base, HEAD_DIM), :], part)
            for (_, values, _, _), part in zip(sides, parts)
        ]
        mixed = mixed[0] if len(mixed) == 1 else jnp.concatenate(mixed, axis=1)
        out_ref[pl.ds(out_start + base, HEAD_DIM), :] = mixed.astype(BF16)

    def normalise(expanded):
        return (expanded * (1.0 / jnp.sum(expanded, axis=0, keepdims=True))).astype(BF16)

    def head_base(group, head):
        return pl.multiple_of(group * LANES + head * HEAD_DIM, HEAD_DIM)

    @pl.when(jnp.logical_not(shifted))
    def _():
        def one_group(group, carry):
            def head_scores(head):
                query = queries_ref[pl.ds(head_base(group, head), HEAD_DIM), :]
                parts = []
                if head > 0:
                    parts.append(jnp.zeros((HEAD_DIM * head, rows), BF16))
                parts.append(query)
                if head < GROUP - 1:
                    parts.append(jnp.zeros((HEAD_DIM * (GROUP - 1 - head), rows), BF16))
                return scores(group, jnp.concatenate(parts, axis=0))

            current = head_scores(0)
            previous = None
            for head in range(GROUP):
                following = head_scores(head + 1) if head < GROUP - 1 else None
                weights = [normalise(jnp.exp2(part * SCALE)) for part in current]
                if previous is not None:
                    store(head_base(group, head - 1), previous)
                previous, current = weights, following
            store(head_base(group, GROUP - 1), previous)
            return carry

        lax.fori_loop(0, groups, one_group, 0)

    @pl.when(shifted)
    def _():
        def one_head(index, carry):
            group = index // GROUP
            start = pl.multiple_of(group * LANES, LANES)
            inside = jnp.right_shift(iota((LANES, rows), 0), 4) == index - group * GROUP
            masked = jnp.where(inside, queries_ref[pl.ds(start, LANES), :], jnp.zeros((), BF16))
            weights = []
            for part in scores(group, masked):
                highest = jnp.max(part, axis=0, keepdims=True)
                weights.append(normalise(jnp.exp2((part - highest) * SCALE)))
            store(pl.multiple_of(index * HEAD_DIM, HEAD_DIM), weights)
            return carry

        lax.fori_loop(0, groups * GROUP, one_head, 0)


def near_kernel(
    seq_ref, query_t_ref, key_ref, value_t_ref, query_bias_ref, key_bias_ref, value_bias_ref,
    attended_ref, far_query_ref, far_key_ref, far_value_ref, far_square_ref, query_s, key_s, value_s,
):
    half = query_s.shape[0]
    seq = seq_ref[...]
    queries = (dot_nt(query_t_ref[...], seq) + query_bias_ref[:, :1]).astype(BF16)
    keys = (dot(seq, key_ref[...]) + key_bias_ref[...]).astype(BF16)
    values = (dot_nt(value_t_ref[...], seq) + value_bias_ref[:, :1]).astype(BF16)
    query_s[...] = queries[:half]
    far_query_ref[...] = queries[half:]
    key_s[...] = keys[:, :half]
    far_key_ref[...] = keys[:, half:]
    value_s[...] = values[:half]
    far_value_ref[...] = values[half:]
    far_square_ref[0, 0] = largest_square(queries[half:], 0)
    safe = in_range(largest_square(queries[:half], 0), largest_square(keys[:, :half], 1))
    rows = seq.shape[0]
    attend(query_s, [(key_s, value_s, 0, rows)], attended_ref, 0, jnp.logical_not(safe))


def far_kernel(
    low_ref, high_ref, near_ref, far_query_ref, far_key_ref, far_value_ref, far_square_ref,
    key_ref, key_bias_ref, value_t_ref, value_bias_ref, proj_t_ref, proj_bias_ref, slot_row_ref,
    outgoing_ref, attended_s, low_key_s, low_value_s, high_key_s, high_value_s,
):
    half, rows = far_query_ref.shape
    middle = rows // 2
    attended_s[:half] = near_ref[...]
    key_weight, key_bias = key_ref[...], key_bias_ref[...]
    value_weight, value_bias = value_t_ref[...], value_bias_ref[:, :1]

    def keys_of(rows_ref):
        return (dot(rows_ref[...], key_weight) + key_bias).astype(BF16)

    def values_of(rows_ref):
        return (dot_nt(value_weight, rows_ref[...]) + value_bias).astype(BF16)

    low_key_s[:middle] = keys_of(low_ref)
    low_key_s[middle:] = far_key_ref[:middle]
    high_key_s[:middle] = far_key_ref[middle:]
    high_key_s[middle:] = keys_of(high_ref)
    low_value_s[:, :middle] = values_of(low_ref)
    low_value_s[:, middle:] = far_value_ref[:, :middle]
    high_value_s[:, :middle] = far_value_ref[:, middle:]
    high_value_s[:, middle:] = values_of(high_ref)
    key_square = jnp.maximum(largest_square(low_key_s[...], 1), largest_square(high_key_s[...], 1))
    safe = in_range(far_square_ref[0, 0], key_square)
    sides = [(low_key_s, low_value_s, 0, middle), (high_key_s, high_value_s, middle, rows)]
    attend(far_query_ref, sides, attended_s, half, jnp.logical_not(safe))
    update = (dot(proj_t_ref[...], attended_s[...]) + proj_bias_ref[:, :1]).astype(BF16)
    slots = outgoing_ref.shape[0]
    onehot = jnp.where(iota((slots, rows), 0) == slot_row_ref[:1], 1.0, 0.0).astype(BF16)
    outgoing_ref[...] = dot_nt(onehot, update).astype(BF16)


def place_kernel(returned_ref, row_ref, out_ref):
    rows = out_ref.shape[0]
    slots = returned_ref.shape[0]
    onehot = jnp.where(iota((rows, slots), 0) + 1 == row_ref[:1], 1.0, 0.0).astype(BF16)
    out_ref[...] = dot(onehot, returned_ref[...]).astype(BF16)


def call(kernel, outs, scratch=(), flops=0, smem_outs=(), smem_ins=(), count=0):
    vmem = pl.BlockSpec(memory_space=pltpu.VMEM)
    smem = pl.BlockSpec(memory_space=pltpu.SMEM)
    return pl.pallas_call(
        kernel,
        out_shape=outs if len(outs) > 1 else outs[0],
        in_specs=[smem if i in smem_ins else vmem for i in range(count)],
        out_specs=[smem if i in smem_outs else vmem for i in range(len(outs))]
        if len(outs) > 1
        else vmem,
        scratch_shapes=list(scratch),
        compiler_params=pltpu.CompilerParams(vmem_limit_bytes=24 * 1024 * 1024),
        cost_estimate=pl.CostEstimate(flops=flops, bytes_accessed=4 * 1024 * 1024, transcendentals=0),
        name=kernel.__name__,
    )


def per_device(feats, order, norm_gain, norm_bias, qkv_weight, qkv_bias, proj_weight, proj_bias):
    rows, width = feats.shape
    peers = lax.axis_size("seq")
    slots = peers * CAPACITY
    half, middle = width // 2, rows // 2
    shape = jax.ShapeDtypeStruct
    order_row = order.reshape(1, rows)
    bias_row = qkv_bias.reshape(1, 3 * width)

    wanted = call(request_kernel, [shape((peers, LANES), jnp.int32)], count=1)(order_row)
    asked = lax.all_to_all(wanted, "seq", split_axis=0, concat_axis=0, tiled=True)
    square, columns = shape((width, width), BF16), shape((width, LANES), F32)
    (normed, slot_row, slot_col, query_t, value_t, proj_t, query_bias, value_bias, proj_bias_col) = call(
        prepare_kernel,
        [
            shape((rows, width), BF16), shape((8, rows), jnp.int32), shape((rows, LANES), jnp.int32),
            square, square, square, columns, columns, columns,
        ],
        flops=4_000_000_000,
        count=8,
    )(
        feats, order_row, norm_gain.reshape(1, width), norm_bias.reshape(1, width), qkv_weight,
        bias_row, proj_weight, proj_bias.reshape(1, width),
    )
    picked = call(pick_kernel, [shape((slots, width), BF16)], count=2)(
        asked.reshape(peers, 1, LANES), normed
    )
    arrived = lax.all_to_all(
        picked.reshape(peers, CAPACITY, width), "seq", split_axis=0, concat_axis=0, tiled=True
    )
    asked_row = call(asked_row_kernel, [shape((8, slots), jnp.int32)], flops=1_000_000_000, count=1)(asked)
    seq = call(arrange_kernel, [shape((rows, width), BF16)], count=2)(
        arrived.reshape(slots, width), slot_col
    )
    forward = [(i, (i + 1) % peers) for i in range(peers)]
    backward = [(target, source) for source, target in forward]
    low = lax.ppermute(seq[middle:], "seq", forward)
    high = lax.ppermute(seq[:middle], "seq", backward)
    key_weight = lax.slice_in_dim(qkv_weight, width, 2 * width, axis=1)
    key_bias = lax.slice_in_dim(bias_row, width, 2 * width, axis=1)
    near, far_query, far_key, far_value, far_square = call(
        near_kernel,
        [
            shape((half, rows), BF16), shape((half, rows), BF16), shape((rows, half), BF16),
            shape((half, rows), BF16), shape((1, 1), F32),
        ],
        [pltpu.VMEM((half, rows), BF16), pltpu.VMEM((rows, half), BF16), pltpu.VMEM((half, rows), BF16)],
        flops=6_000_000_000,
        smem_outs=(4,),
        count=7,
    )(seq, query_t, key_weight, value_t, query_bias, key_bias, value_bias)
    outgoing = call(
        far_kernel,
        [shape((slots, width), BF16)],
        [
            pltpu.VMEM((width, rows), BF16), pltpu.VMEM((rows, half), BF16), pltpu.VMEM((half, rows), BF16),
            pltpu.VMEM((rows, half), BF16), pltpu.VMEM((half, rows), BF16),
        ],
        flops=6_000_000_000,
        smem_ins=(6,),
        count=14,
    )(
        low, high, near, far_query, far_key, far_value, far_square, key_weight[:, half:],
        key_bias[:, half:], value_t[half:], value_bias[half:], proj_t, proj_bias_col, slot_row,
    )
    returned = lax.all_to_all(
        outgoing.reshape(peers, CAPACITY, width), "seq", split_axis=0, concat_axis=0, tiled=True
    )
    return call(place_kernel, [shape((rows, width), BF16)], count=2)(
        returned.reshape(slots, width), asked_row
    )


def solution(mesh):
    return jax.shard_map(
        per_device,
        mesh=mesh,
        in_specs=(P(("dp", "seq"), None), P(("dp", "seq")), P(), P(), P(), P(), P(), P()),
        out_specs=P(("dp", "seq"), None),
        check_vma=False,
    )
```

time: 207 us -> 156 us (0.75)
  matrix products: 49 us -> 0 us
  Pallas kernels: 0 us -> 33.6 us
  blocking collectives: 29.7 us -> 0 us
  starting transfers between devices: 21.7 us -> 47.5 us
  local copies, waits for them, and re-layouts: 34.5 us -> 14.3 us
  other arithmetic: 9.81 us -> 0 us
    pallas_call x0 -> x8, Pallas kernels: none -> 33.6 us  [the longest x1 14.4 us: per_device(): call(far_kernel, [shape((slots, width), BF16)], [pltpu.VMEM((width, rows)...]
    all_to_all x1 -> x0, blocking collectives: 29.7 us -> none  [per_device(): lax.all_to_all(wanted.reshape(peer_count, capacity), 'seq', split_axis=0,...]
    all_to_all x2 -> x3, starting transfers between devices: 15.9 us -> 41.8 us  [the longest x1 18.4 us: per_device(): lax.all_to_all(wanted, 'seq', split_axis=0, concat_axis=0, tiled=True)]
    dot_general x14 -> x0, matrix products: 25.3 us -> none  [the longest x12 23.7 us: one_group(): jnp.einsum('hqk,khd->qhd', weights, value_heads, preferred_element_type=j...]
    sub x12 -> x0, matrix products: 23.8 us -> none  [one_group(): expanded = jnp.exp(scores - highest)]
    scatter x4 -> x0, local copies, waits for them, and re-layouts: 14.2 us -> none  [the longest x1 5.79 us: per_device(): return jnp.zeros_like(feats).at[asked.reshape(-1)].set(returned.reshape(-...]
    gather x4 -> x0, local copies, waits for them, and re-layouts: 12.9 us -> none  [the longest x2 6.98 us: per_device(): slot_sorted = holder[ranking] * capacity + positions - first_slot[ranking]]
    unnamed x22 -> x48, local copies, waits for them, and re-layouts: 2.03 us -> 12.7 us
  transfers between devices with their start and end apart: 4 -> 5, of which waited for: 2 -> 2; matrix products, arithmetic and copies ran while one was open for 15% -> 1% of each run, Pallas kernels for 0% -> 9%
where the time goes in v1:
time: 156 us; the launch traced here: 155 us
  waiting for transfers between devices  59.3 us (38%)
  starting transfers between devices  47.5 us (30%)
  Pallas kernels  33.6 us (22%)
  local copies, waits for them, and re-layouts  14.3 us (9%)
    all_to_all x1, waiting for transfers between devices, per_device(): lax.all_to_all(outgoing.reshape(peers, CAPACITY, width), 'seq', split_axi...  30 us
    all_to_all x1, waiting for transfers between devices, per_device(): lax.all_to_all(picked.reshape(peers, CAPACITY, width), 'seq', split_axis=...  29.2 us
    all_to_all x1, starting transfers between devices, per_device(): lax.all_to_all(wanted, 'seq', split_axis=0, concat_axis=0, tiled=True)  18.4 us
    pallas_call x1, Pallas kernels, per_device(): call(far_kernel, [shape((slots, width), BF16)], [pltpu.VMEM((width, rows)...  14.4 us
    all_to_all x1, starting transfers between devices, per_device(): lax.all_to_all(picked.reshape(peers, CAPACITY, width), 'seq', split_axis=...  13.7 us
    unnamed x48, local copies, waits for them, and re-layouts  12.7 us
    pallas_call x1, Pallas kernels, per_device(): call(near_kernel, [shape((half, rows), BF16), shape((half, rows), BF16),...  12.5 us
    all_to_all x1, starting transfers between devices, per_device(): lax.all_to_all(outgoing.reshape(peers, CAPACITY, width), 'seq', split_axi...  9.66 us
  transfers between devices with their start and end apart: 5, of which 2 were waited for; matrix products, arithmetic and copies ran while one was open for 1% of the time, Pallas kernels for 9%

profile of v1, /device:TPU:1, one launch (start us, length us, event | category | flops | bytes accessed | tf_op | source)
XLA Modules:
  0.0 154.9 jit_solution(15877972858491013943)
XLA Ops:
  0.7 1.1 request_kernel.1
  1.8 18.4 %all-to-all-start = ((s32[128,1,128]{2,1,0:T(1,128)}), s32[128,1,128]{2,1,0:T(1,128)S(1)}, u32[]{:S(2)}, u32[]{:S(2)}) async-start(s32[128,1,128]{2,1,0:T(1,128)} %bitcast.2), calls=%async_computation | async-start | bytes 131072 | tf_op jit(solution)/shard_map/all_to_all | solution.py:289
  20.9 1.4 copy-done
  23.0 1.0 copy-done.11
  24.1 1.0 copy-done.12
  27.1 1.2 prepare_kernel.1
  28.3 0.8 copy-done.3
  29.1 0.7 copy-done.6
  29.8 0.8 copy-done.16
  30.6 0.8 copy-done.18
  31.4 0.7 copy-done.20
  32.8 1.8 %pick_kernel.1 = bf16[1024,512]{1,0:T(8,128)(2,1)} custom-call(s32[128,1,128]{2,1,0:T(1,128)S(1)} %all-to-all-done.asked_ref, bf16[512,512]{1,0:T(8,128)(2,1)S(1)} %get-tuple-element.19.normed_ref), custom_call_target="tpu_custom_call" | custom-call | bytes 4194304 | tf_op jit(solution)/shard_map/pick_kernel/pallas_call | solution.py:303
  34.7 13.7 %all-to-all-start.1 = ((bf16[128,8,512]{2,1,0:T(8,128)(2,1)}), bf16[128,8,512]{2,1,0:T(8,128)(2,1)S(1)}, u32[]{:S(2)}, u32[]{:S(2)}) async-start(bf16[128,8,512]{2,1,0:T(8,128)(2,1)} %bitcast.6), calls=%async_computation.1 | async-start | bytes 2097152 | tf_op jit(solution)/shard_map/all_to_all | solution.py:306
  48.5 0.7 slice.30.key_ref
  49.6 29.2 %all-to-all-done.1 = bf16[128,8,512]{2,1,0:T(8,128)(2,1)S(1)} async-done(((bf16[128,8,512]{2,1,0:T(8,128)(2,1)}), bf16[128,8,512]{2,1,0:T(8,128)(2,1)S(1)}, u32[]{:S(2)}, u32[]{:S(2)}) %all-to-all-start.1) | async-done | bytes 1048608 | tf_op jit(solution)/shard_map/all_to_all | solution.py:306
  78.8 0.7 arrange_kernel.1.seq_ref
  79.6 3.8 %collective-permute-start = (bf16[256,512]{1,0:T(8,128)(2,1)S(1)}, bf16[256,512]{1,0:T(8,128)(2,1)S(1)}, u32[]{:S(2)}, u32[]{:S(2)}) collective-permute-start(bf16[256,512]{1,0:T(8,128)(2,1)S(1)} %get-tuple-element.34), channel_id=1, source_target_pairs={{0,1},{1,2},{2,3},{3,4},{4,5},{5,6},{6,7},{7,8},{8,9},{9,10},{10,1... | collective-permute-start | bytes 786440 | tf_op jit(solution)/shard_map/ppermute | solution.py:315
  83.5 1.9 %collective-permute-start.1 = (bf16[256,512]{1,0:T(8,128)(2,1)S(1)}, bf16[256,512]{1,0:T(8,128)(2,1)S(1)}, u32[]{:S(2)}, u32[]{:S(2)}) collective-permute-start(bf16[256,512]{1,0:T(8,128)(2,1)S(1)} %get-tuple-element.33), channel_id=1, source_target_pairs={{1,0},{2,1},{3,2},{4,3},{5,4},{6,5},{7,6},{8,7},{9,8},{10,9},{11,1... | collective-permute-start | bytes 786440 | tf_op jit(solution)/shard_map/ppermute | solution.py:316
  85.4 0.9 copy-done.23
  86.4 12.5 %near_kernel.1 = (bf16[256,512]{1,0:T(8,128)(2,1)S(1)}, bf16[256,512]{1,0:T(8,128)(2,1)S(1)}, bf16[512,256]{1,0:T(8,128)(2,1)S(1)}, bf16[256,512]{1,0:T(8,128)(2,1)S(1)}, f32[1,1]{1,0:T(1,128)}) custom-call(bf16[512,512]{1,0:T(8,128)(2,1)S(1)} %arrange_kernel.1.seq_ref, bf16[512,512]{1,0:T(8,128)(2,1)S(1)} %copy-done.19, ...), custom_call_target="tpu_custom_call" | custom-call | flops 6000000000 | bytes 4194304 | tf_op jit(solution)/shard_map/near_kernel/pallas_call | solution.py:319
  99.0 14.4 %far_kernel.1 = bf16[1024,512]{1,0:T(8,128)(2,1)} custom-call(bf16[256,512]{1,0:T(8,128)(2,1)S(1)} %collective-permute-done.low_ref, bf16[256,512]{1,0:T(8,128)(2,1)S(1)} %collective-permute-done.1.high_ref, bf16[256,512]{1,0:T(8,128)(2,1)S(1)} %get-tuple-element.25.near_ref, bf16[256,512]{1,0:T(8,128)(2,1)S(1)} %get-tuple-element.26.far_query_ref, ...), custom_call_target="tpu_custom_call" | custom-call | flops 6000000000 | bytes 4194304 | tf_op jit(solution)/shard_map/far_kernel/pallas_call | solution.py:330
  113.4 9.7 %all-to-all-start.2 = ((bf16[128,8,512]{2,1,0:T(8,128)(2,1)}), bf16[128,8,512]{2,1,0:T(8,128)(2,1)S(1)}, u32[]{:S(2)}, u32[]{:S(2)}) async-start(bf16[128,8,512]{2,1,0:T(8,128)(2,1)} %bitcast.8), calls=%async_computation.2 | async-start | bytes 2097152 | tf_op jit(solution)/shard_map/all_to_all | solution.py:344
  123.4 30.0 %all-to-all-done.2 = bf16[128,8,512]{2,1,0:T(8,128)(2,1)S(1)} async-done(((bf16[128,8,512]{2,1,0:T(8,128)(2,1)}), bf16[128,8,512]{2,1,0:T(8,128)(2,1)S(1)}, u32[]{:S(2)}, u32[]{:S(2)}) %all-to-all-start.2) | async-done | bytes 1048608 | tf_op jit(solution)/shard_map/all_to_all | solution.py:344
  153.4 1.5 place_kernel.1
  (50 shorter events, 5.7 us)
Async XLA Ops:
  1.8 31.1 %all-to-all-start = ((s32[128,1,128]{2,1,0:T(1,128)}), s32[128,1,128]{2,1,0:T(1,128)S(1)}, u32[]{:S(2)}, u32[]{:S(2)}) async-start(s32[128,1,128]{2,1,0:T(1,128)} %bitcast.2), calls=%async_computation | async-start | bytes 131072 | tf_op jit(solution)/shard_map/all_to_all | solution.py:289
  20.9 1.4 copy-start
  23.0 1.0 copy-start.11
  24.1 1.0 copy-start.12
  28.3 0.8 copy-start.3
  29.1 0.7 copy-start.6
  29.8 0.8 copy-start.16
  30.6 0.8 copy-start.18
  31.4 0.7 copy-start.20
  32.1 0.7 copy-start.22
  32.8 15.6 %copy-start.1 = (bf16[512,1536]{1,0:T(8,128)(2,1)S(1)}, bf16[512,1536]{1,0:T(8,128)(2,1)}, u32[]{:S(2)}) copy-start(bf16[512,1536]{1,0:T(8,128)(2,1)} %qkv_weight_ref.1) | copy-start | bytes 4718596
  34.7 44.2 %all-to-all-start.1 = ((bf16[128,8,512]{2,1,0:T(8,128)(2,1)}), bf16[128,8,512]{2,1,0:T(8,128)(2,1)S(1)}, u32[]{:S(2)}, u32[]{:S(2)}) async-start(bf16[128,8,512]{2,1,0:T(8,128)(2,1)} %bitcast.6), calls=%async_computation.1 | async-start | bytes 2097152 | tf_op jit(solution)/shard_map/all_to_all | solution.py:306
  48.4 1.1 copy-start.4
  48.4 1.2 copy-start.7
  49.6 35.8 %copy-start.5 = (bf16[512,512]{1,0:T(8,128)(2,1)S(1)}, bf16[512,512]{1,0:T(8,128)(2,1)}, u32[]{:S(2)}) copy-start(bf16[512,512]{1,0:T(8,128)(2,1)} %copy-done.3) | copy-start | bytes 1572868
  49.6 35.8 %copy-start.8 = (f32[512,128]{1,0:T(8,128)S(1)}, f32[512,128]{1,0:T(8,128)}, u32[]{:S(2)}) copy-start(f32[512,128]{1,0:T(8,128)} %copy-done.6) | copy-start | bytes 786436
  78.8 6.6 %copy-start.19 = (bf16[512,512]{1,0:T(8,128)(2,1)S(1)}, bf16[512,512]{1,0:T(8,128)(2,1)}, u32[]{:S(2)}) copy-start(bf16[512,512]{1,0:T(8,128)(2,1)} %copy-done.18) | copy-start | bytes 1572868
  79.6 19.3 %collective-permute-start = (bf16[256,512]{1,0:T(8,128)(2,1)S(1)}, bf16[256,512]{1,0:T(8,128)(2,1)S(1)}, u32[]{:S(2)}, u32[]{:S(2)}) collective-permute-start(bf16[256,512]{1,0:T(8,128)(2,1)S(1)} %get-tuple-element.34), channel_id=1, source_target_pairs={{0,1},{1,2},{2,3},{3,4},{4,5},{5,6},{6,7},{7,8},{8,9},{9,10},{10,1... | collective-permute-start | bytes 786440 | tf_op jit(solution)/shard_map/ppermute | solution.py:315
  83.5 15.5 %collective-permute-start.1 = (bf16[256,512]{1,0:T(8,128)(2,1)S(1)}, bf16[256,512]{1,0:T(8,128)(2,1)S(1)}, u32[]{:S(2)}, u32[]{:S(2)}) collective-permute-start(bf16[256,512]{1,0:T(8,128)(2,1)S(1)} %get-tuple-element.33), channel_id=1, source_target_pairs={{1,0},{2,1},{3,2},{4,3},{5,4},{6,5},{7,6},{8,7},{9,8},{10,9},{11,1... | collective-permute-start | bytes 786440 | tf_op jit(solution)/shard_map/ppermute | solution.py:316
  85.4 1.0 copy-start.23
  86.4 12.6 %copy-start.2 = (bf16[512,256]{1,0:T(8,128)(2,1)S(1)}, bf16[512,256]{1,0:T(8,128)(2,1)}, u32[]{:S(2)}) copy-start(bf16[512,256]{1,0:T(8,128)(2,1)} %slice.30.key_ref) | copy-start | bytes 786436
  86.4 12.6 %copy-start.17 = (bf16[512,512]{1,0:T(8,128)(2,1)S(1)}, bf16[512,512]{1,0:T(8,128)(2,1)}, u32[]{:S(2)}) copy-start(bf16[512,512]{1,0:T(8,128)(2,1)} %copy-done.16) | copy-start | bytes 1572868
  86.4 12.6 %copy-start.21 = (f32[512,128]{1,0:T(8,128)S(1)}, f32[512,128]{1,0:T(8,128)}, u32[]{:S(2)}) copy-start(f32[512,128]{1,0:T(8,128)} %copy-done.20) | copy-start | bytes 786436
  113.4 40.1 %all-to-all-start.2 = ((bf16[128,8,512]{2,1,0:T(8,128)(2,1)}), bf16[128,8,512]{2,1,0:T(8,128)(2,1)S(1)}, u32[]{:S(2)}, u32[]{:S(2)}) async-start(bf16[128,8,512]{2,1,0:T(8,128)(2,1)} %bitcast.8), calls=%async_computation.2 | async-start | bytes 2097152 | tf_op jit(solution)/shard_map/all_to_all | solution.py:344
  (5 other events, 3.4 us)

commit v2 on v0

v2 whole, which is shorter than its diff:
```python
import jax
import jax.numpy as jnp
from jax import lax
from jax.experimental import pallas as pl
from jax.experimental.pallas import tpu as pltpu
from jax.sharding import PartitionSpec as P

HEAD_DIM = 16
CAPACITY = 8
LANES = 128
GROUP = LANES // HEAD_DIM
SCALE = HEAD_DIM ** (-0.5) * 1.4426950408889634
SUM_LOW, SUM_HIGH = 2.0**-60, 2.0**110
CHUNKS = 4
BF16 = jnp.bfloat16
F32 = jnp.float32
NT = (((1,), (1,)), ((), ()))


def iota(shape, dim):
    return lax.broadcasted_iota(jnp.int32, shape, dim)


def dot(a, b):
    return jnp.dot(a, b, preferred_element_type=F32)


def dot_nt(a, b):
    return lax.dot_general(a, b, NT, preferred_element_type=F32)


def ranks(order_row, peers):
    rows = order_row.shape[1]
    holder = jnp.right_shift(order_row, rows.bit_length() - 1)
    mine = iota((peers, rows), 0) == holder
    mine_bf = jnp.where(mine, 1.0, 0.0).astype(BF16)
    before = jnp.where(iota((rows, rows), 0) < iota((rows, rows), 1), 1.0, 0.0).astype(BF16)
    rank = dot(mine_bf, before)
    rank_row = jnp.sum(jnp.where(mine, rank, 0.0), axis=0, keepdims=True).astype(jnp.int32)
    return holder, mine_bf, rank_row


def request_kernel(order_ref, wanted_ref):
    order_row = order_ref[...]
    peers = wanted_ref.shape[0]
    rows = order_row.shape[1]
    _, mine_bf, rank_row = ranks(order_row, peers)
    local = jnp.bitwise_and(order_row, rows - 1) + 1
    chosen = iota((LANES, rows), 0) == rank_row
    high = jnp.where(chosen, jnp.right_shift(local, 4).astype(F32), 0.0).astype(BF16)
    low = jnp.where(chosen, jnp.bitwise_and(local, 15).astype(F32), 0.0).astype(BF16)
    wanted_ref[...] = (dot_nt(mine_bf, high) * 16.0 + dot_nt(mine_bf, low)).astype(jnp.int32)


def column(row, count):
    return jnp.transpose(jnp.broadcast_to(row, (LANES, count)))


def norm_kernel(feats_ref, gain_ref, bias_ref, normed_ref, feats_s, gain_s, bias_s, sems):
    copies = [
        pltpu.make_async_copy(feats_ref, feats_s, sems.at[0]),
        pltpu.make_async_copy(gain_ref, gain_s, sems.at[1]),
        pltpu.make_async_copy(bias_ref, bias_s, sems.at[2]),
    ]
    for copy in copies:
        copy.start()
    for copy in copies:
        copy.wait()
    values = feats_s[...].astype(F32)
    center = jnp.mean(values, axis=-1, keepdims=True)
    spread = jnp.mean(jnp.square(values - center), axis=-1, keepdims=True)
    normed_ref[...] = (
        (values - center) * lax.rsqrt(spread + 1e-05) * gain_s[...] + bias_s[...]
    ).astype(BF16)


def onehot_of(equal):
    return jnp.where(equal, 1.0, 0.0).astype(BF16)


def send_chunks(make, out_ref, stage, sems):
    size = stage.shape[0] // CHUNKS
    copies = []
    for chunk in range(CHUNKS):
        part = pl.ds(chunk * size, size)
        stage[part, :] = make(chunk, size)
        copies.append(pltpu.make_async_copy(stage.at[part, :], out_ref.at[part, :], sems.at[chunk]))
        copies[-1].start()
    for copy in copies:
        copy.wait()


def pick_kernel(asked_ref, normed_ref, picked_ref, stage, sems):
    rows = normed_ref.shape[0]
    normed = normed_ref[...]

    def make(chunk, size):
        peers = size // CAPACITY
        asked = asked_ref[chunk * peers : (chunk + 1) * peers]
        spread = jnp.broadcast_to(asked, (peers, CAPACITY, LANES))
        own = iota(spread.shape, 1) == iota(spread.shape, 2)
        index = jnp.where(own, spread, 0).reshape(size, LANES).astype(F32)
        index = jnp.sum(index, axis=1, keepdims=True).astype(jnp.int32) - 1
        return dot(onehot_of(index == iota((size, rows), 1)), normed).astype(BF16)

    send_chunks(make, picked_ref, stage, sems)


def setup_kernel(
    asked_ref, order_ref, qkv_weight_ref, qkv_bias_ref, proj_weight_ref, proj_bias_ref,
    arrange_ref, send_ref, place_ref, query_t_ref, key_ref, value_t_ref, proj_t_ref,
    query_bias_ref, key_bias_ref, value_bias_ref, proj_bias_col_ref,
):
    peers = asked_ref.shape[0]
    rows, slots = arrange_ref.shape
    width = query_t_ref.shape[0]
    holder, _, rank_row = ranks(order_ref[...], peers)
    slot = holder * CAPACITY + rank_row
    send_ref[...] = onehot_of(iota((slots, rows), 0) == slot)
    slot_col = column(slot.astype(F32), rows).astype(jnp.int32)
    arrange_ref[...] = onehot_of(slot_col[:, :1] == iota((rows, slots), 1))
    flipped = jnp.transpose(asked_ref[...].astype(F32)).astype(jnp.int32)
    expand = onehot_of(jnp.right_shift(iota((peers, slots), 1), 3) == iota((peers, slots), 0))
    high = dot(jnp.right_shift(flipped, 4).astype(F32).astype(BF16), expand)
    low = dot(jnp.bitwise_and(flipped, 15).astype(F32).astype(BF16), expand)
    own = jnp.bitwise_and(iota((LANES, slots), 1), CAPACITY - 1) == iota((LANES, slots), 0)
    asked_row = jnp.sum(jnp.where(own, high * 16.0 + low, 0.0), axis=0, keepdims=True).astype(jnp.int32)
    place_ref[...] = onehot_of(iota((rows, slots), 0) + 1 == asked_row)
    query_t_ref[...] = jnp.transpose(qkv_weight_ref[:, :width])
    key_ref[...] = qkv_weight_ref[:, width : 2 * width]
    value_t_ref[...] = jnp.transpose(qkv_weight_ref[:, 2 * width :])
    proj_t_ref[...] = jnp.transpose(proj_weight_ref[...])
    query_bias_ref[...] = column(qkv_bias_ref[:, :width], width)
    key_bias_ref[...] = qkv_bias_ref[:, width : 2 * width]
    value_bias_ref[...] = column(qkv_bias_ref[:, 2 * width :], width)
    proj_bias_col_ref[...] = column(proj_bias_ref[...], width)


def odd_device():
    return jnp.bitwise_and(lax.axis_index("seq"), 1)


def arrange_kernel(arrived_ref, onehot_ref, seq_ref, cross_ref, core_ref):
    middle = cross_ref.shape[0]
    seq_ref[...] = dot(onehot_ref[...], arrived_ref[...]).astype(BF16)
    odd = odd_device()
    cross_ref[...] = seq_ref[pl.ds(pl.multiple_of(odd * middle, middle), middle), :]
    core_ref[...] = seq_ref[pl.ds(pl.multiple_of((1 - odd) * middle, middle), middle), :]


def attend(queries_ref, sides, out_ref, out_start):
    channels, rows = queries_ref.shape
    heads = channels // HEAD_DIM

    def sums(expanded):
        return jnp.sum(expanded, axis=0, keepdims=True)

    def scores(item):
        head, (keys, _, begin, end) = item
        group, place = divmod(head, GROUP)
        parts = [queries_ref[head * HEAD_DIM : (head + 1) * HEAD_DIM, begin:end]]
        if place > 0:
            parts.insert(0, jnp.zeros((HEAD_DIM * place, end - begin), BF16))
        if place < GROUP - 1:
            parts.append(jnp.zeros((HEAD_DIM * (GROUP - 1 - place), end - begin), BF16))
        return dot(keys[:, group * LANES : (group + 1) * LANES], jnp.concatenate(parts, axis=0))

    def store(item, weights):
        head, (_, values, begin, end) = item
        mixed = dot(values[head * HEAD_DIM : (head + 1) * HEAD_DIM, :], weights)
        start = out_start + head * HEAD_DIM
        out_ref[start : start + HEAD_DIM, begin:end] = mixed.astype(BF16)

    items = [(head, side) for head in range(heads) for side in sides]
    ahead = [scores(item) for item in items[:2]]
    previous = None
    least = most = None
    for index, item in enumerate(items):
        if index + 2 < len(items):
            ahead.append(scores(items[index + 2]))
        expanded = jnp.exp2(ahead.pop(0) * SCALE)
        total = sums(expanded)
        least = total if least is None else jnp.minimum(least, total)
        most = total if most is None else jnp.maximum(most, total)
        weights = (expanded * (1.0 / total)).astype(BF16)
        if previous is not None:
            store(items[index - 1], previous)
        previous = weights
    store(items[-1], previous)
    in_range = jnp.logical_and(jnp.min(least) >= SUM_LOW, jnp.max(most) <= SUM_HIGH)

    @pl.when(jnp.logical_not(in_range))
    def _():
        def one_head(head, carry):
            group = head // GROUP
            start = pl.multiple_of(group * LANES, LANES)
            base = pl.multiple_of(head * HEAD_DIM, HEAD_DIM)
            for keys, values, begin, end in sides:
                inside = jnp.right_shift(iota((LANES, end - begin), 0), 4) == head - group * GROUP
                query = queries_ref[pl.ds(start, LANES), begin:end]
                part = dot(keys[:, pl.ds(start, LANES)], jnp.where(inside, query, jnp.zeros((), BF16)))
                expanded = jnp.exp2((part - jnp.max(part, axis=0, keepdims=True)) * SCALE)
                weights = (expanded * (1.0 / sums(expanded))).astype(BF16)
                mixed = dot(values[pl.ds(base, HEAD_DIM), :], weights)
                out_ref[pl.ds(out_start + base, HEAD_DIM), begin:end] = mixed.astype(BF16)
            return carry

        lax.fori_loop(0, heads, one_head, 0)


def near_kernel(
    seq_ref, query_t_ref, key_ref, value_t_ref, query_bias_ref, key_bias_ref, value_bias_ref,
    attended_ref, far_query_ref, far_key_ref, far_value_ref, query_s, key_s, value_s,
):
    half, rows = query_s.shape
    middle = rows // 2
    seq = seq_ref[...]
    queries = (dot_nt(query_t_ref[...], seq) + query_bias_ref[:, :1]).astype(BF16)
    keys = (dot(seq, key_ref[...]) + key_bias_ref[...]).astype(BF16)
    values = (dot_nt(value_t_ref[...], seq) + value_bias_ref[:, :1]).astype(BF16)
    query_s[...] = queries[:half]
    far_query_ref[...] = queries[half:]
    key_s[...] = keys[:, :half]
    far_key_ref[...] = keys[:, half:]
    value_s[...] = values[:half]
    far_value_ref[...] = values[half:]
    sides = [(key_s, value_s, 0, middle), (key_s, value_s, middle, rows)]
    attend(query_s, sides, attended_ref, 0)


def far_kernel(
    cross_ref, core_ref, near_ref, far_query_ref, far_key_ref, far_value_ref, key_ref, key_bias_ref,
    value_t_ref, value_bias_ref, proj_t_ref, proj_bias_ref, send_ref,
    outgoing_ref, attended_s, key_s, value_s, stage, sems,
):
    half, rows = far_query_ref.shape
    middle = rows // 2
    attended_s[:half] = near_ref[...]
    odd = odd_device()
    for side, rows_ref in ((odd, cross_ref), (1 - odd, core_ref)):
        keys = dot(rows_ref[...], key_ref[:, half:]) + key_bias_ref[:, half:]
        key_s[side, :middle] = keys.astype(BF16)
        values = dot_nt(value_t_ref[half:], rows_ref[...]) + value_bias_ref[half:, :1]
        value_s[side, :, :middle] = values.astype(BF16)
    for side in range(2):
        part = slice(side * middle, (side + 1) * middle)
        key_s[side, middle:] = far_key_ref[part]
        value_s[side, :, middle:] = far_value_ref[:, part]
    sides = [(key_s.at[0], value_s.at[0], 0, middle), (key_s.at[1], value_s.at[1], middle, rows)]
    attend(far_query_ref, sides, attended_s, half)
    update = (dot(proj_t_ref[...], attended_s[...]) + proj_bias_ref[:, :1]).astype(BF16)

    def make(chunk, size):
        return dot_nt(send_ref[chunk * size : (chunk + 1) * size], update).astype(BF16)

    send_chunks(make, outgoing_ref, stage, sems)


def place_kernel(returned_ref, onehot_ref, out_ref, stage, sems):
    returned = returned_ref[...]

    def make(chunk, size):
        return dot(onehot_ref[chunk * size : (chunk + 1) * size], returned).astype(BF16)

    send_chunks(make, out_ref, stage, sems)


def call(kernel, outs, count, scratch=(), flops=0, in_hbm=False, out_hbm=False):
    vmem, hbm = pl.BlockSpec(memory_space=pltpu.VMEM), pl.BlockSpec(memory_space=pl.ANY)
    out_specs = [hbm if out_hbm else vmem] * len(outs)
    return pl.pallas_call(
        kernel,
        out_shape=outs if len(outs) > 1 else outs[0],
        in_specs=[hbm if in_hbm else vmem] * count,
        out_specs=out_specs if len(outs) > 1 else out_specs[0],
        scratch_shapes=list(scratch),
        compiler_params=pltpu.CompilerParams(vmem_limit_bytes=20 * 1024 * 1024),
        cost_estimate=pl.CostEstimate(flops=flops, bytes_accessed=4 * 1024 * 1024, transcendentals=0),
        name=kernel.__name__,
    )


def per_device(feats, order, norm_gain, norm_bias, qkv_weight, qkv_bias, proj_weight, proj_bias):
    rows, width = feats.shape
    peers = lax.axis_size("seq")
    slots = peers * CAPACITY
    half, middle = width // 2, rows // 2
    shape = jax.ShapeDtypeStruct
    chunk_sems = pltpu.SemaphoreType.DMA((CHUNKS,))
    row_vector = pltpu.VMEM((1, width), F32)

    wanted = call(request_kernel, [shape((peers, LANES), jnp.int32)], 1)(order.reshape(1, rows))
    asked = lax.all_to_all(wanted, "seq", split_axis=0, concat_axis=0, tiled=True)
    normed = call(
        norm_kernel,
        [shape((rows, width), BF16)],
        3,
        [pltpu.VMEM((rows, width), BF16), row_vector, row_vector, pltpu.SemaphoreType.DMA((3,))],
        flops=1_000_000_000,
        in_hbm=True,
    )(feats, norm_gain.reshape(1, width), norm_bias.reshape(1, width))
    staging = [pltpu.VMEM((slots, width), BF16), chunk_sems]
    picked = call(pick_kernel, [shape((slots, width), BF16)], 2, staging, out_hbm=True)(
        asked.reshape(peers, 1, LANES), normed
    )
    picked, asked, order, qkv_weight, qkv_bias, proj_weight, proj_bias = lax.optimization_barrier(
        (picked, asked, order, qkv_weight, qkv_bias, proj_weight, proj_bias)
    )
    arrived = lax.all_to_all(
        picked.reshape(peers, CAPACITY, width), "seq", split_axis=0, concat_axis=0, tiled=True
    )
    square, columns = shape((width, width), BF16), shape((width, LANES), F32)
    (
        arrange, send, place, query_t, key_weight, value_t, proj_t,
        query_bias, key_bias, value_bias, proj_bias_col,
    ) = call(
        setup_kernel,
        [
            shape((rows, slots), BF16), shape((slots, rows), BF16), shape((rows, slots), BF16),
            square, square, square, square, columns, shape((1, width), F32), columns, columns,
        ],
        6,
        flops=8_000_000_000,
    )(
        asked, order.reshape(1, rows), qkv_weight, qkv_bias.reshape(1, 3 * width), proj_weight,
        proj_bias.reshape(1, width),
    )
    halves = shape((middle, width), BF16)
    seq, cross, core = call(arrange_kernel, [shape((rows, width), BF16), halves, halves], 2)(
        arrived.reshape(slots, width), arrange
    )
    cross = lax.ppermute(cross, "seq", [(i, (i + 2 * (i % 2) - 1) % peers) for i in range(peers)])
    core = lax.ppermute(core, "seq", [(i, i + 1 - 2 * (i % 2)) for i in range(peers)])
    wide, tall = shape((half, rows), BF16), shape((rows, half), BF16)
    wide_s, tall_s = pltpu.VMEM((half, rows), BF16), pltpu.VMEM((rows, half), BF16)
    near, far_query, far_key, far_value = call(
        near_kernel, [wide, wide, tall, wide], 7, [wide_s, tall_s, wide_s], flops=6_000_000_000
    )(seq, query_t, key_weight, value_t, query_bias, key_bias, value_bias)
    outgoing = call(
        far_kernel,
        [shape((slots, width), BF16)],
        13,
        [
            pltpu.VMEM((width, rows), BF16), pltpu.VMEM((2, rows, half), BF16),
            pltpu.VMEM((2, half, rows), BF16), *staging,
        ],
        flops=6_000_000_000,
        out_hbm=True,
    )(
        cross, core, near, far_query, far_key, far_value, key_weight, key_bias, value_t, value_bias,
        proj_t, proj_bias_col, send,
    )
    returned = lax.all_to_all(
        outgoing.reshape(peers, CAPACITY, width), "seq", split_axis=0, concat_axis=0, tiled=True
    )
    return call(
        place_kernel,
        [shape((rows, width), BF16)],
        2,
        [pltpu.VMEM((rows, width), BF16), chunk_sems],
        out_hbm=True,
    )(returned.reshape(slots, width), place)


def solution(mesh):
    return jax.shard_map(
        per_device,
        mesh=mesh,
        in_specs=(P(("dp", "seq"), None), P(("dp", "seq")), P(), P(), P(), P(), P(), P()),
        out_specs=P(("dp", "seq"), None),
        check_vma=False,
    )
```

time: 207 us -> 160 us (0.77)
  Pallas kernels: 0 us -> 50.4 us
  matrix products: 49 us -> 0 us
  waiting for transfers between devices: 60.7 us -> 29.1 us
  local copies, waits for them, and re-layouts: 34.5 us -> 11.1 us
  other arithmetic: 9.81 us -> 0 us
  blocking collectives: 29.7 us -> 38.2 us
  starting transfers between devices: 21.7 us -> 29.8 us
    pallas_call x0 -> x8, Pallas kernels: none -> 50.4 us  [the longest x1 22.4 us: per_device(): call(far_kernel, [shape((slots, width), BF16)], 13, [pltpu.VMEM((width, r...]
    all_to_all x2, waiting for transfers between devices: 60.7 us -> 29.1 us  [the longest x1 20.5 us: per_device(): lax.all_to_all(picked.reshape(peers, CAPACITY, width), 'seq', split_axis=...]
    dot_general x14 -> x0, matrix products: 25.3 us -> none  [the longest x12 23.7 us: one_group(): jnp.einsum('hqk,khd->qhd', weights, value_heads, preferred_element_type=j...]
    sub x12 -> x0, matrix products: 23.8 us -> none  [one_group(): expanded = jnp.exp(scores - highest)]
    scatter x4 -> x0, local copies, waits for them, and re-layouts: 14.2 us -> none  [the longest x1 5.79 us: per_device(): return jnp.zeros_like(feats).at[asked.reshape(-1)].set(returned.reshape(-...]
    gather x4 -> x0, local copies, waits for them, and re-layouts: 12.9 us -> none  [the longest x2 6.98 us: per_device(): slot_sorted = holder[ranking] * capacity + positions - first_slot[ranking]]
    unnamed x22 -> x46, local copies, waits for them, and re-layouts: 2.03 us -> 11.1 us
    all_to_all x1, blocking collectives: 29.7 us -> 38.2 us  [per_device(): lax.all_to_all(outgoing.reshape(peers, CAPACITY, width), 'seq', split_axi...]
  transfers between devices with their start and end apart: 4 -> 4, of which waited for: 2 -> 2; matrix products, arithmetic and copies ran while one was open for 15% -> 0% of each run, Pallas kernels for 0% -> 15%
where the time goes in v2:
time: 160 us; the launch traced here: 159 us
  Pallas kernels  50.4 us (32%)
  blocking collectives  38.2 us (24%)
  starting transfers between devices  29.8 us (19%)
  waiting for transfers between devices  29.1 us (18%)
  local copies, waits for them, and re-layouts  11.1 us (7%)
    all_to_all x1, blocking collectives, per_device(): lax.all_to_all(outgoing.reshape(peers, CAPACITY, width), 'seq', split_axi...  38.2 us
    pallas_call x1, Pallas kernels, per_device(): call(far_kernel, [shape((slots, width), BF16)], 13, [pltpu.VMEM((width, r...  22.4 us
    pallas_call x1, Pallas kernels, per_device(): call(near_kernel, [wide, wide, tall, wide], 7, [wide_s, tall_s, wide_s],...  21.1 us
    all_to_all x1, waiting for transfers between devices, per_device(): lax.all_to_all(picked.reshape(peers, CAPACITY, width), 'seq', split_axis=...  20.5 us
    all_to_all x1, starting transfers between devices, per_device(): lax.all_to_all(wanted, 'seq', split_axis=0, concat_axis=0, tiled=True)  18.4 us
    unnamed x46, local copies, waits for them, and re-layouts  11.1 us
    all_to_all x1, waiting for transfers between devices, per_device(): lax.all_to_all(wanted, 'seq', split_axis=0, concat_axis=0, tiled=True)  8.58 us
    all_to_all x1, starting transfers between devices, per_device(): lax.all_to_all(picked.reshape(peers, CAPACITY, width), 'seq', split_axis=...  5.75 us
  transfers between devices with their start and end apart: 4, of which 2 were waited for; matrix products, arithmetic and copies ran while one was open for 0% of the time, Pallas kernels for 15%

profile of v2, /device:TPU:1, one launch (start us, length us, event | category | flops | bytes accessed | tf_op | source)
XLA Modules:
  0.0 159.1 jit_solution(4520120000753125119)
XLA Ops:
  0.7 1.1 request_kernel.1
  1.8 18.4 %all-to-all-start = ((s32[128,1,128]{2,1,0:T(1,128)}), s32[128,1,128]{2,1,0:T(1,128)S(1)}, u32[]{:S(2)}, u32[]{:S(2)}) async-start(s32[128,1,128]{2,1,0:T(1,128)} %bitcast.2), calls=%async_computation | async-start | bytes 131072 | tf_op jit(solution)/shard_map/all_to_all | solution.py:293
  20.2 1.0 copy-done.3
  23.1 8.6 %all-to-all-done.asked_ref = s32[128,1,128]{2,1,0:T(1,128)S(1)} async-done(((s32[128,1,128]{2,1,0:T(1,128)}), s32[128,1,128]{2,1,0:T(1,128)S(1)}, u32[]{:S(2)}, u32[]{:S(2)}) %all-to-all-start) | async-done | bytes 65568 | tf_op jit(solution)/shard_map/all_to_all | solution.py:293
  31.7 1.5 pick_kernel.1
  33.2 5.7 %all-to-all-start.1 = ((bf16[128,8,512]{2,1,0:T(8,128)(2,1)}), bf16[128,8,512]{2,1,0:T(8,128)(2,1)S(1)}, u32[]{:S(2)}, u32[]{:S(2)}) async-start(bf16[128,8,512]{2,1,0:T(8,128)(2,1)} %bitcast.6), calls=%async_computation.1 | async-start | bytes 2097152 | tf_op jit(solution)/shard_map/all_to_all | solution.py:309
  39.0 1.4 copy-done.2
  40.4 1.0 copy-done.4
  41.5 1.8 %setup_kernel.1 = (bf16[512,1024]{1,0:T(8,128)(2,1)S(1)}, bf16[1024,512]{1,0:T(8,128)(2,1)S(1)}, bf16[512,1024]{1,0:T(8,128)(2,1)S(1)}, bf16[512,512]{1,0:T(8,12...) custom-call(s32[128,128]{1,0:T(8,128)S(1)} %bitcast.16, ...), custom_call_target="tpu_custom_call" | custom-call | flops 8000000000 | bytes 4194304 | tf_op jit(solution)/shard_map/setup_kernel/pallas_call | solution.py:316
  43.3 1.0 copy-done.8
  44.3 0.8 copy-done.10
  45.0 0.8 copy-done.12
  45.9 0.8 copy-done.14
  46.7 0.8 copy-done.16
  47.5 0.7 copy-done.18
  48.1 0.7 copy-done.20
  48.8 20.5 %all-to-all-done.1 = bf16[128,8,512]{2,1,0:T(8,128)(2,1)S(1)} async-done(((bf16[128,8,512]{2,1,0:T(8,128)(2,1)}), bf16[128,8,512]{2,1,0:T(8,128)(2,1)S(1)}, u32[]{:S(2)}, u32[]{:S(2)}) %all-to-all-start.1) | async-done | bytes 1048608 | tf_op jit(solution)/shard_map/all_to_all | solution.py:309
  69.4 0.8 arrange_kernel.1
  70.1 3.7 %collective-permute-start = (bf16[256,512]{1,0:T(8,128)(2,1)S(1)}, bf16[256,512]{1,0:T(8,128)(2,1)S(1)}, u32[]{:S(2)}, u32[]{:S(2)}) collective-permute-start(bf16[256,512]{1,0:T(8,128)(2,1)S(1)} %get-tuple-element.38), channel_id=1, source_target_pairs={{0,127},{1,2},{2,1},{3,4},{4,3},{5,6},{6,5},{7,8},{8,7},{9,10},{10... | collective-permute-start | bytes 786440 | tf_op jit(solution)/shard_map/ppermute | solution.py:332
  73.8 1.9 %collective-permute-start.1 = (bf16[256,512]{1,0:T(8,128)(2,1)S(1)}, bf16[256,512]{1,0:T(8,128)(2,1)S(1)}, u32[]{:S(2)}, u32[]{:S(2)}) collective-permute-start(bf16[256,512]{1,0:T(8,128)(2,1)S(1)} %get-tuple-element.39), channel_id=1, source_target_pairs={{0,1},{1,0},{2,3},{3,2},{4,5},{5,4},{6,7},{7,6},{8,9},{9,8},{10,11... | collective-permute-start | bytes 786440 | tf_op jit(solution)/shard_map/ppermute | solution.py:333
  75.8 21.1 %near_kernel.1 = (bf16[256,512]{1,0:T(8,128)(2,1)S(1)}, bf16[256,512]{1,0:T(8,128)(2,1)S(1)}, bf16[512,256]{1,0:T(8,128)(2,1)S(1)}, bf16[256,512]{1,0:T(8,128)(2,1)S(1)}) custom-call(bf16[512,512]{1,0:T(8,128)(2,1)S(1)} %get-tuple-element.40.seq_ref, bf16[512,512]{1,0:T(8,128)(2,1)S(1)} %copy-done.17, bf16[512,512]{1,0:T(8,128)(2,1)S(1)} %copy-done.11, ...), custom_call_target="tpu_custom_call" | custom-call | flops 6000000000 | bytes 4194304 | tf_op jit(solution)/shard_map/near_kernel/pallas_call | solution.py:336
  96.9 22.4 %far_kernel.1 = bf16[1024,512]{1,0:T(8,128)(2,1)S(1)} custom-call(bf16[256,512]{1,0:T(8,128)(2,1)S(1)} %collective-permute-done.cross_ref, bf16[256,512]{1,0:T(8,128)(2,1)S(1)} %collective-permute-done.1.core_ref, bf16[256,512]{1,0:T(8,128)(2,1)S(1)} %get-tuple-element.47.near_ref, bf16[256,512]{1,0:T(8,128)(2,1)S(1)} %get-tuple-element.48.far_query_ref, ...), custom_call_target="tpu_custom_call" | custom-call | flops 6000000000 | bytes 4194304 | tf_op jit(solution)/shard_map/far_kernel/pallas_call | solution.py:339
  119.3 38.2 %all_to_all.22 = bf16[128,8,512]{2,1,0:T(8,128)(2,1)S(1)} all-to-all(bf16[128,8,512]{2,1,0:T(8,128)(2,1)S(1)} %bitcast.15), channel_id=1, replica_groups=mesh['dp'=4,'seq'=128] {'seq'}, dimensions={0} | all-to-all | bytes 2097152 | tf_op jit(solution)/shard_map/all_to_all | solution.py:353
  157.5 1.4 place_kernel.1
  (40 shorter events, 2.5 us)
Async XLA Ops:
  1.8 29.9 %all-to-all-start = ((s32[128,1,128]{2,1,0:T(1,128)}), s32[128,1,128]{2,1,0:T(1,128)S(1)}, u32[]{:S(2)}, u32[]{:S(2)}) async-start(s32[128,1,128]{2,1,0:T(1,128)} %bitcast.2), calls=%async_computation | async-start | bytes 131072 | tf_op jit(solution)/shard_map/all_to_all | solution.py:293
  20.2 1.0 copy-start.3
  23.1 15.9 %copy-start.22 = (f32[1536]{0:T(1024)S(1)}, f32[1536]{0:T(1024)}, u32[]{:S(2)}) copy-start(f32[1536]{0:T(1024)} %param.13) | copy-start | bytes 18436
  23.1 15.9 %copy-start.1 = (s32[512]{0:T(512)S(1)}, s32[512]{0:T(512)}, u32[]{:S(2)}) copy-start(s32[512]{0:T(512)} %param.9) | copy-start | bytes 6148
  23.1 15.9 %copy-start.7 = (f32[512]{0:T(512)S(1)}, f32[512]{0:T(512)}, u32[]{:S(2)}) copy-start(f32[512]{0:T(512)} %param.15) | copy-start | bytes 6148
  33.2 36.2 %all-to-all-start.1 = ((bf16[128,8,512]{2,1,0:T(8,128)(2,1)}), bf16[128,8,512]{2,1,0:T(8,128)(2,1)S(1)}, u32[]{:S(2)}, u32[]{:S(2)}) async-start(bf16[128,8,512]{2,1,0:T(8,128)(2,1)} %bitcast.6), calls=%async_computation.1 | async-start | bytes 2097152 | tf_op jit(solution)/shard_map/all_to_all | solution.py:309
  39.0 1.4 copy-start.2
  40.4 1.0 copy-start.4
  43.3 1.0 copy-start.8
  44.3 0.8 copy-start.10
  45.0 0.8 copy-start.12
  45.9 0.8 copy-start.14
  46.7 0.8 copy-start.16
  47.5 0.7 copy-start.18
  48.1 0.7 copy-start.20
  69.4 6.4 %copy-start.11 = (bf16[512,512]{1,0:T(8,128)(2,1)S(1)}, bf16[512,512]{1,0:T(8,128)(2,1)}, u32[]{:S(2)}) copy-start(bf16[512,512]{1,0:T(8,128)(2,1)} %copy-done.10) | copy-start | bytes 1572868
  69.4 6.4 %copy-start.13 = (bf16[512,512]{1,0:T(8,128)(2,1)S(1)}, bf16[512,512]{1,0:T(8,128)(2,1)}, u32[]{:S(2)}) copy-start(bf16[512,512]{1,0:T(8,128)(2,1)} %copy-done.12) | copy-start | bytes 1572868
  69.4 6.4 %copy-start.17 = (bf16[512,512]{1,0:T(8,128)(2,1)S(1)}, bf16[512,512]{1,0:T(8,128)(2,1)}, u32[]{:S(2)}) copy-start(bf16[512,512]{1,0:T(8,128)(2,1)} %copy-done.16) | copy-start | bytes 1572868
  69.4 6.4 %copy-start.21 = (f32[512,128]{1,0:T(8,128)S(1)}, f32[512,128]{1,0:T(8,128)}, u32[]{:S(2)}) copy-start(f32[512,128]{1,0:T(8,128)} %copy-done.20) | copy-start | bytes 786436
  70.1 26.7 %collective-permute-start = (bf16[256,512]{1,0:T(8,128)(2,1)S(1)}, bf16[256,512]{1,0:T(8,128)(2,1)S(1)}, u32[]{:S(2)}, u32[]{:S(2)}) collective-permute-start(bf16[256,512]{1,0:T(8,128)(2,1)S(1)} %get-tuple-element.38), channel_id=1, source_target_pairs={{0,127},{1,2},{2,1},{3,4},{4,3},{5,6},{6,5},{7,8},{8,7},{9,10},{10... | collective-permute-start | bytes 786440 | tf_op jit(solution)/shard_map/ppermute | solution.py:332
  73.8 23.1 %collective-permute-start.1 = (bf16[256,512]{1,0:T(8,128)(2,1)S(1)}, bf16[256,512]{1,0:T(8,128)(2,1)S(1)}, u32[]{:S(2)}, u32[]{:S(2)}) collective-permute-start(bf16[256,512]{1,0:T(8,128)(2,1)S(1)} %get-tuple-element.39), channel_id=1, source_target_pairs={{0,1},{1,0},{2,3},{3,2},{4,5},{5,4},{6,7},{7,6},{8,9},{9,8},{10,11... | collective-permute-start | bytes 786440 | tf_op jit(solution)/shard_map/ppermute | solution.py:333
  75.8 21.1 %copy-start.9 = (bf16[1024,512]{1,0:T(8,128)(2,1)S(1)}, bf16[1024,512]{1,0:T(8,128)(2,1)}, u32[]{:S(2)}) copy-start(bf16[1024,512]{1,0:T(8,128)(2,1)} %copy-done.8) | copy-start | bytes 3145732
  75.8 21.1 %copy-start.15 = (bf16[512,512]{1,0:T(8,128)(2,1)S(1)}, bf16[512,512]{1,0:T(8,128)(2,1)}, u32[]{:S(2)}) copy-start(bf16[512,512]{1,0:T(8,128)(2,1)} %copy-done.14) | copy-start | bytes 1572868
  75.8 21.1 %copy-start.19 = (f32[512,128]{1,0:T(8,128)S(1)}, f32[512,128]{1,0:T(8,128)}, u32[]{:S(2)}) copy-start(f32[512,128]{1,0:T(8,128)} %copy-done.18) | copy-start | bytes 786436
  (3 other events, 2.0 us)

commit v3 on v2

--- a/solution.py
+++ b/solution.py
@@ -116,6 +116,8 @@
     width = query_t_ref.shape[0]
     holder, _, rank_row = ranks(order_ref[...], peers)
     slot = holder * CAPACITY + rank_row
+    swapped = jnp.concatenate([slot[:, rows // 2 :], slot[:, : rows // 2]], axis=1)
+    slot = jnp.where(jnp.bitwise_and(lax.axis_index("seq"), 1) == 1, swapped, slot)
     send_ref[...] = onehot_of(iota((slots, rows), 0) == slot)
     slot_col = column(slot.astype(F32), rows).astype(jnp.int32)
     arrange_ref[...] = onehot_of(slot_col[:, :1] == iota((rows, slots), 1))
@@ -136,16 +138,12 @@
     proj_bias_col_ref[...] = column(proj_bias_ref[...], width)
 
 
-def odd_device():
-    return jnp.bitwise_and(lax.axis_index("seq"), 1)
-
-
 def arrange_kernel(arrived_ref, onehot_ref, seq_ref, cross_ref, core_ref):
     middle = cross_ref.shape[0]
-    seq_ref[...] = dot(onehot_ref[...], arrived_ref[...]).astype(BF16)
-    odd = odd_device()
-    cross_ref[...] = seq_ref[pl.ds(pl.multiple_of(odd * middle, middle), middle), :]
-    core_ref[...] = seq_ref[pl.ds(pl.multiple_of((1 - odd) * middle, middle), middle), :]
+    seq = dot(onehot_ref[...], arrived_ref[...]).astype(BF16)
+    seq_ref[...] = seq
+    cross_ref[...] = seq[:middle]
+    core_ref[...] = seq[middle:]
 
 
 def attend(queries_ref, sides, out_ref, out_start):
@@ -228,26 +226,42 @@
     attend(query_s, sides, attended_ref, 0)
 
 
-def far_kernel(
-    cross_ref, core_ref, near_ref, far_query_ref, far_key_ref, far_value_ref, key_ref, key_bias_ref,
+def extend(rows_ref, own, key_ref, key_bias_ref, value_t_ref, value_bias_ref, far_key_ref, far_value_ref, key_s, value_s):
+    middle, half = rows_ref.shape[0], key_s.shape[1]
+    keys = dot(rows_ref[...], key_ref[:, half:]) + key_bias_ref[:, half:]
+    key_s[:middle] = keys.astype(BF16)
+    values = dot_nt(value_t_ref[half:], rows_ref[...]) + value_bias_ref[half:, :1]
+    value_s[:, :middle] = values.astype(BF16)
+    key_s[middle:] = far_key_ref[own]
+    value_s[:, middle:] = far_value_ref[:, own]
+
+
+def core_kernel(
+    rows_ref, far_query_ref, far_key_ref, far_value_ref, key_ref, key_bias_ref, value_t_ref, value_bias_ref,
+    attended_ref, query_s, key_s, value_s,
+):
+    middle = rows_ref.shape[0]
+    own = slice(middle, 2 * middle)
+    extend(
+        rows_ref, own, key_ref, key_bias_ref, value_t_ref, value_bias_ref, far_key_ref, far_value_ref, key_s, value_s
+    )
+    query_s[...] = far_query_ref[:, own]
+    attend(query_s, [(key_s, value_s, 0, middle)], attended_ref, 0)
+
+
+def cross_kernel(
+    rows_ref, near_ref, core_ref, far_query_ref, far_key_ref, far_value_ref, key_ref, key_bias_ref,
     value_t_ref, value_bias_ref, proj_t_ref, proj_bias_ref, send_ref,
     outgoing_ref, attended_s, key_s, value_s, stage, sems,
 ):
-    half, rows = far_query_ref.shape
-    middle = rows // 2
+    middle, half = rows_ref.shape[0], near_ref.shape[0]
+    extend(
+        rows_ref, slice(0, middle), key_ref, key_bias_ref, value_t_ref, value_bias_ref, far_key_ref,
+        far_value_ref, key_s, value_s,
+    )
     attended_s[:half] = near_ref[...]
-    odd = odd_device()
-    for side, rows_ref in ((odd, cross_ref), (1 - odd, core_ref)):
-        keys = dot(rows_ref[...], key_ref[:, half:]) + key_bias_ref[:, half:]
-        key_s[side, :middle] = keys.astype(BF16)
-        values = dot_nt(value_t_ref[half:], rows_ref[...]) + value_bias_ref[half:, :1]
-        value_s[side, :, :middle] = values.astype(BF16)
-    for side in range(2):
-        part = slice(side * middle, (side + 1) * middle)
-        key_s[side, middle:] = far_key_ref[part]
-        value_s[side, :, middle:] = far_value_ref[:, part]
-    sides = [(key_s.at[0], value_s.at[0], 0, middle), (key_s.at[1], value_s.at[1], middle, rows)]
-    attend(far_query_ref, sides, attended_s, half)
+    attended_s[half:, middle:] = core_ref[...]
+    attend(far_query_ref, [(key_s, value_s, 0, middle)], attended_s, half)
     update = (dot(proj_t_ref[...], attended_s[...]) + proj_bias_ref[:, :1]).astype(BF16)
 
     def make(chunk, size):
@@ -336,18 +350,23 @@
     near, far_query, far_key, far_value = call(
         near_kernel, [wide, wide, tall, wide], 7, [wide_s, tall_s, wide_s], flops=6_000_000_000
     )(seq, query_t, key_weight, value_t, query_bias, key_bias, value_bias)
+    patch_s = [tall_s, wide_s]
+    core_attended = call(
+        core_kernel,
+        [shape((half, middle), BF16)],
+        8,
+        [pltpu.VMEM((half, middle), BF16), *patch_s],
+        flops=3_000_000_000,
+    )(core, far_query, far_key, far_value, key_weight, key_bias, value_t, value_bias)
     outgoing = call(
-        far_kernel,
+        cross_kernel,
         [shape((slots, width), BF16)],
         13,
-        [
-            pltpu.VMEM((width, rows), BF16), pltpu.VMEM((2, rows, half), BF16),
-            pltpu.VMEM((2, half, rows), BF16), *staging,
-        ],
+        [pltpu.VMEM((width, rows), BF16), *patch_s, *staging],
         flops=6_000_000_000,
         out_hbm=True,
     )(
-        cross, core, near, far_query, far_key, far_value, key_weight, key_bias, value_t, value_bias,
+        cross, near, core_attended, far_query, far_key, far_value, key_weight, key_bias, value_t, value_bias,
         proj_t, proj_bias_col, send,
     )
     returned = lax.all_to_all(

time: 160 us -> 161 us (level)
    pallas_call x1 -> x2, Pallas kernels: 22.4 us -> 23.7 us  [the longest x1 12.8 us: per_device(): call(cross_kernel, [shape((slots, width), BF16)], 13, [pltpu.VMEM((width,...]
  transfers between devices with their start and end apart: 4 -> 4, of which waited for: 2 -> 2; matrix products, arithmetic and copies ran while one was open for 0% -> 0% of each run, Pallas kernels for 15% -> 21%
where the time goes in v3:
time: 161 us; the launch traced here: 160 us
  Pallas kernels  51.7 us (32%)
  blocking collectives  38.2 us (24%)
  starting transfers between devices  29.8 us (19%)
  waiting for transfers between devices  29.1 us (18%)
  local copies, waits for them, and re-layouts  11.2 us (7%)
    all_to_all x1, blocking collectives, per_device(): lax.all_to_all(outgoing.reshape(peers, CAPACITY, width), 'seq', split_axi...  38.2 us
    pallas_call x1, Pallas kernels, per_device(): call(near_kernel, [wide, wide, tall, wide], 7, [wide_s, tall_s, wide_s],...  21 us
    all_to_all x1, waiting for transfers between devices, per_device(): lax.all_to_all(picked.reshape(peers, CAPACITY, width), 'seq', split_axis=...  20.5 us
    all_to_all x1, starting transfers between devices, per_device(): lax.all_to_all(wanted, 'seq', split_axis=0, concat_axis=0, tiled=True)  18.4 us
    pallas_call x1, Pallas kernels, per_device(): call(cross_kernel, [shape((slots, width), BF16)], 13, [pltpu.VMEM((width,...  12.8 us
    unnamed x46, local copies, waits for them, and re-layouts  11.2 us
    pallas_call x1, Pallas kernels, per_device(): call(core_kernel, [shape((half, middle), BF16)], 8, [pltpu.VMEM((half, mi...  10.9 us
    all_to_all x1, waiting for transfers between devices, per_device(): lax.all_to_all(wanted, 'seq', split_axis=0, concat_axis=0, tiled=True)  8.58 us
  transfers between devices with their start and end apart: 4, of which 2 were waited for; matrix products, arithmetic and copies ran while one was open for 0% of the time, Pallas kernels for 21%

profile of v3, /device:TPU:1, one launch (start us, length us, event | category | flops | bytes accessed | tf_op | source)
XLA Modules:
  0.0 160.4 jit_solution(15832965294264045575)
XLA Ops:
  0.7 1.1 request_kernel.1
  1.8 18.4 %all-to-all-start = ((s32[128,1,128]{2,1,0:T(1,128)}), s32[128,1,128]{2,1,0:T(1,128)S(1)}, u32[]{:S(2)}, u32[]{:S(2)}) async-start(s32[128,1,128]{2,1,0:T(1,128)} %bitcast.2), calls=%async_computation | async-start | bytes 131072 | tf_op jit(solution)/shard_map/all_to_all | solution.py:307
  20.2 1.0 copy-done.3
  23.1 8.6 %all-to-all-done.asked_ref = s32[128,1,128]{2,1,0:T(1,128)S(1)} async-done(((s32[128,1,128]{2,1,0:T(1,128)}), s32[128,1,128]{2,1,0:T(1,128)S(1)}, u32[]{:S(2)}, u32[]{:S(2)}) %all-to-all-start) | async-done | bytes 65568 | tf_op jit(solution)/shard_map/all_to_all | solution.py:307
  31.7 1.5 pick_kernel.1
  33.2 5.7 %all-to-all-start.1 = ((bf16[128,8,512]{2,1,0:T(8,128)(2,1)}), bf16[128,8,512]{2,1,0:T(8,128)(2,1)S(1)}, u32[]{:S(2)}, u32[]{:S(2)}) async-start(bf16[128,8,512]{2,1,0:T(8,128)(2,1)} %bitcast.6), calls=%async_computation.1 | async-start | bytes 2097152 | tf_op jit(solution)/shard_map/all_to_all | solution.py:323
  39.0 1.4 copy-done.2
  40.4 1.0 copy-done.4
  41.5 1.8 %setup_kernel.1 = (bf16[512,1024]{1,0:T(8,128)(2,1)S(1)}, bf16[1024,512]{1,0:T(8,128)(2,1)S(1)}, bf16[512,1024]{1,0:T(8,128)(2,1)S(1)}, bf16[512,512]{1,0:T(8,12...) custom-call(s32[128,128]{1,0:T(8,128)S(1)} %bitcast.16, ...), custom_call_target="tpu_custom_call" | custom-call | flops 8000000000 | bytes 4194304 | tf_op jit(solution)/shard_map/setup_kernel/pallas_call | solution.py:330
  43.3 0.8 copy-done.8
  44.1 0.8 copy-done.10
  44.9 1.0 copy-done.12
  45.9 0.8 copy-done.14
  46.7 0.8 copy-done.16
  48.2 0.7 copy-done.20
  48.9 20.5 %all-to-all-done.1 = bf16[128,8,512]{2,1,0:T(8,128)(2,1)S(1)} async-done(((bf16[128,8,512]{2,1,0:T(8,128)(2,1)}), bf16[128,8,512]{2,1,0:T(8,128)(2,1)S(1)}, u32[]{:S(2)}, u32[]{:S(2)}) %all-to-all-start.1) | async-done | bytes 1048608 | tf_op jit(solution)/shard_map/all_to_all | solution.py:323
  69.4 0.7 arrange_kernel.1
  70.1 3.7 %collective-permute-start = (bf16[256,512]{1,0:T(8,128)(2,1)S(1)}, bf16[256,512]{1,0:T(8,128)(2,1)S(1)}, u32[]{:S(2)}, u32[]{:S(2)}) collective-permute-start(bf16[256,512]{1,0:T(8,128)(2,1)S(1)} %get-tuple-element.38), channel_id=1, source_target_pairs={{0,127},{1,2},{2,1},{3,4},{4,3},{5,6},{6,5},{7,8},{8,7},{9,10},{10... | collective-permute-start | bytes 786440 | tf_op jit(solution)/shard_map/ppermute | solution.py:346
  73.8 1.9 %collective-permute-start.1 = (bf16[256,512]{1,0:T(8,128)(2,1)S(1)}, bf16[256,512]{1,0:T(8,128)(2,1)S(1)}, u32[]{:S(2)}, u32[]{:S(2)}) collective-permute-start(bf16[256,512]{1,0:T(8,128)(2,1)S(1)} %get-tuple-element.47), channel_id=1, source_target_pairs={{0,1},{1,0},{2,3},{3,2},{4,5},{5,4},{6,7},{7,6},{8,9},{9,8},{10,11... | collective-permute-start | bytes 786440 | tf_op jit(solution)/shard_map/ppermute | solution.py:347
  75.7 21.0 %near_kernel.1 = (bf16[256,512]{1,0:T(8,128)(2,1)S(1)}, bf16[256,512]{1,0:T(8,128)(2,1)S(1)}, bf16[512,256]{1,0:T(8,128)(2,1)S(1)}, bf16[256,512]{1,0:T(8,128)(2,1)S(1)}) custom-call(bf16[512,512]{1,0:T(8,128)(2,1)S(1)} %get-tuple-element.39.seq_ref, bf16[512,512]{1,0:T(8,128)(2,1)S(1)} %copy-done.17, bf16[512,512]{1,0:T(8,128)(2,1)S(1)} %copy-done.9, ...), custom_call_target="tpu_custom_call" | custom-call | flops 6000000000 | bytes 4194304 | tf_op jit(solution)/shard_map/near_kernel/pallas_call | solution.py:350
  96.8 10.9 %core_kernel.1.core_ref = bf16[256,256]{1,0:T(8,128)(2,1)S(1)} custom-call(bf16[256,512]{1,0:T(8,128)(2,1)S(1)} %collective-permute-done.1.rows_ref, bf16[256,512]{1,0:T(8,128)(2,1)S(1)} %get-tuple-element.48.far_query_ref, bf16[512,256]{1,0:T(8,128)(2,1)S(1)} %get-tuple-element.49.far_key_ref, bf16[256,512]{1,0:T(8,128)(2,1)S(1)} %get-tuple-element.50.far_value_ref, ...), custom_call_target="tpu_custom_call" | custom-call | flops 3000000000 | bytes 4194304 | tf_op jit(solution)/shard_map/core_kernel/pallas_call | solution.py:354
  107.8 12.8 %cross_kernel.1 = bf16[1024,512]{1,0:T(8,128)(2,1)S(1)} custom-call(bf16[256,512]{1,0:T(8,128)(2,1)S(1)} %collective-permute-done.rows_ref, bf16[256,512]{1,0:T(8,128)(2,1)S(1)} %get-tuple-element.46.near_ref, bf16[256,256]{1,0:T(8,128)(2,1)S(1)} %core_kernel.1.core_ref, bf16[256,512]{1,0:T(8,128)(2,1)S(1)} %get-tuple-element.48.far_query_ref, ...), custom_call_target="tpu_custom_call" | custom-call | flops 6000000000 | bytes 4194304 | tf_op jit(solution)/shard_map/cross_kernel/pallas_call | solution.py:361
  120.6 38.2 %all_to_all.22 = bf16[128,8,512]{2,1,0:T(8,128)(2,1)S(1)} all-to-all(bf16[128,8,512]{2,1,0:T(8,128)(2,1)S(1)} %bitcast.15), channel_id=1, replica_groups=mesh['dp'=4,'seq'=128] {'seq'}, dimensions={0} | all-to-all | bytes 2097152 | tf_op jit(solution)/shard_map/all_to_all | solution.py:372
  158.8 1.4 place_kernel.1
  (41 shorter events, 3.2 us)
Async XLA Ops:
  1.8 29.9 %all-to-all-start = ((s32[128,1,128]{2,1,0:T(1,128)}), s32[128,1,128]{2,1,0:T(1,128)S(1)}, u32[]{:S(2)}, u32[]{:S(2)}) async-start(s32[128,1,128]{2,1,0:T(1,128)} %bitcast.2), calls=%async_computation | async-start | bytes 131072 | tf_op jit(solution)/shard_map/all_to_all | solution.py:307
  20.2 1.0 copy-start.3
  23.1 15.9 %copy-start.22 = (f32[1536]{0:T(1024)S(1)}, f32[1536]{0:T(1024)}, u32[]{:S(2)}) copy-start(f32[1536]{0:T(1024)} %param.13) | copy-start | bytes 18436
  23.1 15.9 %copy-start.1 = (s32[512]{0:T(512)S(1)}, s32[512]{0:T(512)}, u32[]{:S(2)}) copy-start(s32[512]{0:T(512)} %param.9) | copy-start | bytes 6148
  23.1 15.9 %copy-start.7 = (f32[512]{0:T(512)S(1)}, f32[512]{0:T(512)}, u32[]{:S(2)}) copy-start(f32[512]{0:T(512)} %param.15) | copy-start | bytes 6148
  33.2 36.2 %all-to-all-start.1 = ((bf16[128,8,512]{2,1,0:T(8,128)(2,1)}), bf16[128,8,512]{2,1,0:T(8,128)(2,1)S(1)}, u32[]{:S(2)}, u32[]{:S(2)}) async-start(bf16[128,8,512]{2,1,0:T(8,128)(2,1)} %bitcast.6), calls=%async_computation.1 | async-start | bytes 2097152 | tf_op jit(solution)/shard_map/all_to_all | solution.py:323
  39.0 1.4 copy-start.2
  40.4 1.0 copy-start.4
  43.3 0.8 copy-start.8
  44.1 0.8 copy-start.10
  44.9 1.0 copy-start.12
  45.9 0.8 copy-start.14
  46.7 0.8 copy-start.16
  47.5 0.7 copy-start.18
  48.2 0.7 copy-start.20
  69.4 6.3 %copy-start.9 = (bf16[512,512]{1,0:T(8,128)(2,1)S(1)}, bf16[512,512]{1,0:T(8,128)(2,1)}, u32[]{:S(2)}) copy-start(bf16[512,512]{1,0:T(8,128)(2,1)} %copy-done.8) | copy-start | bytes 1572868
  69.4 6.4 %copy-start.11 = (bf16[512,512]{1,0:T(8,128)(2,1)S(1)}, bf16[512,512]{1,0:T(8,128)(2,1)}, u32[]{:S(2)}) copy-start(bf16[512,512]{1,0:T(8,128)(2,1)} %copy-done.10) | copy-start | bytes 1572868
  69.4 6.4 %copy-start.17 = (bf16[512,512]{1,0:T(8,128)(2,1)S(1)}, bf16[512,512]{1,0:T(8,128)(2,1)}, u32[]{:S(2)}) copy-start(bf16[512,512]{1,0:T(8,128)(2,1)} %copy-done.16) | copy-start | bytes 1572868
  69.4 6.4 %copy-start.21 = (f32[512,128]{1,0:T(8,128)S(1)}, f32[512,128]{1,0:T(8,128)}, u32[]{:S(2)}) copy-start(f32[512,128]{1,0:T(8,128)} %copy-done.20) | copy-start | bytes 786436
  70.1 37.7 %collective-permute-start = (bf16[256,512]{1,0:T(8,128)(2,1)S(1)}, bf16[256,512]{1,0:T(8,128)(2,1)S(1)}, u32[]{:S(2)}, u32[]{:S(2)}) collective-permute-start(bf16[256,512]{1,0:T(8,128)(2,1)S(1)} %get-tuple-element.38), channel_id=1, source_target_pairs={{0,127},{1,2},{2,1},{3,4},{4,3},{5,6},{6,5},{7,8},{8,7},{9,10},{10... | collective-permute-start | bytes 786440 | tf_op jit(solution)/shard_map/ppermute | solution.py:346
  73.8 23.0 %collective-permute-start.1 = (bf16[256,512]{1,0:T(8,128)(2,1)S(1)}, bf16[256,512]{1,0:T(8,128)(2,1)S(1)}, u32[]{:S(2)}, u32[]{:S(2)}) collective-permute-start(bf16[256,512]{1,0:T(8,128)(2,1)S(1)} %get-tuple-element.47), channel_id=1, source_target_pairs={{0,1},{1,0},{2,3},{3,2},{4,5},{5,4},{6,7},{7,6},{8,9},{9,8},{10,11... | collective-permute-start | bytes 786440 | tf_op jit(solution)/shard_map/ppermute | solution.py:347
  96.8 11.0 %copy-start.13 = (bf16[1024,512]{1,0:T(8,128)(2,1)S(1)}, bf16[1024,512]{1,0:T(8,128)(2,1)}, u32[]{:S(2)}) copy-start(bf16[1024,512]{1,0:T(8,128)(2,1)} %copy-done.12) | copy-start | bytes 3145732
  96.8 11.0 %copy-start.15 = (bf16[512,512]{1,0:T(8,128)(2,1)S(1)}, bf16[512,512]{1,0:T(8,128)(2,1)}, u32[]{:S(2)}) copy-start(bf16[512,512]{1,0:T(8,128)(2,1)} %copy-done.14) | copy-start | bytes 1572868
  96.8 11.0 %copy-start.19 = (f32[512,128]{1,0:T(8,128)S(1)}, f32[512,128]{1,0:T(8,128)}, u32[]{:S(2)}) copy-start(f32[512,128]{1,0:T(8,128)} %copy-done.18) | copy-start | bytes 786436
  (3 other events, 2.0 us)

commit v4 on v3

--- a/solution.py
+++ b/solution.py
@@ -40,8 +40,11 @@
     return holder, mine_bf, rank_row
 
 
-def request_kernel(order_ref, wanted_ref):
-    order_row = order_ref[...]
+def request_kernel(order_ref, wanted_ref, order_s, sem):
+    copy = pltpu.make_async_copy(order_ref, order_s, sem)
+    copy.start()
+    copy.wait()
+    order_row = order_s[...]
     peers = wanted_ref.shape[0]
     rows = order_row.shape[1]
     _, mine_bf, rank_row = ranks(order_row, peers)
@@ -56,32 +59,32 @@
     return jnp.transpose(jnp.broadcast_to(row, (LANES, count)))
 
 
-def norm_kernel(feats_ref, gain_ref, bias_ref, normed_ref, feats_s, gain_s, bias_s, sems):
-    copies = [
-        pltpu.make_async_copy(feats_ref, feats_s, sems.at[0]),
-        pltpu.make_async_copy(gain_ref, gain_s, sems.at[1]),
-        pltpu.make_async_copy(bias_ref, bias_s, sems.at[2]),
-    ]
+def norm_kernel(own_ref, other_ref, gain_ref, bias_ref, normed_ref, own_s, other_s, gain_s, bias_s, sems):
+    rows = own_s.shape[0]
+    pairs = [(own_ref, own_s), (other_ref, other_s), (gain_ref, gain_s), (bias_ref, bias_s)]
+    copies = [pltpu.make_async_copy(source, target, sems.at[i]) for i, (source, target) in enumerate(pairs)]
     for copy in copies:
         copy.start()
     for copy in copies:
         copy.wait()
-    values = feats_s[...].astype(F32)
-    center = jnp.mean(values, axis=-1, keepdims=True)
-    spread = jnp.mean(jnp.square(values - center), axis=-1, keepdims=True)
-    normed_ref[...] = (
-        (values - center) * lax.rsqrt(spread + 1e-05) * gain_s[...] + bias_s[...]
-    ).astype(BF16)
+    odd = jnp.bitwise_and(lax.axis_index("seq"), 1)
+    for start, source in ((odd * rows, own_s), ((1 - odd) * rows, other_s)):
+        values = source[...].astype(F32)
+        center = jnp.mean(values, axis=-1, keepdims=True)
+        spread = jnp.mean(jnp.square(values - center), axis=-1, keepdims=True)
+        normed_ref[pl.ds(pl.multiple_of(start, rows), rows), :] = (
+            (values - center) * lax.rsqrt(spread + 1e-05) * gain_s[...] + bias_s[...]
+        ).astype(BF16)
 
 
 def onehot_of(equal):
     return jnp.where(equal, 1.0, 0.0).astype(BF16)
 
 
-def send_chunks(make, out_ref, stage, sems):
-    size = stage.shape[0] // CHUNKS
+def send_chunks(make, out_ref, stage, sems, chunks=CHUNKS):
+    size = stage.shape[0] // chunks
     copies = []
-    for chunk in range(CHUNKS):
+    for chunk in range(chunks):
         part = pl.ds(chunk * size, size)
         stage[part, :] = make(chunk, size)
         copies.append(pltpu.make_async_copy(stage.at[part, :], out_ref.at[part, :], sems.at[chunk]))
@@ -91,28 +94,32 @@
 
 
 def pick_kernel(asked_ref, normed_ref, picked_ref, stage, sems):
-    rows = normed_ref.shape[0]
-    normed = normed_ref[...]
+    rows = normed_ref.shape[0] // 2
 
     def make(chunk, size):
-        peers = size // CAPACITY
-        asked = asked_ref[chunk * peers : (chunk + 1) * peers]
-        spread = jnp.broadcast_to(asked, (peers, CAPACITY, LANES))
-        own = iota(spread.shape, 1) == iota(spread.shape, 2)
-        index = jnp.where(own, spread, 0).reshape(size, LANES).astype(F32)
-        index = jnp.sum(index, axis=1, keepdims=True).astype(jnp.int32) - 1
-        return dot(onehot_of(index == iota((size, rows), 1)), normed).astype(BF16)
-
-    send_chunks(make, picked_ref, stage, sems)
+        chips = size // (2 * CAPACITY)
+        parts = []
+        for core in range(2):
+            asked = asked_ref[chunk * chips : (chunk + 1) * chips, core : core + 1]
+            spread = jnp.broadcast_to(asked, (chips, CAPACITY, LANES))
+            own = iota(spread.shape, 1) == iota(spread.shape, 2)
+            index = jnp.where(own, spread, 0).reshape(chips * CAPACITY, LANES).astype(F32)
+            index = jnp.sum(index, axis=1, keepdims=True).astype(jnp.int32) - 1
+            onehot = onehot_of(index == iota((chips * CAPACITY, rows), 1))
+            part = dot(onehot, normed_ref[core * rows : (core + 1) * rows])
+            parts.append(part.reshape(chips, CAPACITY, part.shape[1]))
+        return jnp.concatenate(parts, axis=1).reshape(size, parts[0].shape[2]).astype(BF16)
+
+    send_chunks(make, picked_ref, stage, sems, 2)
 
 
 def setup_kernel(
-    asked_ref, order_ref, qkv_weight_ref, qkv_bias_ref, proj_weight_ref, proj_bias_ref,
-    arrange_ref, send_ref, place_ref, query_t_ref, key_ref, value_t_ref, proj_t_ref,
+    order_ref, qkv_weight_ref, qkv_bias_ref, proj_weight_ref, proj_bias_ref,
+    arrange_ref, send_ref, query_t_ref, key_ref, value_t_ref, proj_t_ref,
     query_bias_ref, key_bias_ref, value_bias_ref, proj_bias_col_ref,
 ):
-    peers = asked_ref.shape[0]
     rows, slots = arrange_ref.shape
+    peers = slots // CAPACITY
     width = query_t_ref.shape[0]
     holder, _, rank_row = ranks(order_ref[...], peers)
     slot = holder * CAPACITY + rank_row
@@ -121,13 +128,6 @@
     send_ref[...] = onehot_of(iota((slots, rows), 0) == slot)
     slot_col = column(slot.astype(F32), rows).astype(jnp.int32)
     arrange_ref[...] = onehot_of(slot_col[:, :1] == iota((rows, slots), 1))
-    flipped = jnp.transpose(asked_ref[...].astype(F32)).astype(jnp.int32)
-    expand = onehot_of(jnp.right_shift(iota((peers, slots), 1), 3) == iota((peers, slots), 0))
-    high = dot(jnp.right_shift(flipped, 4).astype(F32).astype(BF16), expand)
-    low = dot(jnp.bitwise_and(flipped, 15).astype(F32).astype(BF16), expand)
-    own = jnp.bitwise_and(iota((LANES, slots), 1), CAPACITY - 1) == iota((LANES, slots), 0)
-    asked_row = jnp.sum(jnp.where(own, high * 16.0 + low, 0.0), axis=0, keepdims=True).astype(jnp.int32)
-    place_ref[...] = onehot_of(iota((rows, slots), 0) + 1 == asked_row)
     query_t_ref[...] = jnp.transpose(qkv_weight_ref[:, :width])
     key_ref[...] = qkv_weight_ref[:, width : 2 * width]
     value_t_ref[...] = jnp.transpose(qkv_weight_ref[:, 2 * width :])
@@ -136,6 +136,22 @@
     key_bias_ref[...] = qkv_bias_ref[:, width : 2 * width]
     value_bias_ref[...] = column(qkv_bias_ref[:, 2 * width :], width)
     proj_bias_col_ref[...] = column(proj_bias_ref[...], width)
+
+
+def place_setup_kernel(mine_ref, other_ref, place_ref):
+    rows, slots = place_ref.shape
+    chips = mine_ref.shape[0]
+    asked = jnp.concatenate([mine_ref[...], other_ref[...]], axis=0)
+    flipped = jnp.transpose(asked.astype(F32)).astype(jnp.int32)
+    source, slot = iota((2 * chips, slots), 0), iota((2 * chips, slots), 1)
+    core = jnp.bitwise_xor(jnp.bitwise_and(lax.axis_index("seq"), 1), (source >= chips).astype(jnp.int32))
+    owner = jnp.bitwise_and(source, chips - 1) * 2 + core
+    expand = onehot_of(jnp.right_shift(slot, 3) == owner)
+    high = dot(jnp.right_shift(flipped, 4).astype(F32).astype(BF16), expand)
+    low = dot(jnp.bitwise_and(flipped, 15).astype(F32).astype(BF16), expand)
+    own = jnp.bitwise_and(iota((LANES, slots), 1), CAPACITY - 1) == iota((LANES, slots), 0)
+    asked_row = jnp.sum(jnp.where(own, high * 16.0 + low, 0.0), axis=0, keepdims=True).astype(jnp.int32)
+    place_ref[...] = onehot_of(iota((rows, slots), 0) + 1 == asked_row)
 
 
 def arrange_kernel(arrived_ref, onehot_ref, seq_ref, cross_ref, core_ref):
@@ -303,48 +319,66 @@
     chunk_sems = pltpu.SemaphoreType.DMA((CHUNKS,))
     row_vector = pltpu.VMEM((1, width), F32)
 
-    wanted = call(request_kernel, [shape((peers, LANES), jnp.int32)], 1)(order.reshape(1, rows))
-    asked = lax.all_to_all(wanted, "seq", split_axis=0, concat_axis=0, tiled=True)
+    chips = peers // 2
+    same_core = [list(range(core, peers, 2)) for core in range(2)]
+    core_pairs = [(i, i + 1 - 2 * (i % 2)) for i in range(peers)]
+    wanted = call(
+        request_kernel,
+        [shape((peers, LANES), jnp.int32)],
+        1,
+        [pltpu.VMEM((1, rows), jnp.int32), pltpu.SemaphoreType.DMA],
+        in_hbm=True,
+    )(order.reshape(1, rows))
+    wanted, feats = lax.optimization_barrier((wanted, feats))
+    asked = lax.all_to_all(
+        wanted.reshape(chips, 2, LANES), "seq", split_axis=0, concat_axis=0, axis_index_groups=same_core, tiled=True
+    )
+    other_feats = lax.ppermute(feats, "seq", core_pairs)
     normed = call(
         norm_kernel,
-        [shape((rows, width), BF16)],
-        3,
-        [pltpu.VMEM((rows, width), BF16), row_vector, row_vector, pltpu.SemaphoreType.DMA((3,))],
+        [shape((2 * rows, width), BF16)],
+        4,
+        [
+            pltpu.VMEM((rows, width), BF16), pltpu.VMEM((rows, width), BF16), row_vector, row_vector,
+            pltpu.SemaphoreType.DMA((4,)),
+        ],
         flops=1_000_000_000,
         in_hbm=True,
-    )(feats, norm_gain.reshape(1, width), norm_bias.reshape(1, width))
+    )(feats, other_feats, norm_gain.reshape(1, width), norm_bias.reshape(1, width))
     staging = [pltpu.VMEM((slots, width), BF16), chunk_sems]
     picked = call(pick_kernel, [shape((slots, width), BF16)], 2, staging, out_hbm=True)(
-        asked.reshape(peers, 1, LANES), normed
+        asked, normed
     )
     picked, asked, order, qkv_weight, qkv_bias, proj_weight, proj_bias = lax.optimization_barrier(
         (picked, asked, order, qkv_weight, qkv_bias, proj_weight, proj_bias)
     )
     arrived = lax.all_to_all(
-        picked.reshape(peers, CAPACITY, width), "seq", split_axis=0, concat_axis=0, tiled=True
+        picked.reshape(chips, 2 * CAPACITY, width), "seq", split_axis=0, concat_axis=0,
+        axis_index_groups=same_core, tiled=True,
     )
     square, columns = shape((width, width), BF16), shape((width, LANES), F32)
     (
-        arrange, send, place, query_t, key_weight, value_t, proj_t,
+        arrange, send, query_t, key_weight, value_t, proj_t,
         query_bias, key_bias, value_bias, proj_bias_col,
     ) = call(
         setup_kernel,
         [
-            shape((rows, slots), BF16), shape((slots, rows), BF16), shape((rows, slots), BF16),
-            square, square, square, square, columns, shape((1, width), F32), columns, columns,
+            shape((rows, slots), BF16), shape((slots, rows), BF16), square, square, square, square, columns, shape((1, width), F32), columns, columns,
         ],
-        6,
+        5,
         flops=8_000_000_000,
-    )(
-        asked, order.reshape(1, rows), qkv_weight, qkv_bias.reshape(1, 3 * width), proj_weight,
-        proj_bias.reshape(1, width),
-    )
+    )(order.reshape(1, rows), qkv_weight, qkv_bias.reshape(1, 3 * width), proj_weight, proj_bias.reshape(1, width))
+    asked, key_bias = lax.optimization_barrier((asked, key_bias))
+    odd = lax.axis_index("seq") % 2 == 1
+    mine = jnp.where(odd, asked[:, 1], asked[:, 0])
+    other = lax.ppermute(jnp.where(odd, asked[:, 0], asked[:, 1]), "seq", core_pairs)
+    place = call(place_setup_kernel, [shape((rows, slots), BF16)], 2, flops=2_000_000_000)(mine, other)
     halves = shape((middle, width), BF16)
     seq, cross, core = call(arrange_kernel, [shape((rows, width), BF16), halves, halves], 2)(
         arrived.reshape(slots, width), arrange
     )
     cross = lax.ppermute(cross, "seq", [(i, (i + 2 * (i % 2) - 1) % peers) for i in range(peers)])
-    core = lax.ppermute(core, "seq", [(i, i + 1 - 2 * (i % 2)) for i in range(peers)])
+    core = lax.ppermute(core, "seq", core_pairs)
     wide, tall = shape((half, rows), BF16), shape((rows, half), BF16)
     wide_s, tall_s = pltpu.VMEM((half, rows), BF16), pltpu.VMEM((rows, half), BF16)
     near, far_query, far_key, far_value = call(

time: 161 us -> 161 us (level)
  blocking collectives: 38.2 us -> 0 us
  waiting for transfers between devices: 29.1 us -> 53.7 us
  starting transfers between devices: 29.8 us -> 44.4 us
  local copies, waits for them, and re-layouts: 11.2 us -> 9.33 us
    all_to_all x1 -> x0, blocking collectives: 38.2 us -> none  [per_device(): lax.all_to_all(outgoing.reshape(peers, CAPACITY, width), 'seq', split_axi...]
    all_to_all x2 -> x3, waiting for transfers between devices: 29.1 us -> 52.9 us  [the longest x1 26.2 us: per_device(): lax.all_to_all(outgoing.reshape(peers, CAPACITY, width), 'seq', split_axi...]
    ppermute x1 -> x3, starting transfers between devices: 1.92 us -> 13.6 us  [the longest x1 8.79 us: per_device(): other_feats = lax.ppermute(feats, 'seq', core_pairs)]
    ppermute x1, starting transfers between devices: 3.68 us -> 5.94 us  [per_device(): lax.ppermute(cross, 'seq', [(i, (i + 2 * (i % 2) - 1) % peers) for i in r...]
    unnamed x46 -> x42, local copies, waits for them, and re-layouts: 11.2 us -> 9.32 us
    all_to_all x2 -> x3, starting transfers between devices: 24.2 us -> 24.8 us  [the longest x1 10.9 us: per_device(): lax.all_to_all(wanted.reshape(chips, 2, LANES), 'seq', split_axis=0, conc...]
  transfers between devices with their start and end apart: 4 -> 7, of which waited for: 2 -> 4; matrix products, arithmetic and copies ran while one was open for 0% -> 0% of each run, Pallas kernels for 21% -> 22%
where the time goes in v4:
time: 161 us; the launch traced here: 160 us
  waiting for transfers between devices  53.7 us (33%)
  Pallas kernels  52.5 us (33%)
  starting transfers between devices  44.4 us (28%)
  local copies, waits for them, and re-layouts  9.33 us (6%)
    all_to_all x1, waiting for transfers between devices, per_device(): lax.all_to_all(outgoing.reshape(peers, CAPACITY, width), 'seq', split_axi...  26.2 us
    pallas_call x1, Pallas kernels, per_device(): call(near_kernel, [wide, wide, tall, wide], 7, [wide_s, tall_s, wide_s],...  21 us
    all_to_all x1, waiting for transfers between devices, per_device(): lax.all_to_all(picked.reshape(chips, 2 * CAPACITY, width), 'seq', split_a...  18.8 us
    pallas_call x1, Pallas kernels, per_device(): call(cross_kernel, [shape((slots, width), BF16)], 13, [pltpu.VMEM((width,...  12.8 us
    all_to_all x1, starting transfers between devices, per_device(): lax.all_to_all(wanted.reshape(chips, 2, LANES), 'seq', split_axis=0, conc...  10.9 us
    pallas_call x1, Pallas kernels, per_device(): call(core_kernel, [shape((half, middle), BF16)], 8, [pltpu.VMEM((half, mi...  10.9 us
    unnamed x42, local copies, waits for them, and re-layouts  9.32 us
    all_to_all x1, starting transfers between devices, per_device(): lax.all_to_all(outgoing.reshape(peers, CAPACITY, width), 'seq', split_axi...  9.1 us
  transfers between devices with their start and end apart: 7, of which 4 were waited for; matrix products, arithmetic and copies ran while one was open for 0% of the time, Pallas kernels for 22%

profile of v4, /device:TPU:1, one launch (start us, length us, event | category | flops | bytes accessed | tf_op | source)
XLA Modules:
  0.0 160.4 jit_solution(6108953054923915520)
XLA Ops:
  0.7 1.1 request_kernel.1
  1.8 8.8 %collective-permute-start = (bf16[512,512]{1,0:T(8,128)(2,1)}, bf16[512,512]{1,0:T(8,128)(2,1)S(1)}, u32[]{:S(2)}, u32[]{:S(2)}) collective-permute-start(bf16[512,512]{1,0:T(8,128)(2,1)} %own_ref), channel_id=1, source_target_pairs={{0,1},{1,0},{2,3},{3,2},{4,5},{5,4},{6,7},{7,6},{8,9},{9,8},{10,11... | collective-permute-start | bytes 1572872 | tf_op jit(solution)/shard_map/ppermute | solution.py:336
  10.6 10.9 %all-to-all-start = ((s32[64,2,128]{2,1,0:T(2,128)}), s32[64,2,128]{2,1,0:T(2,128)S(1)}, u32[]{:S(2)}, u32[]{:S(2)}) async-start(s32[64,2,128]{2,1,0:T(2,128)} %bitcast.1), calls=%async_computation | async-start | bytes 131072 | tf_op jit(solution)/shard_map/all_to_all | solution.py:333
  21.6 1.0 copy-done.3
  24.0 0.8 norm_kernel.1.normed_ref
  24.8 7.9 %all-to-all-done.asked_ref = s32[64,2,128]{2,1,0:T(2,128)S(1)} async-done(((s32[64,2,128]{2,1,0:T(2,128)}), s32[64,2,128]{2,1,0:T(2,128)S(1)}, u32[]{:S(2)}, u32[]{:S(2)}) %all-to-all-start) | async-done | bytes 65568 | tf_op jit(solution)/shard_map/all_to_all | solution.py:333
  32.7 1.6 %pick_kernel.1 = bf16[1024,512]{1,0:T(8,128)(2,1)} custom-call(s32[64,2,128]{2,1,0:T(2,128)S(1)} %all-to-all-done.asked_ref, bf16[1024,512]{1,0:T(8,128)(2,1)S(1)} %norm_kernel.1.normed_ref), custom_call_target="tpu_custom_call" | custom-call | bytes 4194304 | tf_op jit(solution)/shard_map/pick_kernel/pallas_call | solution.py:349
  34.4 4.8 %all-to-all-start.1 = ((bf16[64,16,512]{2,1,0:T(8,128)(2,1)}), bf16[64,16,512]{2,1,0:T(8,128)(2,1)S(1)}, u32[]{:S(2)}, u32[]{:S(2)}) async-start(bf16[64,16,512]{2,1,0:T(8,128)(2,1)} %bitcast.4), calls=%async_computation.1 | async-start | bytes 2097152 | tf_op jit(solution)/shard_map/all_to_all | solution.py:355
  39.2 1.4 copy-done.2
  40.6 1.5 setup_kernel.1
  42.9 1.0 copy-done.10
  43.9 0.8 copy-done.12
  44.7 0.8 copy-done.14
  46.9 18.8 %all-to-all-done.1 = bf16[64,16,512]{2,1,0:T(8,128)(2,1)S(1)} async-done(((bf16[64,16,512]{2,1,0:T(8,128)(2,1)}), bf16[64,16,512]{2,1,0:T(8,128)(2,1)S(1)}, u32[]{:S(2)}, u32[]{:S(2)}) %all-to-all-start.1) | async-done | bytes 1048608 | tf_op jit(solution)/shard_map/all_to_all | solution.py:355
  66.5 5.9 %collective-permute-start.1 = (bf16[256,512]{1,0:T(8,128)(2,1)S(1)}, bf16[256,512]{1,0:T(8,128)(2,1)S(1)}, u32[]{:S(2)}, u32[]{:S(2)}) collective-permute-start(bf16[256,512]{1,0:T(8,128)(2,1)S(1)} %get-tuple-element.42), channel_id=1, source_target_pairs={{0,127},{1,2},{2,1},{3,4},{4,3},{5,6},{6,5},{7,8},{8,7},{9,10},{10... | collective-permute-start | bytes 786440 | tf_op jit(solution)/shard_map/ppermute | solution.py:380
  72.4 2.0 %collective-permute-start.2 = (bf16[256,512]{1,0:T(8,128)(2,1)S(1)}, bf16[256,512]{1,0:T(8,128)(2,1)S(1)}, u32[]{:S(2)}, u32[]{:S(2)}) collective-permute-start(bf16[256,512]{1,0:T(8,128)(2,1)S(1)} %get-tuple-element.53), channel_id=1, source_target_pairs={{0,1},{1,0},{2,3},{3,2},{4,5},{5,4},{6,7},{7,6},{8,9},{9,8},{10,11... | collective-permute-start | bytes 786440 | tf_op jit(solution)/shard_map/ppermute | solution.py:381
  74.4 21.0 %near_kernel.1 = (bf16[256,512]{1,0:T(8,128)(2,1)S(1)}, bf16[256,512]{1,0:T(8,128)(2,1)S(1)}, bf16[512,256]{1,0:T(8,128)(2,1)S(1)}, bf16[256,512]{1,0:T(8,128)(2,1)S(1)}) custom-call(bf16[512,512]{1,0:T(8,128)(2,1)S(1)} %get-tuple-element.43.seq_ref, bf16[512,512]{1,0:T(8,128)(2,1)S(1)} %copy-done.15, bf16[512,512]{1,0:T(8,128)(2,1)S(1)} %get-tuple-element.45.key_ref, ...), custom_call_target="tpu_custom_call" | custom-call | flops 6000000000 | bytes 4194304 | tf_op jit(solution)/shard_map/near_kernel/pallas_call | solution.py:384
  95.5 10.9 %core_kernel.1.core_ref = bf16[256,256]{1,0:T(8,128)(2,1)S(1)} custom-call(bf16[256,512]{1,0:T(8,128)(2,1)S(1)} %collective-permute-done.2.rows_ref, bf16[256,512]{1,0:T(8,128)(2,1)S(1)} %get-tuple-element.54.far_query_ref, bf16[512,256]{1,0:T(8,128)(2,1)S(1)} %get-tuple-element.55.far_key_ref, bf16[256,512]{1,0:T(8,128)(2,1)S(1)} %get-tuple-element.56.far_value_ref, ...), custom_call_target="tpu_custom_call" | custom-call | flops 3000000000 | bytes 4194304 | tf_op jit(solution)/shard_map/core_kernel/pallas_call | solution.py:388
  106.5 12.8 %cross_kernel.1 = bf16[1024,512]{1,0:T(8,128)(2,1)} custom-call(bf16[256,512]{1,0:T(8,128)(2,1)S(1)} %collective-permute-done.1.rows_ref, bf16[256,512]{1,0:T(8,128)(2,1)S(1)} %get-tuple-element.52.near_ref, bf16[256,256]{1,0:T(8,128)(2,1)S(1)} %core_kernel.1.core_ref, bf16[256,512]{1,0:T(8,128)(2,1)S(1)} %get-tuple-element.54.far_query_ref, ...), custom_call_target="tpu_custom_call" | custom-call | flops 6000000000 | bytes 4194304 | tf_op jit(solution)/shard_map/cross_kernel/pallas_call | solution.py:395
  119.3 9.1 %all-to-all-start.2 = ((bf16[128,8,512]{2,1,0:T(8,128)(2,1)}), bf16[128,8,512]{2,1,0:T(8,128)(2,1)S(1)}, u32[]{:S(2)}, u32[]{:S(2)}) async-start(bf16[128,8,512]{2,1,0:T(8,128)(2,1)} %bitcast.8), calls=%async_computation.2 | async-start | bytes 2097152 | tf_op jit(solution)/shard_map/all_to_all | solution.py:406
  128.4 2.8 %collective-permute-start.3 = (s32[64,128]{1,0:T(8,128)S(1)}, s32[64,128]{1,0:T(8,128)S(1)}, u32[]{:S(2)}, u32[]{:S(2)}) collective-permute-start(s32[64,128]{1,0:T(8,128)S(1)} %get-tuple-element.61), channel_id=1, source_target_pairs={{0,1},{1,0},{2,3},{3,2},{4,5},{5,4},{6,7},{7,6},{8,9},{9,8},{10,11... | collective-permute-start | bytes 98312 | tf_op jit(solution)/shard_map/ppermute | solution.py:374
  131.3 0.8 collective-permute-done.3.other_ref
  132.7 26.2 %all-to-all-done.2 = bf16[128,8,512]{2,1,0:T(8,128)(2,1)S(1)} async-done(((bf16[128,8,512]{2,1,0:T(8,128)(2,1)}), bf16[128,8,512]{2,1,0:T(8,128)(2,1)S(1)}, u32[]{:S(2)}, u32[]{:S(2)}) %all-to-all-start.2) | async-done | bytes 1048608 | tf_op jit(solution)/shard_map/all_to_all | solution.py:406
  158.8 1.4 place_kernel.1
  (45 shorter events, 5.6 us)
Async XLA Ops:
  1.8 19.8 %collective-permute-start = (bf16[512,512]{1,0:T(8,128)(2,1)}, bf16[512,512]{1,0:T(8,128)(2,1)S(1)}, u32[]{:S(2)}, u32[]{:S(2)}) collective-permute-start(bf16[512,512]{1,0:T(8,128)(2,1)} %own_ref), channel_id=1, source_target_pairs={{0,1},{1,0},{2,3},{3,2},{4,5},{5,4},{6,7},{7,6},{8,9},{9,8},{10,11... | collective-permute-start | bytes 1572872 | tf_op jit(solution)/shard_map/ppermute | solution.py:336
  10.6 22.1 %all-to-all-start = ((s32[64,2,128]{2,1,0:T(2,128)}), s32[64,2,128]{2,1,0:T(2,128)S(1)}, u32[]{:S(2)}, u32[]{:S(2)}) async-start(s32[64,2,128]{2,1,0:T(2,128)} %bitcast.1), calls=%async_computation | async-start | bytes 131072 | tf_op jit(solution)/shard_map/all_to_all | solution.py:333
  21.6 1.0 copy-start.3
  34.3 4.9 %copy-start.20 = (f32[1536]{0:T(1024)S(1)}, f32[1536]{0:T(1024)}, u32[]{:S(2)}) copy-start(f32[1536]{0:T(1024)} %param.13) | copy-start | bytes 18436
  34.3 4.9 %copy-start.1 = (s32[512]{0:T(512)S(1)}, s32[512]{0:T(512)}, u32[]{:S(2)}) copy-start(s32[512]{0:T(512)} %param.9) | copy-start | bytes 6148
  34.4 4.9 %copy-start.4 = (bf16[512,512]{1,0:T(8,128)(2,1)S(1)}, bf16[512,512]{1,0:T(8,128)(2,1)}, u32[]{:S(2)}) copy-start(bf16[512,512]{1,0:T(8,128)(2,1)} %proj_weight_ref) | copy-start | bytes 1572868
  34.4 4.9 %copy-start.7 = (f32[512]{0:T(512)S(1)}, f32[512]{0:T(512)}, u32[]{:S(2)}) copy-start(f32[512]{0:T(512)} %param.15) | copy-start | bytes 6148
  34.4 31.4 %all-to-all-start.1 = ((bf16[64,16,512]{2,1,0:T(8,128)(2,1)}), bf16[64,16,512]{2,1,0:T(8,128)(2,1)S(1)}, u32[]{:S(2)}, u32[]{:S(2)}) async-start(bf16[64,16,512]{2,1,0:T(8,128)(2,1)} %bitcast.4), calls=%async_computation.1 | async-start | bytes 2097152 | tf_op jit(solution)/shard_map/all_to_all | solution.py:355
  39.2 1.4 copy-start.2
  42.1 0.8 copy-start.8
  42.9 1.0 copy-start.10
  43.9 0.8 copy-start.12
  44.7 0.8 copy-start.14
  46.2 0.7 copy-start.18
  46.9 27.5 %copy-start.9 = (bf16[512,512]{1,0:T(8,128)(2,1)S(1)}, bf16[512,512]{1,0:T(8,128)(2,1)}, u32[]{:S(2)}) copy-start(bf16[512,512]{1,0:T(8,128)(2,1)} %copy-done.8) | copy-start | bytes 1572868
  65.7 8.7 %copy-start.15 = (bf16[512,512]{1,0:T(8,128)(2,1)S(1)}, bf16[512,512]{1,0:T(8,128)(2,1)}, u32[]{:S(2)}) copy-start(bf16[512,512]{1,0:T(8,128)(2,1)} %copy-done.14) | copy-start | bytes 1572868
  65.7 8.7 %copy-start.19 = (f32[512,128]{1,0:T(8,128)S(1)}, f32[512,128]{1,0:T(8,128)}, u32[]{:S(2)}) copy-start(f32[512,128]{1,0:T(8,128)} %copy-done.18) | copy-start | bytes 786436
  66.5 40.0 %collective-permute-start.1 = (bf16[256,512]{1,0:T(8,128)(2,1)S(1)}, bf16[256,512]{1,0:T(8,128)(2,1)S(1)}, u32[]{:S(2)}, u32[]{:S(2)}) collective-permute-start(bf16[256,512]{1,0:T(8,128)(2,1)S(1)} %get-tuple-element.42), channel_id=1, source_target_pairs={{0,127},{1,2},{2,1},{3,4},{4,3},{5,6},{6,5},{7,8},{8,7},{9,10},{10... | collective-permute-start | bytes 786440 | tf_op jit(solution)/shard_map/ppermute | solution.py:380
  72.4 23.1 %collective-permute-start.2 = (bf16[256,512]{1,0:T(8,128)(2,1)S(1)}, bf16[256,512]{1,0:T(8,128)(2,1)S(1)}, u32[]{:S(2)}, u32[]{:S(2)}) collective-permute-start(bf16[256,512]{1,0:T(8,128)(2,1)S(1)} %get-tuple-element.53), channel_id=1, source_target_pairs={{0,1},{1,0},{2,3},{3,2},{4,5},{5,4},{6,7},{7,6},{8,9},{9,8},{10,11... | collective-permute-start | bytes 786440 | tf_op jit(solution)/shard_map/ppermute | solution.py:381
  95.5 11.0 %copy-start.11 = (bf16[1024,512]{1,0:T(8,128)(2,1)S(1)}, bf16[1024,512]{1,0:T(8,128)(2,1)}, u32[]{:S(2)}) copy-start(bf16[1024,512]{1,0:T(8,128)(2,1)} %copy-done.10) | copy-start | bytes 3145732
  95.5 11.0 %copy-start.13 = (bf16[512,512]{1,0:T(8,128)(2,1)S(1)}, bf16[512,512]{1,0:T(8,128)(2,1)}, u32[]{:S(2)}) copy-start(bf16[512,512]{1,0:T(8,128)(2,1)} %copy-done.12) | copy-start | bytes 1572868
  95.5 11.0 %copy-start.17 = (f32[512,128]{1,0:T(8,128)S(1)}, f32[512,128]{1,0:T(8,128)}, u32[]{:S(2)}) copy-start(f32[512,128]{1,0:T(8,128)} %copy-done.16) | copy-start | bytes 786436
  119.3 39.5 %all-to-all-start.2 = ((bf16[128,8,512]{2,1,0:T(8,128)(2,1)}), bf16[128,8,512]{2,1,0:T(8,128)(2,1)S(1)}, u32[]{:S(2)}, u32[]{:S(2)}) async-start(bf16[128,8,512]{2,1,0:T(8,128)(2,1)} %bitcast.8), calls=%async_computation.2 | async-start | bytes 2097152 | tf_op jit(solution)/shard_map/all_to_all | solution.py:406
  128.4 3.6 %collective-permute-start.3 = (s32[64,128]{1,0:T(8,128)S(1)}, s32[64,128]{1,0:T(8,128)S(1)}, u32[]{:S(2)}, u32[]{:S(2)}) collective-permute-start(s32[64,128]{1,0:T(8,128)S(1)} %get-tuple-element.61), channel_id=1, source_target_pairs={{0,1},{1,0},{2,3},{3,2},{4,5},{5,4},{6,7},{7,6},{8,9},{9,8},{10,11... | collective-permute-start | bytes 98312 | tf_op jit(solution)/shard_map/ppermute | solution.py:374
  (4 other events, 2.7 us)

commit v5 on v4

--- a/solution.py
+++ b/solution.py
@@ -29,6 +29,10 @@
     return lax.dot_general(a, b, NT, preferred_element_type=F32)
 
 
+def odd_device():
+    return jnp.bitwise_and(lax.axis_index("seq"), 1)
+
+
 def ranks(order_row, peers):
     rows = order_row.shape[1]
     holder = jnp.right_shift(order_row, rows.bit_length() - 1)
@@ -44,9 +48,9 @@
     copy = pltpu.make_async_copy(order_ref, order_s, sem)
     copy.start()
     copy.wait()
-    order_row = order_s[...]
     peers = wanted_ref.shape[0]
-    rows = order_row.shape[1]
+    rows = order_s.shape[1]
+    order_row = jnp.bitwise_xor(order_s[...], odd_device() * rows)
     _, mine_bf, rank_row = ranks(order_row, peers)
     local = jnp.bitwise_and(order_row, rows - 1) + 1
     chosen = iota((LANES, rows), 0) == rank_row
@@ -59,22 +63,19 @@
     return jnp.transpose(jnp.broadcast_to(row, (LANES, count)))
 
 
-def norm_kernel(own_ref, other_ref, gain_ref, bias_ref, normed_ref, own_s, other_s, gain_s, bias_s, sems):
-    rows = own_s.shape[0]
-    pairs = [(own_ref, own_s), (other_ref, other_s), (gain_ref, gain_s), (bias_ref, bias_s)]
+def norm_kernel(feats_ref, gain_ref, bias_ref, normed_ref, feats_s, gain_s, bias_s, sems):
+    pairs = [(feats_ref, feats_s), (gain_ref, gain_s), (bias_ref, bias_s)]
     copies = [pltpu.make_async_copy(source, target, sems.at[i]) for i, (source, target) in enumerate(pairs)]
     for copy in copies:
         copy.start()
     for copy in copies:
         copy.wait()
-    odd = jnp.bitwise_and(lax.axis_index("seq"), 1)
-    for start, source in ((odd * rows, own_s), ((1 - odd) * rows, other_s)):
-        values = source[...].astype(F32)
-        center = jnp.mean(values, axis=-1, keepdims=True)
-        spread = jnp.mean(jnp.square(values - center), axis=-1, keepdims=True)
-        normed_ref[pl.ds(pl.multiple_of(start, rows), rows), :] = (
-            (values - center) * lax.rsqrt(spread + 1e-05) * gain_s[...] + bias_s[...]
-        ).astype(BF16)
+    values = feats_s[...].astype(F32)
+    center = jnp.mean(values, axis=-1, keepdims=True)
+    spread = jnp.mean(jnp.square(values - center), axis=-1, keepdims=True)
+    normed_ref[...] = (
+        (values - center) * lax.rsqrt(spread + 1e-05) * gain_s[...] + bias_s[...]
+    ).astype(BF16)
 
 
 def onehot_of(equal):
@@ -93,20 +94,20 @@
         copy.wait()
 
 
-def pick_kernel(asked_ref, normed_ref, picked_ref, stage, sems):
-    rows = normed_ref.shape[0] // 2
+def pick_kernel(asked_ref, own_ref, other_ref, picked_ref, stage, sems):
+    rows = own_ref.shape[0]
 
     def make(chunk, size):
         chips = size // (2 * CAPACITY)
         parts = []
-        for core in range(2):
-            asked = asked_ref[chunk * chips : (chunk + 1) * chips, core : core + 1]
+        for which, normed_ref in enumerate((own_ref, other_ref)):
+            asked = asked_ref[chunk * chips : (chunk + 1) * chips, which : which + 1]
             spread = jnp.broadcast_to(asked, (chips, CAPACITY, LANES))
             own = iota(spread.shape, 1) == iota(spread.shape, 2)
             index = jnp.where(own, spread, 0).reshape(chips * CAPACITY, LANES).astype(F32)
             index = jnp.sum(index, axis=1, keepdims=True).astype(jnp.int32) - 1
             onehot = onehot_of(index == iota((chips * CAPACITY, rows), 1))
-            part = dot(onehot, normed_ref[core * rows : (core + 1) * rows])
+            part = dot(onehot, normed_ref[...])
             parts.append(part.reshape(chips, CAPACITY, part.shape[1]))
         return jnp.concatenate(parts, axis=1).reshape(size, parts[0].shape[2]).astype(BF16)
 
@@ -124,9 +125,11 @@
     holder, _, rank_row = ranks(order_ref[...], peers)
     slot = holder * CAPACITY + rank_row
     swapped = jnp.concatenate([slot[:, rows // 2 :], slot[:, : rows // 2]], axis=1)
-    slot = jnp.where(jnp.bitwise_and(lax.axis_index("seq"), 1) == 1, swapped, slot)
+    odd = odd_device()
+    slot = jnp.where(odd == 1, swapped, slot)
     send_ref[...] = onehot_of(iota((slots, rows), 0) == slot)
-    slot_col = column(slot.astype(F32), rows).astype(jnp.int32)
+    arrives = jnp.bitwise_xor(slot, odd * CAPACITY)
+    slot_col = column(arrives.astype(F32), rows).astype(jnp.int32)
     arrange_ref[...] = onehot_of(slot_col[:, :1] == iota((rows, slots), 1))
     query_t_ref[...] = jnp.transpose(qkv_weight_ref[:, :width])
     key_ref[...] = qkv_weight_ref[:, width : 2 * width]
@@ -144,7 +147,7 @@
     asked = jnp.concatenate([mine_ref[...], other_ref[...]], axis=0)
     flipped = jnp.transpose(asked.astype(F32)).astype(jnp.int32)
     source, slot = iota((2 * chips, slots), 0), iota((2 * chips, slots), 1)
-    core = jnp.bitwise_xor(jnp.bitwise_and(lax.axis_index("seq"), 1), (source >= chips).astype(jnp.int32))
+    core = jnp.bitwise_xor(odd_device(), (source >= chips).astype(jnp.int32))
     owner = jnp.bitwise_and(source, chips - 1) * 2 + core
     expand = onehot_of(jnp.right_shift(slot, 3) == owner)
     high = dot(jnp.right_shift(flipped, 4).astype(F32).astype(BF16), expand)
@@ -295,8 +298,8 @@
     send_chunks(make, out_ref, stage, sems)
 
 
-def call(kernel, outs, count, scratch=(), flops=0, in_hbm=False, out_hbm=False):
-    vmem, hbm = pl.BlockSpec(memory_space=pltpu.VMEM), pl.BlockSpec(memory_space=pl.ANY)
+def call(kernel, outs, count, scratch=(), flops=0, in_hbm=False, out_hbm=False, mib=20):
+    vmem, hbm = pl.BlockSpec(memory_space=pltpu.VMEM), pl.BlockSpec(memory_space=pltpu.HBM)
     out_specs = [hbm if out_hbm else vmem] * len(outs)
     return pl.pallas_call(
         kernel,
@@ -304,7 +307,7 @@
         in_specs=[hbm if in_hbm else vmem] * count,
         out_specs=out_specs if len(outs) > 1 else out_specs[0],
         scratch_shapes=list(scratch),
-        compiler_params=pltpu.CompilerParams(vmem_limit_bytes=20 * 1024 * 1024),
+        compiler_params=pltpu.CompilerParams(vmem_limit_bytes=mib * 1024 * 1024),
         cost_estimate=pl.CostEstimate(flops=flops, bytes_accessed=4 * 1024 * 1024, transcendentals=0),
         name=kernel.__name__,
     )
@@ -328,26 +331,25 @@
         1,
         [pltpu.VMEM((1, rows), jnp.int32), pltpu.SemaphoreType.DMA],
         in_hbm=True,
+        mib=60,
     )(order.reshape(1, rows))
-    wanted, feats = lax.optimization_barrier((wanted, feats))
+    wanted, feats, norm_gain, norm_bias = lax.optimization_barrier((wanted, feats, norm_gain, norm_bias))
     asked = lax.all_to_all(
         wanted.reshape(chips, 2, LANES), "seq", split_axis=0, concat_axis=0, axis_index_groups=same_core, tiled=True
     )
-    other_feats = lax.ppermute(feats, "seq", core_pairs)
     normed = call(
         norm_kernel,
-        [shape((2 * rows, width), BF16)],
-        4,
-        [
-            pltpu.VMEM((rows, width), BF16), pltpu.VMEM((rows, width), BF16), row_vector, row_vector,
-            pltpu.SemaphoreType.DMA((4,)),
-        ],
+        [shape((rows, width), BF16)],
+        3,
+        [pltpu.VMEM((rows, width), BF16), row_vector, row_vector, pltpu.SemaphoreType.DMA((3,))],
         flops=1_000_000_000,
         in_hbm=True,
-    )(feats, other_feats, norm_gain.reshape(1, width), norm_bias.reshape(1, width))
+        mib=60,
+    )(feats, norm_gain.reshape(1, width), norm_bias.reshape(1, width))
+    other_normed = lax.ppermute(normed, "seq", core_pairs)
     staging = [pltpu.VMEM((slots, width), BF16), chunk_sems]
-    picked = call(pick_kernel, [shape((slots, width), BF16)], 2, staging, out_hbm=True)(
-        asked, normed
+    picked = call(pick_kernel, [shape((slots, width), BF16)], 3, staging, out_hbm=True)(
+        asked, normed, other_normed
     )
     picked, asked, order, qkv_weight, qkv_bias, proj_weight, proj_bias = lax.optimization_barrier(
         (picked, asked, order, qkv_weight, qkv_bias, proj_weight, proj_bias)
@@ -369,10 +371,8 @@
         flops=8_000_000_000,
     )(order.reshape(1, rows), qkv_weight, qkv_bias.reshape(1, 3 * width), proj_weight, proj_bias.reshape(1, width))
     asked, key_bias = lax.optimization_barrier((asked, key_bias))
-    odd = lax.axis_index("seq") % 2 == 1
-    mine = jnp.where(odd, asked[:, 1], asked[:, 0])
-    other = lax.ppermute(jnp.where(odd, asked[:, 0], asked[:, 1]), "seq", core_pairs)
-    place = call(place_setup_kernel, [shape((rows, slots), BF16)], 2, flops=2_000_000_000)(mine, other)
+    other = lax.ppermute(asked[:, 1], "seq", core_pairs)
+    place = call(place_setup_kernel, [shape((rows, slots), BF16)], 2, flops=2_000_000_000)(asked[:, 0], other)
     halves = shape((middle, width), BF16)
     seq, cross, core = call(arrange_kernel, [shape((rows, width), BF16), halves, halves], 2)(
         arrived.reshape(slots, width), arrange

time: 161 us -> 164 us (1.019)
  blocking collectives: 0 us -> 21.9 us
  starting transfers between devices: 44.4 us -> 33.4 us
  waiting for transfers between devices: 53.7 us -> 45.8 us
  Pallas kernels: 52.5 us -> 54.7 us
  local copies, waits for them, and re-layouts: 9.33 us -> 7.35 us
    all_to_all x0 -> x1, blocking collectives: none -> 21.9 us  [per_device(): lax.all_to_all(wanted.reshape(chips, 2, LANES), 'seq', split_axis=0, conc...]
    all_to_all x1 -> x0, starting transfers between devices: 10.9 us -> none  [per_device(): lax.all_to_all(wanted.reshape(chips, 2, LANES), 'seq', split_axis=0, conc...]
    all_to_all x1 -> x0, waiting for transfers between devices: 7.89 us -> none  [per_device(): lax.all_to_all(wanted.reshape(chips, 2, LANES), 'seq', split_axis=0, conc...]
    unnamed x42 -> x38, local copies, waits for them, and re-layouts: 9.32 us -> 7.33 us
  transfers between devices with their start and end apart: 7 -> 6, of which waited for: 4 -> 3; matrix products, arithmetic and copies ran while one was open for 0% -> 0% of each run, Pallas kernels for 22% -> 21%
where the time goes in v5:
time: 164 us
  Pallas kernels  54.7 us (33%)
  waiting for transfers between devices  45.8 us (28%)
  starting transfers between devices  33.4 us (20%)
  blocking collectives  21.9 us (13%)
  local copies, waits for them, and re-layouts  7.35 us (4%)
    all_to_all x1, waiting for transfers between devices, per_device(): lax.all_to_all(outgoing.reshape(peers, CAPACITY, width), 'seq', split_axi...  26.2 us
    all_to_all x1, blocking collectives, per_device(): lax.all_to_all(wanted.reshape(chips, 2, LANES), 'seq', split_axis=0, conc...  21.9 us
    pallas_call x1, Pallas kernels, per_device(): call(near_kernel, [wide, wide, tall, wide], 7, [wide_s, tall_s, wide_s],...  21 us
    all_to_all x1, waiting for transfers between devices, per_device(): lax.all_to_all(picked.reshape(chips, 2 * CAPACITY, width), 'seq', split_a...  18.8 us
    pallas_call x1, Pallas kernels, per_device(): call(cross_kernel, [shape((slots, width), BF16)], 13, [pltpu.VMEM((width,...  12.8 us
    pallas_call x1, Pallas kernels, per_device(): call(core_kernel, [shape((half, middle), BF16)], 8, [pltpu.VMEM((half, mi...  10.9 us
    all_to_all x1, starting transfers between devices, per_device(): lax.all_to_all(outgoing.reshape(peers, CAPACITY, width), 'seq', split_axi...  9.11 us
    ppermute x1, starting transfers between devices, per_device(): other_normed = lax.ppermute(normed, 'seq', core_pairs)  8.78 us
  transfers between devices with their start and end apart: 6, of which 3 were waited for; matrix products, arithmetic and copies ran while one was open for 0% of the time, Pallas kernels for 21%

profile of v5, /device:TPU:1, one launch (start us, length us, event | category | flops | bytes accessed | tf_op | source)
XLA Modules:
  0.0 163.6 jit_solution(11147404252027036259)
XLA Ops:
  0.0 1.8 %request_kernel.1 = s32[128,128]{1,0:T(8,128)} custom-call(s32[1,512]{1,0:T(1,128)} %bitcast.16), custom_call_target="tpu_custom_call" | custom-call | bytes 4194304 | tf_op jit(solution)/shard_map/request_kernel/pallas_call | solution.py:328
  1.8 2.3 %norm_kernel.1.own_ref = bf16[512,512]{1,0:T(8,128)(2,1)} custom-call(bf16[512,512]{1,0:T(8,128)(2,1)} %feats_ref, f32[1,512]{1,0:T(1,128)} %bitcast.20, f32[1,512]{1,0:T(1,128)} %bitcast.21), custom_call_target="tpu_custom_call" | custom-call | flops 1000000000 | bytes 4194304 | tf_op jit(solution)/shard_map/norm_kernel/pallas_call | solution.py:340
  4.1 8.8 %collective-permute-start = (bf16[512,512]{1,0:T(8,128)(2,1)}, bf16[512,512]{1,0:T(8,128)(2,1)S(1)}, u32[]{:S(2)}, u32[]{:S(2)}) collective-permute-start(bf16[512,512]{1,0:T(8,128)(2,1)} %norm_kernel.1.own_ref), channel_id=1, source_target_pairs={{0,1},{1,0},{2,3},{3,2},{4,5},{5,4},{6,7},{7,6},{8,9},{9,8},{10,11... | collective-permute-start | bytes 1572872 | tf_op jit(solution)/shard_map/ppermute | solution.py:349
  12.9 21.9 %all_to_all.15.asked_ref = s32[64,2,128]{2,1,0:T(2,128)S(1)} all-to-all(s32[64,2,128]{2,1,0:T(2,128)S(1)} %bitcast.19), channel_id=1, replica_groups={{0,2,4,6,8,10,12,14,16,18,20,22,24,26,28,30,32,34,36,38,40,42,44,46,48,..., dimensions={0} | all-to-all | bytes 131072 | tf_op jit(solution)/shard_map/all_to_all | solution.py:337
  34.8 1.0 copy-done
  35.8 1.6 %pick_kernel.1 = bf16[1024,512]{1,0:T(8,128)(2,1)} custom-call(s32[64,2,128]{2,1,0:T(2,128)S(1)} %all_to_all.15.asked_ref, bf16[512,512]{1,0:T(8,128)(2,1)S(1)} %copy-done, bf16[512,512]{1,0:T(8,128)(2,1)S(1)} %collective-permute-done.other_ref), custom_call_target="tpu_custom_call" | custom-call | bytes 4194304 | tf_op jit(solution)/shard_map/pick_kernel/pallas_call | solution.py:351
  37.5 4.8 %all-to-all-start.1 = ((bf16[64,16,512]{2,1,0:T(8,128)(2,1)}), bf16[64,16,512]{2,1,0:T(8,128)(2,1)S(1)}, u32[]{:S(2)}, u32[]{:S(2)}) async-start(bf16[64,16,512]{2,1,0:T(8,128)(2,1)} %bitcast.4), calls=%async_computation.1 | async-start | bytes 2097152 | tf_op jit(solution)/shard_map/all_to_all | solution.py:357
  42.4 1.4 copy-done.2
  43.8 1.5 setup_kernel.1
  45.3 0.8 copy-done.5
  46.0 1.0 copy-done.7
  47.0 0.8 copy-done.9
  47.8 0.8 copy-done.11
  50.1 18.8 %all-to-all-done.1 = bf16[64,16,512]{2,1,0:T(8,128)(2,1)S(1)} async-done(((bf16[64,16,512]{2,1,0:T(8,128)(2,1)}), bf16[64,16,512]{2,1,0:T(8,128)(2,1)S(1)}, u32[]{:S(2)}, u32[]{:S(2)}) %all-to-all-start.1) | async-done | bytes 1048608 | tf_op jit(solution)/shard_map/all_to_all | solution.py:357
  69.6 5.9 %collective-permute-start.1 = (bf16[256,512]{1,0:T(8,128)(2,1)S(1)}, bf16[256,512]{1,0:T(8,128)(2,1)S(1)}, u32[]{:S(2)}, u32[]{:S(2)}) collective-permute-start(bf16[256,512]{1,0:T(8,128)(2,1)S(1)} %get-tuple-element.46), channel_id=1, source_target_pairs={{0,127},{1,2},{2,1},{3,4},{4,3},{5,6},{6,5},{7,8},{8,7},{9,10},{10... | collective-permute-start | bytes 786440 | tf_op jit(solution)/shard_map/ppermute | solution.py:380
  75.5 2.0 %collective-permute-start.2 = (bf16[256,512]{1,0:T(8,128)(2,1)S(1)}, bf16[256,512]{1,0:T(8,128)(2,1)S(1)}, u32[]{:S(2)}, u32[]{:S(2)}) collective-permute-start(bf16[256,512]{1,0:T(8,128)(2,1)S(1)} %get-tuple-element.57), channel_id=1, source_target_pairs={{0,1},{1,0},{2,3},{3,2},{4,5},{5,4},{6,7},{7,6},{8,9},{9,8},{10,11... | collective-permute-start | bytes 786440 | tf_op jit(solution)/shard_map/ppermute | solution.py:381
  77.6 21.0 %near_kernel.1 = (bf16[256,512]{1,0:T(8,128)(2,1)S(1)}, bf16[256,512]{1,0:T(8,128)(2,1)S(1)}, bf16[512,256]{1,0:T(8,128)(2,1)S(1)}, bf16[256,512]{1,0:T(8,128)(2,1)S(1)}) custom-call(bf16[512,512]{1,0:T(8,128)(2,1)S(1)} %get-tuple-element.47.seq_ref, bf16[512,512]{1,0:T(8,128)(2,1)S(1)} %copy-done.12, bf16[512,512]{1,0:T(8,128)(2,1)S(1)} %get-tuple-element.49.key_ref, ...), custom_call_target="tpu_custom_call" | custom-call | flops 6000000000 | bytes 4194304 | tf_op jit(solution)/shard_map/near_kernel/pallas_call | solution.py:384
  98.6 10.9 %core_kernel.1.core_ref = bf16[256,256]{1,0:T(8,128)(2,1)S(1)} custom-call(bf16[256,512]{1,0:T(8,128)(2,1)S(1)} %collective-permute-done.2.rows_ref, bf16[256,512]{1,0:T(8,128)(2,1)S(1)} %get-tuple-element.58.far_query_ref, bf16[512,256]{1,0:T(8,128)(2,1)S(1)} %get-tuple-element.59.far_key_ref, bf16[256,512]{1,0:T(8,128)(2,1)S(1)} %get-tuple-element.60.far_value_ref, ...), custom_call_target="tpu_custom_call" | custom-call | flops 3000000000 | bytes 4194304 | tf_op jit(solution)/shard_map/core_kernel/pallas_call | solution.py:388
  109.6 12.8 %cross_kernel.1 = bf16[1024,512]{1,0:T(8,128)(2,1)} custom-call(bf16[256,512]{1,0:T(8,128)(2,1)S(1)} %collective-permute-done.1.rows_ref, bf16[256,512]{1,0:T(8,128)(2,1)S(1)} %get-tuple-element.56.near_ref, bf16[256,256]{1,0:T(8,128)(2,1)S(1)} %core_kernel.1.core_ref, bf16[256,512]{1,0:T(8,128)(2,1)S(1)} %get-tuple-element.58.far_query_ref, ...), custom_call_target="tpu_custom_call" | custom-call | flops 6000000000 | bytes 4194304 | tf_op jit(solution)/shard_map/cross_kernel/pallas_call | solution.py:395
  122.4 9.1 %all-to-all-start.2 = ((bf16[128,8,512]{2,1,0:T(8,128)(2,1)}), bf16[128,8,512]{2,1,0:T(8,128)(2,1)S(1)}, u32[]{:S(2)}, u32[]{:S(2)}) async-start(bf16[128,8,512]{2,1,0:T(8,128)(2,1)} %bitcast.8), calls=%async_computation.2 | async-start | bytes 2097152 | tf_op jit(solution)/shard_map/all_to_all | solution.py:406
  131.6 2.8 %collective-permute-start.3 = (s32[64,128]{1,0:T(8,128)S(1)}, s32[64,128]{1,0:T(8,128)S(1)}, u32[]{:S(2)}, u32[]{:S(2)}) collective-permute-start(s32[64,128]{1,0:T(8,128)S(1)} %get-tuple-element.65), channel_id=1, source_target_pairs={{0,1},{1,0},{2,3},{3,2},{4,5},{5,4},{6,7},{7,6},{8,9},{9,8},{10,11... | collective-permute-start | bytes 98312 | tf_op jit(solution)/shard_map/ppermute | solution.py:374
  134.4 0.8 collective-permute-done.3.other_ref
  135.8 26.2 %all-to-all-done.2 = bf16[128,8,512]{2,1,0:T(8,128)(2,1)S(1)} async-done(((bf16[128,8,512]{2,1,0:T(8,128)(2,1)}), bf16[128,8,512]{2,1,0:T(8,128)(2,1)S(1)}, u32[]{:S(2)}, u32[]{:S(2)}) %all-to-all-start.2) | async-done | bytes 1048608 | tf_op jit(solution)/shard_map/all_to_all | solution.py:406
  162.0 1.4 place_kernel.1
  (40 shorter events, 2.8 us)
Async XLA Ops:
  1.8 11.1 %copy-start.17 = (s32[128,128]{1,0:T(8,128)S(1)}, s32[128,128]{1,0:T(8,128)}, u32[]{:S(2)}) copy-start(s32[128,128]{1,0:T(8,128)} %request_kernel.1) | copy-start | bytes 196612
  4.1 30.7 %collective-permute-start = (bf16[512,512]{1,0:T(8,128)(2,1)}, bf16[512,512]{1,0:T(8,128)(2,1)S(1)}, u32[]{:S(2)}, u32[]{:S(2)}) collective-permute-start(bf16[512,512]{1,0:T(8,128)(2,1)} %norm_kernel.1.own_ref), channel_id=1, source_target_pairs={{0,1},{1,0},{2,3},{3,2},{4,5},{5,4},{6,7},{7,6},{8,9},{9,8},{10,11... | collective-permute-start | bytes 1572872 | tf_op jit(solution)/shard_map/ppermute | solution.py:349
  34.8 1.0 copy-start
  37.4 4.9 %copy-start.18 = (f32[1536]{0:T(1024)S(1)}, f32[1536]{0:T(1024)}, u32[]{:S(2)}) copy-start(f32[1536]{0:T(1024)} %param.13) | copy-start | bytes 18436
  37.5 4.9 %copy-start.1 = (s32[512]{0:T(512)S(1)}, s32[512]{0:T(512)}, u32[]{:S(2)}) copy-start(s32[512]{0:T(512)} %param.9) | copy-start | bytes 6148
  37.5 4.9 %copy-start.3 = (bf16[512,512]{1,0:T(8,128)(2,1)S(1)}, bf16[512,512]{1,0:T(8,128)(2,1)}, u32[]{:S(2)}) copy-start(bf16[512,512]{1,0:T(8,128)(2,1)} %proj_weight_ref) | copy-start | bytes 1572868
  37.5 4.9 %copy-start.4 = (f32[512]{0:T(512)S(1)}, f32[512]{0:T(512)}, u32[]{:S(2)}) copy-start(f32[512]{0:T(512)} %param.15) | copy-start | bytes 6148
  37.5 31.4 %all-to-all-start.1 = ((bf16[64,16,512]{2,1,0:T(8,128)(2,1)}), bf16[64,16,512]{2,1,0:T(8,128)(2,1)S(1)}, u32[]{:S(2)}, u32[]{:S(2)}) async-start(bf16[64,16,512]{2,1,0:T(8,128)(2,1)} %bitcast.4), calls=%async_computation.1 | async-start | bytes 2097152 | tf_op jit(solution)/shard_map/all_to_all | solution.py:357
  42.4 1.4 copy-start.2
  45.2 0.8 copy-start.5
  46.0 1.0 copy-start.7
  47.0 0.8 copy-start.9
  47.8 0.8 copy-start.11
  49.3 0.7 copy-start.15
  50.1 27.5 %copy-start.6 = (bf16[512,512]{1,0:T(8,128)(2,1)S(1)}, bf16[512,512]{1,0:T(8,128)(2,1)}, u32[]{:S(2)}) copy-start(bf16[512,512]{1,0:T(8,128)(2,1)} %copy-done.5) | copy-start | bytes 1572868
  68.9 8.7 %copy-start.12 = (bf16[512,512]{1,0:T(8,128)(2,1)S(1)}, bf16[512,512]{1,0:T(8,128)(2,1)}, u32[]{:S(2)}) copy-start(bf16[512,512]{1,0:T(8,128)(2,1)} %copy-done.11) | copy-start | bytes 1572868
  68.9 8.7 %copy-start.16 = (f32[512,128]{1,0:T(8,128)S(1)}, f32[512,128]{1,0:T(8,128)}, u32[]{:S(2)}) copy-start(f32[512,128]{1,0:T(8,128)} %copy-done.15) | copy-start | bytes 786436
  69.6 40.0 %collective-permute-start.1 = (bf16[256,512]{1,0:T(8,128)(2,1)S(1)}, bf16[256,512]{1,0:T(8,128)(2,1)S(1)}, u32[]{:S(2)}, u32[]{:S(2)}) collective-permute-start(bf16[256,512]{1,0:T(8,128)(2,1)S(1)} %get-tuple-element.46), channel_id=1, source_target_pairs={{0,127},{1,2},{2,1},{3,4},{4,3},{5,6},{6,5},{7,8},{8,7},{9,10},{10... | collective-permute-start | bytes 786440 | tf_op jit(solution)/shard_map/ppermute | solution.py:380
  75.5 23.1 %collective-permute-start.2 = (bf16[256,512]{1,0:T(8,128)(2,1)S(1)}, bf16[256,512]{1,0:T(8,128)(2,1)S(1)}, u32[]{:S(2)}, u32[]{:S(2)}) collective-permute-start(bf16[256,512]{1,0:T(8,128)(2,1)S(1)} %get-tuple-element.57), channel_id=1, source_target_pairs={{0,1},{1,0},{2,3},{3,2},{4,5},{5,4},{6,7},{7,6},{8,9},{9,8},{10,11... | collective-permute-start | bytes 786440 | tf_op jit(solution)/shard_map/ppermute | solution.py:381
  98.6 11.0 %copy-start.8 = (bf16[1024,512]{1,0:T(8,128)(2,1)S(1)}, bf16[1024,512]{1,0:T(8,128)(2,1)}, u32[]{:S(2)}) copy-start(bf16[1024,512]{1,0:T(8,128)(2,1)} %copy-done.7) | copy-start | bytes 3145732
  98.6 11.0 %copy-start.10 = (bf16[512,512]{1,0:T(8,128)(2,1)S(1)}, bf16[512,512]{1,0:T(8,128)(2,1)}, u32[]{:S(2)}) copy-start(bf16[512,512]{1,0:T(8,128)(2,1)} %copy-done.9) | copy-start | bytes 1572868
  98.6 11.0 %copy-start.14 = (f32[512,128]{1,0:T(8,128)S(1)}, f32[512,128]{1,0:T(8,128)}, u32[]{:S(2)}) copy-start(f32[512,128]{1,0:T(8,128)} %copy-done.13) | copy-start | bytes 786436
  122.4 39.6 %all-to-all-start.2 = ((bf16[128,8,512]{2,1,0:T(8,128)(2,1)}), bf16[128,8,512]{2,1,0:T(8,128)(2,1)S(1)}, u32[]{:S(2)}, u32[]{:S(2)}) async-start(bf16[128,8,512]{2,1,0:T(8,128)(2,1)} %bitcast.8), calls=%async_computation.2 | async-start | bytes 2097152 | tf_op jit(solution)/shard_map/all_to_all | solution.py:406
  131.6 3.6 %collective-permute-start.3 = (s32[64,128]{1,0:T(8,128)S(1)}, s32[64,128]{1,0:T(8,128)S(1)}, u32[]{:S(2)}, u32[]{:S(2)}) collective-permute-start(s32[64,128]{1,0:T(8,128)S(1)} %get-tuple-element.65), channel_id=1, source_target_pairs={{0,1},{1,0},{2,3},{3,2},{4,5},{5,4},{6,7},{7,6},{8,9},{9,8},{10,11... | collective-permute-start | bytes 98312 | tf_op jit(solution)/shard_map/ppermute | solution.py:374
  (1 other events, 0.7 us)

commit v6 on v3

--- a/solution.py
+++ b/solution.py
@@ -138,12 +138,25 @@
     proj_bias_col_ref[...] = column(proj_bias_ref[...], width)
 
 
-def arrange_kernel(arrived_ref, onehot_ref, seq_ref, cross_ref, core_ref):
-    middle = cross_ref.shape[0]
+def arrange_kernel(
+    arrived_ref, onehot_ref, query_t_ref, key_ref, value_t_ref, query_bias_ref, key_bias_ref, value_bias_ref,
+    cross_ref, core_ref, query_ref, key_out_ref, value_ref, far_query_ref, far_key_ref, far_value_ref,
+):
+    half, rows = query_ref.shape
+    middle = rows // 2
     seq = dot(onehot_ref[...], arrived_ref[...]).astype(BF16)
-    seq_ref[...] = seq
-    cross_ref[...] = seq[:middle]
-    core_ref[...] = seq[middle:]
+    keys = (dot(seq, key_ref[...]) + key_bias_ref[...]).astype(BF16)
+    values = (dot_nt(value_t_ref[...], seq) + value_bias_ref[:, :1]).astype(BF16)
+    for ref, part in ((cross_ref, slice(0, middle)), (core_ref, slice(middle, rows))):
+        ref[:, :half] = keys[part, half:]
+        ref[:, half:] = values[half:, part]
+    key_out_ref[...] = keys[:, :half]
+    far_key_ref[...] = keys[:, half:]
+    value_ref[...] = values[:half]
+    far_value_ref[...] = values[half:]
+    queries = (dot_nt(query_t_ref[...], seq) + query_bias_ref[:, :1]).astype(BF16)
+    query_ref[...] = queries[:half]
+    far_query_ref[...] = queries[half:]
 
 
 def attend(queries_ref, sides, out_ref, out_start):
@@ -206,59 +219,35 @@
         lax.fori_loop(0, heads, one_head, 0)
 
 
-def near_kernel(
-    seq_ref, query_t_ref, key_ref, value_t_ref, query_bias_ref, key_bias_ref, value_bias_ref,
-    attended_ref, far_query_ref, far_key_ref, far_value_ref, query_s, key_s, value_s,
-):
-    half, rows = query_s.shape
+def near_kernel(query_ref, key_ref, value_ref, attended_ref):
+    rows = query_ref.shape[1]
     middle = rows // 2
-    seq = seq_ref[...]
-    queries = (dot_nt(query_t_ref[...], seq) + query_bias_ref[:, :1]).astype(BF16)
-    keys = (dot(seq, key_ref[...]) + key_bias_ref[...]).astype(BF16)
-    values = (dot_nt(value_t_ref[...], seq) + value_bias_ref[:, :1]).astype(BF16)
-    query_s[...] = queries[:half]
-    far_query_ref[...] = queries[half:]
-    key_s[...] = keys[:, :half]
-    far_key_ref[...] = keys[:, half:]
-    value_s[...] = values[:half]
-    far_value_ref[...] = values[half:]
-    sides = [(key_s, value_s, 0, middle), (key_s, value_s, middle, rows)]
-    attend(query_s, sides, attended_ref, 0)
-
-
-def extend(rows_ref, own, key_ref, key_bias_ref, value_t_ref, value_bias_ref, far_key_ref, far_value_ref, key_s, value_s):
-    middle, half = rows_ref.shape[0], key_s.shape[1]
-    keys = dot(rows_ref[...], key_ref[:, half:]) + key_bias_ref[:, half:]
-    key_s[:middle] = keys.astype(BF16)
-    values = dot_nt(value_t_ref[half:], rows_ref[...]) + value_bias_ref[half:, :1]
-    value_s[:, :middle] = values.astype(BF16)
+    sides = [(key_ref, value_ref, 0, middle), (key_ref, value_ref, middle, rows)]
+    attend(query_ref, sides, attended_ref, 0)
+
+
+def extend(received_ref, own, far_key_ref, far_value_ref, key_s, value_s):
+    middle, half = received_ref.shape[0], key_s.shape[1]
+    key_s[:middle] = received_ref[:, :half]
+    value_s[:, :middle] = received_ref[:, half:]
     key_s[middle:] = far_key_ref[own]
     value_s[:, middle:] = far_value_ref[:, own]
 
 
-def core_kernel(
-    rows_ref, far_query_ref, far_key_ref, far_value_ref, key_ref, key_bias_ref, value_t_ref, value_bias_ref,
-    attended_ref, query_s, key_s, value_s,
-):
-    middle = rows_ref.shape[0]
+def core_kernel(received_ref, far_query_ref, far_key_ref, far_value_ref, attended_ref, query_s, key_s, value_s):
+    middle = received_ref.shape[0]
     own = slice(middle, 2 * middle)
-    extend(
-        rows_ref, own, key_ref, key_bias_ref, value_t_ref, value_bias_ref, far_key_ref, far_value_ref, key_s, value_s
-    )
+    extend(received_ref, own, far_key_ref, far_value_ref, key_s, value_s)
     query_s[...] = far_query_ref[:, own]
     attend(query_s, [(key_s, value_s, 0, middle)], attended_ref, 0)
 
 
 def cross_kernel(
-    rows_ref, near_ref, core_ref, far_query_ref, far_key_ref, far_value_ref, key_ref, key_bias_ref,
-    value_t_ref, value_bias_ref, proj_t_ref, proj_bias_ref, send_ref,
+    received_ref, near_ref, core_ref, far_query_ref, far_key_ref, far_value_ref, proj_t_ref, proj_bias_ref, send_ref,
     outgoing_ref, attended_s, key_s, value_s, stage, sems,
 ):
-    middle, half = rows_ref.shape[0], near_ref.shape[0]
-    extend(
-        rows_ref, slice(0, middle), key_ref, key_bias_ref, value_t_ref, value_bias_ref, far_key_ref,
-        far_value_ref, key_s, value_s,
-    )
+    middle, half = received_ref.shape[0], near_ref.shape[0]
+    extend(received_ref, slice(0, middle), far_key_ref, far_value_ref, key_s, value_s)
     attended_s[:half] = near_ref[...]
     attended_s[half:, middle:] = core_ref[...]
     attend(far_query_ref, [(key_s, value_s, 0, middle)], attended_s, half)
@@ -340,35 +329,29 @@
         proj_bias.reshape(1, width),
     )
     halves = shape((middle, width), BF16)
-    seq, cross, core = call(arrange_kernel, [shape((rows, width), BF16), halves, halves], 2)(
-        arrived.reshape(slots, width), arrange
-    )
+    wide, tall = shape((half, rows), BF16), shape((rows, half), BF16)
+    cross, core, query, key, value, far_query, far_key, far_value = call(
+        arrange_kernel, [halves, halves, wide, tall, wide, wide, tall, wide], 8
+    )(arrived.reshape(slots, width), arrange, query_t, key_weight, value_t, query_bias, key_bias, value_bias)
     cross = lax.ppermute(cross, "seq", [(i, (i + 2 * (i % 2) - 1) % peers) for i in range(peers)])
     core = lax.ppermute(core, "seq", [(i, i + 1 - 2 * (i % 2)) for i in range(peers)])
-    wide, tall = shape((half, rows), BF16), shape((rows, half), BF16)
-    wide_s, tall_s = pltpu.VMEM((half, rows), BF16), pltpu.VMEM((rows, half), BF16)
-    near, far_query, far_key, far_value = call(
-        near_kernel, [wide, wide, tall, wide], 7, [wide_s, tall_s, wide_s], flops=6_000_000_000
-    )(seq, query_t, key_weight, value_t, query_bias, key_bias, value_bias)
-    patch_s = [tall_s, wide_s]
+    near = call(near_kernel, [wide], 3, flops=6_000_000_000)(query, key, value)
+    patch_s = [pltpu.VMEM((rows, half), BF16), pltpu.VMEM((half, rows), BF16)]
     core_attended = call(
         core_kernel,
         [shape((half, middle), BF16)],
-        8,
+        4,
         [pltpu.VMEM((half, middle), BF16), *patch_s],
         flops=3_000_000_000,
-    )(core, far_query, far_key, far_value, key_weight, key_bias, value_t, value_bias)
+    )(core, far_query, far_key, far_value)
     outgoing = call(
         cross_kernel,
         [shape((slots, width), BF16)],
-        13,
+        9,
         [pltpu.VMEM((width, rows), BF16), *patch_s, *staging],
         flops=6_000_000_000,
         out_hbm=True,
-    )(
-        cross, near, core_attended, far_query, far_key, far_value, key_weight, key_bias, value_t, value_bias,
-        proj_t, proj_bias_col, send,
-    )
+    )(cross, near, core_attended, far_query, far_key, far_value, proj_t, proj_bias_col, send)
     returned = lax.all_to_all(
         outgoing.reshape(peers, CAPACITY, width), "seq", split_axis=0, concat_axis=0, tiled=True
     )

time: 161 us -> 165 us (1.025)
  local copies, waits for them, and re-layouts: 11.2 us -> 15.2 us
    unnamed x46, local copies, waits for them, and re-layouts: 11.2 us -> 15.2 us
  transfers between devices with their start and end apart: 4 -> 4, of which waited for: 2 -> 2; matrix products, arithmetic and copies ran while one was open for 0% -> 0% of each run, Pallas kernels for 21% -> 20%
where the time goes in v6:
time: 165 us; the launch traced here: 164 us
  Pallas kernels  51.4 us (31%)
  blocking collectives  38.2 us (23%)
  starting transfers between devices  29.8 us (18%)
  waiting for transfers between devices  29.1 us (18%)
  local copies, waits for them, and re-layouts  15.2 us (9%)
    all_to_all x1, blocking collectives, per_device(): lax.all_to_all(outgoing.reshape(peers, CAPACITY, width), 'seq', split_axi...  38.2 us
    all_to_all x1, waiting for transfers between devices, per_device(): lax.all_to_all(picked.reshape(peers, CAPACITY, width), 'seq', split_axis=...  20.5 us
    pallas_call x1, Pallas kernels, per_device(): near = call(near_kernel, [wide], 3, flops=6000000000)(query, key, value)  20.3 us
    all_to_all x1, starting transfers between devices, per_device(): lax.all_to_all(wanted, 'seq', split_axis=0, concat_axis=0, tiled=True)  18.4 us
    unnamed x46, local copies, waits for them, and re-layouts  15.2 us
    pallas_call x1, Pallas kernels, per_device(): call(cross_kernel, [shape((slots, width), BF16)], 9, [pltpu.VMEM((width,...  12.6 us
    pallas_call x1, Pallas kernels, per_device(): call(core_kernel, [shape((half, middle), BF16)], 4, [pltpu.VMEM((half, mi...  10.7 us
    all_to_all x1, waiting for transfers between devices, per_device(): lax.all_to_all(wanted, 'seq', split_axis=0, concat_axis=0, tiled=True)  8.58 us
  transfers between devices with their start and end apart: 4, of which 2 were waited for; matrix products, arithmetic and copies ran while one was open for 0% of the time, Pallas kernels for 20%

profile of v6, /device:TPU:1, one launch (start us, length us, event | category | flops | bytes accessed | tf_op | source)
XLA Modules:
  0.0 164.1 jit_solution(18118279532287331187)
XLA Ops:
  0.7 1.1 request_kernel.1
  1.8 18.4 %all-to-all-start = ((s32[128,1,128]{2,1,0:T(1,128)}), s32[128,1,128]{2,1,0:T(1,128)S(1)}, u32[]{:S(2)}, u32[]{:S(2)}) async-start(s32[128,1,128]{2,1,0:T(1,128)} %bitcast.2), calls=%async_computation | async-start | bytes 131072 | tf_op jit(solution)/shard_map/all_to_all | solution.py:296
  20.2 1.0 copy-done.11
  23.1 8.6 %all-to-all-done.asked_ref = s32[128,1,128]{2,1,0:T(1,128)S(1)} async-done(((s32[128,1,128]{2,1,0:T(1,128)}), s32[128,1,128]{2,1,0:T(1,128)S(1)}, u32[]{:S(2)}, u32[]{:S(2)}) %all-to-all-start) | async-done | bytes 65568 | tf_op jit(solution)/shard_map/all_to_all | solution.py:296
  31.7 1.5 pick_kernel.1
  33.2 5.7 %all-to-all-start.1 = ((bf16[128,8,512]{2,1,0:T(8,128)(2,1)}), bf16[128,8,512]{2,1,0:T(8,128)(2,1)S(1)}, u32[]{:S(2)}, u32[]{:S(2)}) async-start(bf16[128,8,512]{2,1,0:T(8,128)(2,1)} %bitcast.6), calls=%async_computation.1 | async-start | bytes 2097152 | tf_op jit(solution)/shard_map/all_to_all | solution.py:312
  39.0 1.4 copy-done.10
  40.4 1.0 copy-done.12
  41.5 1.8 %setup_kernel.1 = (bf16[512,1024]{1,0:T(8,128)(2,1)S(1)}, bf16[1024,512]{1,0:T(8,128)(2,1)S(1)}, bf16[512,1024]{1,0:T(8,128)(2,1)S(1)}, bf16[512,512]{1,0:T(8,12...) custom-call(s32[128,128]{1,0:T(8,128)S(1)} %bitcast.16, ...), custom_call_target="tpu_custom_call" | custom-call | flops 8000000000 | bytes 4194304 | tf_op jit(solution)/shard_map/setup_kernel/pallas_call | solution.py:319
  46.4 1.0 copy-done.16
  47.4 0.8 copy-done.18
  48.9 20.5 %all-to-all-done.1 = bf16[128,8,512]{2,1,0:T(8,128)(2,1)S(1)} async-done(((bf16[128,8,512]{2,1,0:T(8,128)(2,1)}), bf16[128,8,512]{2,1,0:T(8,128)(2,1)S(1)}, u32[]{:S(2)}, u32[]{:S(2)}) %all-to-all-start.1) | async-done | bytes 1048608 | tf_op jit(solution)/shard_map/all_to_all | solution.py:312
  69.4 1.0 copy-done.1
  70.4 1.0 copy-done.3
  71.5 1.0 copy-done.5
  72.5 0.9 copy-done.7
  73.5 1.5 arrange_kernel.1
  75.0 3.7 %collective-permute-start = (bf16[256,512]{1,0:T(8,128)(2,1)S(1)}, bf16[256,512]{1,0:T(8,128)(2,1)S(1)}, u32[]{:S(2)}, u32[]{:S(2)}) collective-permute-start(bf16[256,512]{1,0:T(8,128)(2,1)S(1)} %get-tuple-element.45), channel_id=1, source_target_pairs={{0,127},{1,2},{2,1},{3,4},{4,3},{5,6},{6,5},{7,8},{8,7},{9,10},{10... | collective-permute-start | bytes 786440 | tf_op jit(solution)/shard_map/ppermute | solution.py:336
  78.7 1.9 %collective-permute-start.1 = (bf16[256,512]{1,0:T(8,128)(2,1)S(1)}, bf16[256,512]{1,0:T(8,128)(2,1)S(1)}, u32[]{:S(2)}, u32[]{:S(2)}) collective-permute-start(bf16[256,512]{1,0:T(8,128)(2,1)S(1)} %get-tuple-element.49), channel_id=1, source_target_pairs={{0,1},{1,0},{2,3},{3,2},{4,5},{5,4},{6,7},{7,6},{8,9},{9,8},{10,11... | collective-permute-start | bytes 786440 | tf_op jit(solution)/shard_map/ppermute | solution.py:337
  80.6 20.3 %near_kernel.1.near_ref = bf16[256,512]{1,0:T(8,128)(2,1)S(1)} custom-call(bf16[256,512]{1,0:T(8,128)(2,1)S(1)} %get-tuple-element.46.query_ref, bf16[512,256]{1,0:T(8,128)(2,1)S(1)} %get-tuple-element.47.key_ref, bf16[256,512]{1,0:T(8,128)(2,1)S(1)} %get-tuple-element.48.value_ref), custom_call_target="tpu_custom_call" | custom-call | flops 6000000000 | bytes 4194304 | tf_op jit(solution)/shard_map/near_kernel/pallas_call | solution.py:338
  100.9 10.7 %core_kernel.1.core_ref = bf16[256,256]{1,0:T(8,128)(2,1)S(1)} custom-call(bf16[256,512]{1,0:T(8,128)(2,1)S(1)} %collective-permute-done.1.received_ref, bf16[256,512]{1,0:T(8,128)(2,1)S(1)} %get-tuple-element.50.far_query_ref, bf16[512,256]{1,0:T(8,128)(2,1)S(1)} %get-tuple-element.51.far_key_ref, bf16[256,512]{1,0:T(8,128)(2,1)S(1)} %get-tuple-element.52.far_value_ref), custom_call_target="tpu_custom_call" | custom-call | flops 3000000000 | bytes 4194304 | tf_op jit(solution)/shard_map/core_kernel/pallas_call | solution.py:340
  111.7 12.6 %cross_kernel.1 = bf16[1024,512]{1,0:T(8,128)(2,1)S(1)} custom-call(bf16[256,512]{1,0:T(8,128)(2,1)S(1)} %collective-permute-done.received_ref, bf16[256,512]{1,0:T(8,128)(2,1)S(1)} %near_kernel.1.near_ref, bf16[256,256]{1,0:T(8,128)(2,1)S(1)} %core_kernel.1.core_ref, bf16[256,512]{1,0:T(8,128)(2,1)S(1)} %get-tuple-element.50.far_query_ref, ...), custom_call_target="tpu_custom_call" | custom-call | flops 6000000000 | bytes 4194304 | tf_op jit(solution)/shard_map/cross_kernel/pallas_call | solution.py:347
  124.3 38.2 %all_to_all.22 = bf16[128,8,512]{2,1,0:T(8,128)(2,1)S(1)} all-to-all(bf16[128,8,512]{2,1,0:T(8,128)(2,1)S(1)} %bitcast.15), channel_id=1, replica_groups=mesh['dp'=4,'seq'=128] {'seq'}, dimensions={0} | all-to-all | bytes 2097152 | tf_op jit(solution)/shard_map/all_to_all | solution.py:355
  162.5 1.4 place_kernel.1
  (41 shorter events, 6.3 us)
Async XLA Ops:
  1.8 29.9 %all-to-all-start = ((s32[128,1,128]{2,1,0:T(1,128)}), s32[128,1,128]{2,1,0:T(1,128)S(1)}, u32[]{:S(2)}, u32[]{:S(2)}) async-start(s32[128,1,128]{2,1,0:T(1,128)} %bitcast.2), calls=%async_computation | async-start | bytes 131072 | tf_op jit(solution)/shard_map/all_to_all | solution.py:296
  20.2 1.0 copy-start.11
  23.1 15.9 %copy-start.22 = (f32[1536]{0:T(1024)S(1)}, f32[1536]{0:T(1024)}, u32[]{:S(2)}) copy-start(f32[1536]{0:T(1024)} %param.13) | copy-start | bytes 18436
  23.1 15.9 %copy-start.9 = (s32[512]{0:T(512)S(1)}, s32[512]{0:T(512)}, u32[]{:S(2)}) copy-start(s32[512]{0:T(512)} %param.9) | copy-start | bytes 6148
  23.1 15.9 %copy-start.15 = (f32[512]{0:T(512)S(1)}, f32[512]{0:T(512)}, u32[]{:S(2)}) copy-start(f32[512]{0:T(512)} %param.15) | copy-start | bytes 6148
  33.2 36.2 %all-to-all-start.1 = ((bf16[128,8,512]{2,1,0:T(8,128)(2,1)}), bf16[128,8,512]{2,1,0:T(8,128)(2,1)S(1)}, u32[]{:S(2)}, u32[]{:S(2)}) async-start(bf16[128,8,512]{2,1,0:T(8,128)(2,1)} %bitcast.6), calls=%async_computation.1 | async-start | bytes 2097152 | tf_op jit(solution)/shard_map/all_to_all | solution.py:312
  39.0 1.4 copy-start.10
  40.4 1.0 copy-start.12
  43.3 0.8 copy-start
  44.1 0.8 copy-start.2
  44.9 0.8 copy-start.4
  45.7 0.7 copy-start.6
  46.4 1.0 copy-start.16
  47.4 0.8 copy-start.18
  48.2 0.7 copy-start.20
  69.4 1.0 copy-start.1
  70.4 1.0 copy-start.3
  71.5 1.0 copy-start.5
  72.5 0.9 copy-start.7
  75.0 36.7 %collective-permute-start = (bf16[256,512]{1,0:T(8,128)(2,1)S(1)}, bf16[256,512]{1,0:T(8,128)(2,1)S(1)}, u32[]{:S(2)}, u32[]{:S(2)}) collective-permute-start(bf16[256,512]{1,0:T(8,128)(2,1)S(1)} %get-tuple-element.45), channel_id=1, source_target_pairs={{0,127},{1,2},{2,1},{3,4},{4,3},{5,6},{6,5},{7,8},{8,7},{9,10},{10... | collective-permute-start | bytes 786440 | tf_op jit(solution)/shard_map/ppermute | solution.py:336
  78.7 22.2 %collective-permute-start.1 = (bf16[256,512]{1,0:T(8,128)(2,1)S(1)}, bf16[256,512]{1,0:T(8,128)(2,1)S(1)}, u32[]{:S(2)}, u32[]{:S(2)}) collective-permute-start(bf16[256,512]{1,0:T(8,128)(2,1)S(1)} %get-tuple-element.49), channel_id=1, source_target_pairs={{0,1},{1,0},{2,3},{3,2},{4,5},{5,4},{6,7},{7,6},{8,9},{9,8},{10,11... | collective-permute-start | bytes 786440 | tf_op jit(solution)/shard_map/ppermute | solution.py:337
  100.9 10.7 %copy-start.17 = (bf16[1024,512]{1,0:T(8,128)(2,1)S(1)}, bf16[1024,512]{1,0:T(8,128)(2,1)}, u32[]{:S(2)}) copy-start(bf16[1024,512]{1,0:T(8,128)(2,1)} %copy-done.16) | copy-start | bytes 3145732
  100.9 10.8 %copy-start.19 = (bf16[512,512]{1,0:T(8,128)(2,1)S(1)}, bf16[512,512]{1,0:T(8,128)(2,1)}, u32[]{:S(2)}) copy-start(bf16[512,512]{1,0:T(8,128)(2,1)} %copy-done.18) | copy-start | bytes 1572868
  100.9 10.7 %copy-start.21 = (f32[512,128]{1,0:T(8,128)S(1)}, f32[512,128]{1,0:T(8,128)}, u32[]{:S(2)}) copy-start(f32[512,128]{1,0:T(8,128)} %copy-done.20) | copy-start | bytes 786436
  (3 other events, 2.0 us)

commit v7 on v6

--- a/solution.py
+++ b/solution.py
@@ -29,22 +29,28 @@
     return lax.dot_general(a, b, NT, preferred_element_type=F32)
 
 
-def ranks(order_row, peers):
+def before_matrix(rows):
+    return jnp.where(iota((rows, rows), 0) < iota((rows, rows), 1), 1.0, 0.0).astype(BF16)
+
+
+def ranks(order_row, peers, before):
     rows = order_row.shape[1]
     holder = jnp.right_shift(order_row, rows.bit_length() - 1)
     mine = iota((peers, rows), 0) == holder
     mine_bf = jnp.where(mine, 1.0, 0.0).astype(BF16)
-    before = jnp.where(iota((rows, rows), 0) < iota((rows, rows), 1), 1.0, 0.0).astype(BF16)
     rank = dot(mine_bf, before)
     rank_row = jnp.sum(jnp.where(mine, rank, 0.0), axis=0, keepdims=True).astype(jnp.int32)
     return holder, mine_bf, rank_row
 
 
-def request_kernel(order_ref, wanted_ref):
-    order_row = order_ref[...]
-    peers = wanted_ref.shape[0]
-    rows = order_row.shape[1]
-    _, mine_bf, rank_row = ranks(order_row, peers)
+def request_kernel(order_ref, wanted_ref, order_s, sem):
+    peers, rows = wanted_ref.shape[0], order_s.shape[1]
+    copy = pltpu.make_async_copy(order_ref, order_s, sem)
+    copy.start()
+    before = before_matrix(rows)
+    copy.wait()
+    order_row = order_s[...]
+    _, mine_bf, rank_row = ranks(order_row, peers, before)
     local = jnp.bitwise_and(order_row, rows - 1) + 1
     chosen = iota((LANES, rows), 0) == rank_row
     high = jnp.where(chosen, jnp.right_shift(local, 4).astype(F32), 0.0).astype(BF16)
@@ -107,20 +113,33 @@
 
 
 def setup_kernel(
-    asked_ref, order_ref, qkv_weight_ref, qkv_bias_ref, proj_weight_ref, proj_bias_ref,
-    arrange_ref, send_ref, place_ref, query_t_ref, key_ref, value_t_ref, proj_t_ref,
-    query_bias_ref, key_bias_ref, value_bias_ref, proj_bias_col_ref,
+    order_ref, qkv_weight_ref, qkv_bias_ref, proj_weight_ref, proj_bias_ref,
+    send_ref, query_t_ref, key_ref, value_t_ref, proj_t_ref, columns_ref, key_bias_ref,
 ):
-    peers = asked_ref.shape[0]
-    rows, slots = arrange_ref.shape
+    slots, rows = send_ref.shape
+    peers = slots // CAPACITY
     width = query_t_ref.shape[0]
-    holder, _, rank_row = ranks(order_ref[...], peers)
+    holder, _, rank_row = ranks(order_ref[...], peers, before_matrix(rows))
     slot = holder * CAPACITY + rank_row
     swapped = jnp.concatenate([slot[:, rows // 2 :], slot[:, : rows // 2]], axis=1)
     slot = jnp.where(jnp.bitwise_and(lax.axis_index("seq"), 1) == 1, swapped, slot)
     send_ref[...] = onehot_of(iota((slots, rows), 0) == slot)
-    slot_col = column(slot.astype(F32), rows).astype(jnp.int32)
-    arrange_ref[...] = onehot_of(slot_col[:, :1] == iota((rows, slots), 1))
+    query_t_ref[...] = jnp.transpose(qkv_weight_ref[:, :width])
+    key_ref[...] = qkv_weight_ref[:, width : 2 * width]
+    value_t_ref[...] = jnp.transpose(qkv_weight_ref[:, 2 * width :])
+    proj_t_ref[...] = jnp.transpose(proj_weight_ref[...])
+    key_bias_ref[...] = qkv_bias_ref[:, width : 2 * width]
+    place = iota((LANES, width), 0)
+    packed = jnp.where(place == 0, qkv_bias_ref[:, :width], 0.0)
+    packed = jnp.where(place == 1, qkv_bias_ref[:, 2 * width :], packed)
+    packed = jnp.where(place == 2, proj_bias_ref[...], packed)
+    packed = jnp.where(place == 3, slot.astype(F32), packed)
+    columns_ref[...] = jnp.transpose(packed)
+
+
+def place_setup_kernel(asked_ref, place_ref):
+    peers = asked_ref.shape[0]
+    rows, slots = place_ref.shape
     flipped = jnp.transpose(asked_ref[...].astype(F32)).astype(jnp.int32)
     expand = onehot_of(jnp.right_shift(iota((peers, slots), 1), 3) == iota((peers, slots), 0))
     high = dot(jnp.right_shift(flipped, 4).astype(F32).astype(BF16), expand)
@@ -128,25 +147,22 @@
     own = jnp.bitwise_and(iota((LANES, slots), 1), CAPACITY - 1) == iota((LANES, slots), 0)
     asked_row = jnp.sum(jnp.where(own, high * 16.0 + low, 0.0), axis=0, keepdims=True).astype(jnp.int32)
     place_ref[...] = onehot_of(iota((rows, slots), 0) + 1 == asked_row)
-    query_t_ref[...] = jnp.transpose(qkv_weight_ref[:, :width])
-    key_ref[...] = qkv_weight_ref[:, width : 2 * width]
-    value_t_ref[...] = jnp.transpose(qkv_weight_ref[:, 2 * width :])
-    proj_t_ref[...] = jnp.transpose(proj_weight_ref[...])
-    query_bias_ref[...] = column(qkv_bias_ref[:, :width], width)
-    key_bias_ref[...] = qkv_bias_ref[:, width : 2 * width]
-    value_bias_ref[...] = column(qkv_bias_ref[:, 2 * width :], width)
-    proj_bias_col_ref[...] = column(proj_bias_ref[...], width)
 
 
 def arrange_kernel(
-    arrived_ref, onehot_ref, query_t_ref, key_ref, value_t_ref, query_bias_ref, key_bias_ref, value_bias_ref,
+    arrived_ref, columns_ref, query_t_ref, key_ref, value_t_ref, key_bias_ref,
     cross_ref, core_ref, query_ref, key_out_ref, value_ref, far_query_ref, far_key_ref, far_value_ref,
 ):
     half, rows = query_ref.shape
-    middle = rows // 2
-    seq = dot(onehot_ref[...], arrived_ref[...]).astype(BF16)
+    middle, slots = rows // 2, arrived_ref.shape[0]
+    arrived = arrived_ref[...]
+    parts = []
+    for part in (slice(0, middle), slice(middle, rows)):
+        slot = columns_ref[part, 3:4].astype(jnp.int32)
+        parts.append(dot(onehot_of(slot == iota((middle, slots), 1)), arrived).astype(BF16))
+    seq = jnp.concatenate(parts, axis=0)
     keys = (dot(seq, key_ref[...]) + key_bias_ref[...]).astype(BF16)
-    values = (dot_nt(value_t_ref[...], seq) + value_bias_ref[:, :1]).astype(BF16)
+    values = (dot_nt(value_t_ref[...], seq) + columns_ref[:, 1:2]).astype(BF16)
     for ref, part in ((cross_ref, slice(0, middle)), (core_ref, slice(middle, rows))):
         ref[:, :half] = keys[part, half:]
         ref[:, half:] = values[half:, part]
@@ -154,7 +170,7 @@
     far_key_ref[...] = keys[:, half:]
     value_ref[...] = values[:half]
     far_value_ref[...] = values[half:]
-    queries = (dot_nt(query_t_ref[...], seq) + query_bias_ref[:, :1]).astype(BF16)
+    queries = (dot_nt(query_t_ref[...], seq) + columns_ref[:, 0:1]).astype(BF16)
     query_ref[...] = queries[:half]
     far_query_ref[...] = queries[half:]
 
@@ -243,7 +259,7 @@
 
 
 def cross_kernel(
-    received_ref, near_ref, core_ref, far_query_ref, far_key_ref, far_value_ref, proj_t_ref, proj_bias_ref, send_ref,
+    received_ref, near_ref, core_ref, far_query_ref, far_key_ref, far_value_ref, proj_t_ref, columns_ref, send_ref,
     outgoing_ref, attended_s, key_s, value_s, stage, sems,
 ):
     middle, half = received_ref.shape[0], near_ref.shape[0]
@@ -251,7 +267,7 @@
     attended_s[:half] = near_ref[...]
     attended_s[half:, middle:] = core_ref[...]
     attend(far_query_ref, [(key_s, value_s, 0, middle)], attended_s, half)
-    update = (dot(proj_t_ref[...], attended_s[...]) + proj_bias_ref[:, :1]).astype(BF16)
+    update = (dot(proj_t_ref[...], attended_s[...]) + columns_ref[:, 2:3]).astype(BF16)
 
     def make(chunk, size):
         return dot_nt(send_ref[chunk * size : (chunk + 1) * size], update).astype(BF16)
@@ -268,7 +284,7 @@
     send_chunks(make, out_ref, stage, sems)
 
 
-def call(kernel, outs, count, scratch=(), flops=0, in_hbm=False, out_hbm=False):
+def call(kernel, outs, count, scratch=(), flops=0, in_hbm=False, out_hbm=False, mib=20):
     vmem, hbm = pl.BlockSpec(memory_space=pltpu.VMEM), pl.BlockSpec(memory_space=pl.ANY)
     out_specs = [hbm if out_hbm else vmem] * len(outs)
     return pl.pallas_call(
@@ -277,7 +293,7 @@
         in_specs=[hbm if in_hbm else vmem] * count,
         out_specs=out_specs if len(outs) > 1 else out_specs[0],
         scratch_shapes=list(scratch),
-        compiler_params=pltpu.CompilerParams(vmem_limit_bytes=20 * 1024 * 1024),
+        compiler_params=pltpu.CompilerParams(vmem_limit_bytes=mib * 1024 * 1024),
         cost_estimate=pl.CostEstimate(flops=flops, bytes_accessed=4 * 1024 * 1024, transcendentals=0),
         name=kernel.__name__,
     )
@@ -292,7 +308,14 @@
     chunk_sems = pltpu.SemaphoreType.DMA((CHUNKS,))
     row_vector = pltpu.VMEM((1, width), F32)
 
-    wanted = call(request_kernel, [shape((peers, LANES), jnp.int32)], 1)(order.reshape(1, rows))
+    wanted = call(
+        request_kernel,
+        [shape((peers, LANES), jnp.int32)],
+        1,
+        [pltpu.VMEM((1, rows), jnp.int32), pltpu.SemaphoreType.DMA],
+        in_hbm=True,
+        mib=60,
+    )(order.reshape(1, rows))
     asked = lax.all_to_all(wanted, "seq", split_axis=0, concat_axis=0, tiled=True)
     normed = call(
         norm_kernel,
@@ -306,33 +329,27 @@
     picked = call(pick_kernel, [shape((slots, width), BF16)], 2, staging, out_hbm=True)(
         asked.reshape(peers, 1, LANES), normed
     )
-    picked, asked, order, qkv_weight, qkv_bias, proj_weight, proj_bias = lax.optimization_barrier(
-        (picked, asked, order, qkv_weight, qkv_bias, proj_weight, proj_bias)
+    picked, order, qkv_weight, qkv_bias, proj_weight, proj_bias = lax.optimization_barrier(
+        (picked, order, qkv_weight, qkv_bias, proj_weight, proj_bias)
     )
     arrived = lax.all_to_all(
         picked.reshape(peers, CAPACITY, width), "seq", split_axis=0, concat_axis=0, tiled=True
     )
-    square, columns = shape((width, width), BF16), shape((width, LANES), F32)
-    (
-        arrange, send, place, query_t, key_weight, value_t, proj_t,
-        query_bias, key_bias, value_bias, proj_bias_col,
-    ) = call(
+    square = shape((width, width), BF16)
+    send, query_t, key_weight, value_t, proj_t, columns, key_bias = call(
         setup_kernel,
         [
-            shape((rows, slots), BF16), shape((slots, rows), BF16), shape((rows, slots), BF16),
-            square, square, square, square, columns, shape((1, width), F32), columns, columns,
+            shape((slots, rows), BF16), square, square, square, square, shape((width, LANES), F32),
+            shape((1, width), F32),
         ],
-        6,
+        5,
         flops=8_000_000_000,
-    )(
-        asked, order.reshape(1, rows), qkv_weight, qkv_bias.reshape(1, 3 * width), proj_weight,
-        proj_bias.reshape(1, width),
-    )
+    )(order.reshape(1, rows), qkv_weight, qkv_bias.reshape(1, 3 * width), proj_weight, proj_bias.reshape(1, width))
     halves = shape((middle, width), BF16)
     wide, tall = shape((half, rows), BF16), shape((rows, half), BF16)
     cross, core, query, key, value, far_query, far_key, far_value = call(
-        arrange_kernel, [halves, halves, wide, tall, wide, wide, tall, wide], 8
-    )(arrived.reshape(slots, width), arrange, query_t, key_weight, value_t, query_bias, key_bias, value_bias)
+        arrange_kernel, [halves, halves, wide, tall, wide, wide, tall, wide], 6
+    )(arrived.reshape(slots, width), columns, query_t, key_weight, value_t, key_bias)
     cross = lax.ppermute(cross, "seq", [(i, (i + 2 * (i % 2) - 1) % peers) for i in range(peers)])
     core = lax.ppermute(core, "seq", [(i, i + 1 - 2 * (i % 2)) for i in range(peers)])
     near = call(near_kernel, [wide], 3, flops=6_000_000_000)(query, key, value)
@@ -351,7 +368,9 @@
         [pltpu.VMEM((width, rows), BF16), *patch_s, *staging],
         flops=6_000_000_000,
         out_hbm=True,
-    )(cross, near, core_attended, far_query, far_key, far_value, proj_t, proj_bias_col, send)
+    )(cross, near, core_attended, far_query, far_key, far_value, proj_t, columns, send)
+    outgoing, asked = lax.optimization_barrier((outgoing, asked))
+    place = call(place_setup_kernel, [shape((rows, slots), BF16)], 1, flops=2_000_000_000)(asked)
     returned = lax.all_to_all(
         outgoing.reshape(peers, CAPACITY, width), "seq", split_axis=0, concat_axis=0, tiled=True
     )

time: 165 us -> 161 us (0.976)
  blocking collectives: 38.2 us -> 0 us
  waiting for transfers between devices: 29.1 us -> 64.7 us
  local copies, waits for them, and re-layouts: 15.2 us -> 5.62 us
  starting transfers between devices: 29.8 us -> 37.8 us
    all_to_all x1 -> x0, blocking collectives: 38.2 us -> none  [per_device(): lax.all_to_all(outgoing.reshape(peers, CAPACITY, width), 'seq', split_axi...]
    all_to_all x0 -> x1, waiting for transfers between devices: none -> 29.8 us  [per_device(): lax.all_to_all(outgoing.reshape(peers, CAPACITY, width), 'seq', split_axi...]
    unnamed x46 -> x24, local copies, waits for them, and re-layouts: 15.2 us -> 5.61 us
    all_to_all x0 -> x1, starting transfers between devices: none -> 8 us  [per_device(): lax.all_to_all(outgoing.reshape(peers, CAPACITY, width), 'seq', split_axi...]
    all_to_all x1, waiting for transfers between devices: 20.5 us -> 26.3 us  [per_device(): lax.all_to_all(picked.reshape(peers, CAPACITY, width), 'seq', split_axis=...]
  transfers between devices with their start and end apart: 4 -> 5, of which waited for: 2 -> 3; matrix products, arithmetic and copies ran while one was open for 0% -> 0% of each run, Pallas kernels for 20% -> 20%
where the time goes in v7:
time: 161 us; the launch traced here: 160 us
  waiting for transfers between devices  64.7 us (40%)
  Pallas kernels  51.7 us (32%)
  starting transfers between devices  37.8 us (23%)
  local copies, waits for them, and re-layouts  5.62 us (3%)
    all_to_all x1, waiting for transfers between devices, per_device(): lax.all_to_all(outgoing.reshape(peers, CAPACITY, width), 'seq', split_axi...  29.8 us
    all_to_all x1, waiting for transfers between devices, per_device(): lax.all_to_all(picked.reshape(peers, CAPACITY, width), 'seq', split_axis=...  26.3 us
    pallas_call x1, Pallas kernels, per_device(): near = call(near_kernel, [wide], 3, flops=6000000000)(query, key, value)  20.2 us
    all_to_all x1, starting transfers between devices, per_device(): lax.all_to_all(wanted, 'seq', split_axis=0, concat_axis=0, tiled=True)  18.4 us
    pallas_call x1, Pallas kernels, per_device(): call(cross_kernel, [shape((slots, width), BF16)], 9, [pltpu.VMEM((width,...  12.6 us
    pallas_call x1, Pallas kernels, per_device(): call(core_kernel, [shape((half, middle), BF16)], 4, [pltpu.VMEM((half, mi...  10.7 us
    all_to_all x1, waiting for transfers between devices, per_device(): lax.all_to_all(wanted, 'seq', split_axis=0, concat_axis=0, tiled=True)  8.57 us
    all_to_all x1, starting transfers between devices, per_device(): lax.all_to_all(outgoing.reshape(peers, CAPACITY, width), 'seq', split_axi...  8 us
  transfers between devices with their start and end apart: 5, of which 3 were waited for; matrix products, arithmetic and copies ran while one was open for 0% of the time, Pallas kernels for 20%

profile of v7, /device:TPU:1, one launch (start us, length us, event | category | flops | bytes accessed | tf_op | source)
XLA Modules:
  0.0 160.1 jit_solution(3639630972917209595)
XLA Ops:
  0.0 1.8 %request_kernel.1 = s32[128,128]{1,0:T(8,128)} custom-call(s32[1,512]{1,0:T(1,128)} %bitcast.16), custom_call_target="tpu_custom_call" | custom-call | bytes 4194304 | tf_op jit(solution)/shard_map/request_kernel/pallas_call | solution.py:311
  1.8 18.4 %all-to-all-start = ((s32[128,1,128]{2,1,0:T(1,128)}), s32[128,1,128]{2,1,0:T(1,128)S(1)}, u32[]{:S(2)}, u32[]{:S(2)}) async-start(s32[128,1,128]{2,1,0:T(1,128)} %bitcast.21), calls=%async_computation | async-start | bytes 131072 | tf_op jit(solution)/shard_map/all_to_all | solution.py:319
  20.3 1.0 copy-done.2
  21.3 0.7 copy-done.4
  22.0 0.7 copy-done.5
  22.7 0.4 norm_kernel.1.normed_ref
  23.1 8.6 %all-to-all-done.asked_ref = s32[128,1,128]{2,1,0:T(1,128)S(1)} async-done(((s32[128,1,128]{2,1,0:T(1,128)}), s32[128,1,128]{2,1,0:T(1,128)S(1)}, u32[]{:S(2)}, u32[]{:S(2)}) %all-to-all-start) | async-done | bytes 65568 | tf_op jit(solution)/shard_map/all_to_all | solution.py:319
  31.7 1.5 pick_kernel.1
  33.2 5.7 %all-to-all-start.1 = ((bf16[128,8,512]{2,1,0:T(8,128)(2,1)}), bf16[128,8,512]{2,1,0:T(8,128)(2,1)S(1)}, u32[]{:S(2)}, u32[]{:S(2)}) async-start(bf16[128,8,512]{2,1,0:T(8,128)(2,1)} %bitcast.5), calls=%async_computation.1 | async-start | bytes 2097152 | tf_op jit(solution)/shard_map/all_to_all | solution.py:335
  39.0 1.4 copy-done.1
  40.4 0.9 setup_kernel.1
  41.3 1.0 copy-done.7
  42.3 0.8 copy-done.9
  43.1 26.3 %all-to-all-done.1 = bf16[128,8,512]{2,1,0:T(8,128)(2,1)S(1)} async-done(((bf16[128,8,512]{2,1,0:T(8,128)(2,1)}), bf16[128,8,512]{2,1,0:T(8,128)(2,1)S(1)}, u32[]{:S(2)}, u32[]{:S(2)}) %all-to-all-start.1) | async-done | bytes 1048608 | tf_op jit(solution)/shard_map/all_to_all | solution.py:335
  69.4 1.6 arrange_kernel.1
  70.9 3.7 %collective-permute-start = (bf16[256,512]{1,0:T(8,128)(2,1)S(1)}, bf16[256,512]{1,0:T(8,128)(2,1)S(1)}, u32[]{:S(2)}, u32[]{:S(2)}) collective-permute-start(bf16[256,512]{1,0:T(8,128)(2,1)S(1)} %get-tuple-element.39), channel_id=1, source_target_pairs={{0,127},{1,2},{2,1},{3,4},{4,3},{5,6},{6,5},{7,8},{8,7},{9,10},{10... | collective-permute-start | bytes 786440 | tf_op jit(solution)/shard_map/ppermute | solution.py:353
  74.6 1.9 %collective-permute-start.1 = (bf16[256,512]{1,0:T(8,128)(2,1)S(1)}, bf16[256,512]{1,0:T(8,128)(2,1)S(1)}, u32[]{:S(2)}, u32[]{:S(2)}) collective-permute-start(bf16[256,512]{1,0:T(8,128)(2,1)S(1)} %get-tuple-element.43), channel_id=1, source_target_pairs={{0,1},{1,0},{2,3},{3,2},{4,5},{5,4},{6,7},{7,6},{8,9},{9,8},{10,11... | collective-permute-start | bytes 786440 | tf_op jit(solution)/shard_map/ppermute | solution.py:354
  76.6 20.2 %near_kernel.1.near_ref = bf16[256,512]{1,0:T(8,128)(2,1)S(1)} custom-call(bf16[256,512]{1,0:T(8,128)(2,1)S(1)} %get-tuple-element.40.query_ref, bf16[512,256]{1,0:T(8,128)(2,1)S(1)} %get-tuple-element.41.key_ref, bf16[256,512]{1,0:T(8,128)(2,1)S(1)} %get-tuple-element.42.value_ref), custom_call_target="tpu_custom_call" | custom-call | flops 6000000000 | bytes 4194304 | tf_op jit(solution)/shard_map/near_kernel/pallas_call | solution.py:355
  96.8 10.7 %core_kernel.1.core_ref = bf16[256,256]{1,0:T(8,128)(2,1)S(1)} custom-call(bf16[256,512]{1,0:T(8,128)(2,1)S(1)} %collective-permute-done.1.received_ref, bf16[256,512]{1,0:T(8,128)(2,1)S(1)} %get-tuple-element.44.far_query_ref, bf16[512,256]{1,0:T(8,128)(2,1)S(1)} %get-tuple-element.45.far_key_ref, bf16[256,512]{1,0:T(8,128)(2,1)S(1)} %get-tuple-element.46.far_value_ref), custom_call_target="tpu_custom_call" | custom-call | flops 3000000000 | bytes 4194304 | tf_op jit(solution)/shard_map/core_kernel/pallas_call | solution.py:357
  107.5 12.6 %cross_kernel.1 = bf16[1024,512]{1,0:T(8,128)(2,1)} custom-call(bf16[256,512]{1,0:T(8,128)(2,1)S(1)} %collective-permute-done.received_ref, bf16[256,512]{1,0:T(8,128)(2,1)S(1)} %near_kernel.1.near_ref, bf16[256,256]{1,0:T(8,128)(2,1)S(1)} %core_kernel.1.core_ref, bf16[256,512]{1,0:T(8,128)(2,1)S(1)} %get-tuple-element.44.far_query_ref, ...), custom_call_target="tpu_custom_call" | custom-call | flops 6000000000 | bytes 4194304 | tf_op jit(solution)/shard_map/cross_kernel/pallas_call | solution.py:364
  120.1 8.0 %all-to-all-start.2 = ((bf16[128,8,512]{2,1,0:T(8,128)(2,1)}), bf16[128,8,512]{2,1,0:T(8,128)(2,1)S(1)}, u32[]{:S(2)}, u32[]{:S(2)}) async-start(bf16[128,8,512]{2,1,0:T(8,128)(2,1)} %bitcast.10), calls=%async_computation.2 | async-start | bytes 2097152 | tf_op jit(solution)/shard_map/all_to_all | solution.py:374
  128.1 0.6 place_setup_kernel.1.onehot_ref
  128.7 29.8 %all-to-all-done.2 = bf16[128,8,512]{2,1,0:T(8,128)(2,1)S(1)} async-done(((bf16[128,8,512]{2,1,0:T(8,128)(2,1)}), bf16[128,8,512]{2,1,0:T(8,128)(2,1)S(1)}, u32[]{:S(2)}, u32[]{:S(2)}) %all-to-all-start.2) | async-done | bytes 1048608 | tf_op jit(solution)/shard_map/all_to_all | solution.py:374
  158.5 1.4 place_kernel.1
  (21 shorter events, 0.1 us)
Async XLA Ops:
  1.8 29.9 %all-to-all-start = ((s32[128,1,128]{2,1,0:T(1,128)}), s32[128,1,128]{2,1,0:T(1,128)S(1)}, u32[]{:S(2)}, u32[]{:S(2)}) async-start(s32[128,1,128]{2,1,0:T(1,128)} %bitcast.21), calls=%async_computation | async-start | bytes 131072 | tf_op jit(solution)/shard_map/all_to_all | solution.py:319
  20.2 1.0 copy-start.2
  21.3 0.7 copy-start.4
  22.0 0.7 copy-start.5
  23.1 15.9 %copy-start.11 = (f32[1536]{0:T(1024)S(1)}, f32[1536]{0:T(1024)}, u32[]{:S(2)}) copy-start(f32[1536]{0:T(1024)} %param.13) | copy-start | bytes 18436
  23.1 15.9 %copy-start = (s32[512]{0:T(512)S(1)}, s32[512]{0:T(512)}, u32[]{:S(2)}) copy-start(s32[512]{0:T(512)} %param.9) | copy-start | bytes 6148
  23.1 15.9 %copy-start.3 = (bf16[512,512]{1,0:T(8,128)(2,1)S(1)}, bf16[512,512]{1,0:T(8,128)(2,1)}, u32[]{:S(2)}) copy-start(bf16[512,512]{1,0:T(8,128)(2,1)} %proj_weight_ref) | copy-start | bytes 1572868
  23.1 15.9 %copy-start.6 = (f32[512]{0:T(512)S(1)}, f32[512]{0:T(512)}, u32[]{:S(2)}) copy-start(f32[512]{0:T(512)} %param.15) | copy-start | bytes 6148
  33.2 36.2 %all-to-all-start.1 = ((bf16[128,8,512]{2,1,0:T(8,128)(2,1)}), bf16[128,8,512]{2,1,0:T(8,128)(2,1)S(1)}, u32[]{:S(2)}, u32[]{:S(2)}) async-start(bf16[128,8,512]{2,1,0:T(8,128)(2,1)} %bitcast.5), calls=%async_computation.1 | async-start | bytes 2097152 | tf_op jit(solution)/shard_map/all_to_all | solution.py:335
  39.0 1.4 copy-start.1
  41.3 1.0 copy-start.7
  42.3 0.8 copy-start.9
  70.9 36.5 %collective-permute-start = (bf16[256,512]{1,0:T(8,128)(2,1)S(1)}, bf16[256,512]{1,0:T(8,128)(2,1)S(1)}, u32[]{:S(2)}, u32[]{:S(2)}) collective-permute-start(bf16[256,512]{1,0:T(8,128)(2,1)S(1)} %get-tuple-element.39), channel_id=1, source_target_pairs={{0,127},{1,2},{2,1},{3,4},{4,3},{5,6},{6,5},{7,8},{8,7},{9,10},{10... | collective-permute-start | bytes 786440 | tf_op jit(solution)/shard_map/ppermute | solution.py:353
  74.6 22.1 %collective-permute-start.1 = (bf16[256,512]{1,0:T(8,128)(2,1)S(1)}, bf16[256,512]{1,0:T(8,128)(2,1)S(1)}, u32[]{:S(2)}, u32[]{:S(2)}) collective-permute-start(bf16[256,512]{1,0:T(8,128)(2,1)S(1)} %get-tuple-element.43), channel_id=1, source_target_pairs={{0,1},{1,0},{2,3},{3,2},{4,5},{5,4},{6,7},{7,6},{8,9},{9,8},{10,11... | collective-permute-start | bytes 786440 | tf_op jit(solution)/shard_map/ppermute | solution.py:354
  96.7 10.7 %copy-start.8 = (bf16[1024,512]{1,0:T(8,128)(2,1)S(1)}, bf16[1024,512]{1,0:T(8,128)(2,1)}, u32[]{:S(2)}) copy-start(bf16[1024,512]{1,0:T(8,128)(2,1)} %copy-done.7) | copy-start | bytes 3145732
  96.7 10.7 %copy-start.10 = (bf16[512,512]{1,0:T(8,128)(2,1)S(1)}, bf16[512,512]{1,0:T(8,128)(2,1)}, u32[]{:S(2)}) copy-start(bf16[512,512]{1,0:T(8,128)(2,1)} %copy-done.9) | copy-start | bytes 1572868
  120.1 38.4 %all-to-all-start.2 = ((bf16[128,8,512]{2,1,0:T(8,128)(2,1)}), bf16[128,8,512]{2,1,0:T(8,128)(2,1)S(1)}, u32[]{:S(2)}, u32[]{:S(2)}) async-start(bf16[128,8,512]{2,1,0:T(8,128)(2,1)} %bitcast.10), calls=%async_computation.2 | async-start | bytes 2097152 | tf_op jit(solution)/shard_map/all_to_all | solution.py:374

commit v8 on v7

--- a/solution.py
+++ b/solution.py
@@ -31,6 +31,10 @@
 
 def before_matrix(rows):
     return jnp.where(iota((rows, rows), 0) < iota((rows, rows), 1), 1.0, 0.0).astype(BF16)
+
+
+def odd_device():
+    return jnp.bitwise_and(lax.axis_index("seq"), 1)
 
 
 def ranks(order_row, peers, before):
@@ -122,7 +126,7 @@
     holder, _, rank_row = ranks(order_ref[...], peers, before_matrix(rows))
     slot = holder * CAPACITY + rank_row
     swapped = jnp.concatenate([slot[:, rows // 2 :], slot[:, : rows // 2]], axis=1)
-    slot = jnp.where(jnp.bitwise_and(lax.axis_index("seq"), 1) == 1, swapped, slot)
+    slot = jnp.where(odd_device() == 1, swapped, slot)
     send_ref[...] = onehot_of(iota((slots, rows), 0) == slot)
     query_t_ref[...] = jnp.transpose(qkv_weight_ref[:, :width])
     key_ref[...] = qkv_weight_ref[:, width : 2 * width]
@@ -149,9 +153,77 @@
     place_ref[...] = onehot_of(iota((rows, slots), 0) + 1 == asked_row)
 
 
+def attend(queries_ref, sides, out_ref, out_start):
+    channels, rows = queries_ref.shape
+    heads = channels // HEAD_DIM
+
+    def sums(expanded):
+        return jnp.sum(expanded, axis=0, keepdims=True)
+
+    def scores(item):
+        head, (keys, _, begin, end) = item
+        group, place = divmod(head, GROUP)
+        parts = [queries_ref[head * HEAD_DIM : (head + 1) * HEAD_DIM, begin:end]]
+        if place > 0:
+            parts.insert(0, jnp.zeros((HEAD_DIM * place, end - begin), BF16))
+        if place < GROUP - 1:
+            parts.append(jnp.zeros((HEAD_DIM * (GROUP - 1 - place), end - begin), BF16))
+        return dot(keys[:, group * LANES : (group + 1) * LANES], jnp.concatenate(parts, axis=0))
+
+    def store(item, weights):
+        head, (_, values, begin, end) = item
+        mixed = dot(values[head * HEAD_DIM : (head + 1) * HEAD_DIM, :], weights)
+        start = out_start + head * HEAD_DIM
+        out_ref[start : start + HEAD_DIM, begin:end] = mixed.astype(BF16)
+
+    items = [(head, side) for head in range(heads) for side in sides]
+    ahead = [scores(item) for item in items[:2]]
+    previous = None
+    least = most = None
+    for index, item in enumerate(items):
+        if index + 2 < len(items):
+            ahead.append(scores(items[index + 2]))
+        expanded = jnp.exp2(ahead.pop(0) * SCALE)
+        total = sums(expanded)
+        least = total if least is None else jnp.minimum(least, total)
+        most = total if most is None else jnp.maximum(most, total)
+        weights = (expanded * (1.0 / total)).astype(BF16)
+        if previous is not None:
+            store(items[index - 1], previous)
+        previous = weights
+    store(items[-1], previous)
+    in_range = jnp.logical_and(jnp.min(least) >= SUM_LOW, jnp.max(most) <= SUM_HIGH)
+
+    @pl.when(jnp.logical_not(in_range))
+    def _():
+        def one_head(head, carry):
+            group = head // GROUP
+            start = pl.multiple_of(group * LANES, LANES)
+            base = pl.multiple_of(head * HEAD_DIM, HEAD_DIM)
+            for keys, values, begin, end in sides:
+                inside = jnp.right_shift(iota((LANES, end - begin), 0), 4) == head - group * GROUP
+                query = queries_ref[pl.ds(start, LANES), begin:end]
+                part = dot(keys[:, pl.ds(start, LANES)], jnp.where(inside, query, jnp.zeros((), BF16)))
+                expanded = jnp.exp2((part - jnp.max(part, axis=0, keepdims=True)) * SCALE)
+                weights = (expanded * (1.0 / sums(expanded))).astype(BF16)
+                mixed = dot(values[pl.ds(base, HEAD_DIM), :], weights)
+                out_ref[pl.ds(out_start + base, HEAD_DIM), begin:end] = mixed.astype(BF16)
+            return carry
+
+        lax.fori_loop(0, heads, one_head, 0)
+
+
+def attend_near(query_ref, key_ref, value_ref, start, out_ref, out_start):
+    rows = query_ref.shape[1]
+    middle, part = rows // 2, pl.ds(start, LANES)
+    keys, values = key_ref.at[:, part], value_ref.at[part, :]
+    sides = [(keys, values, 0, middle), (keys, values, middle, rows)]
+    attend(query_ref.at[part, :], sides, out_ref, out_start)
+
+
 def arrange_kernel(
     arrived_ref, columns_ref, query_t_ref, key_ref, value_t_ref, key_bias_ref,
-    cross_ref, core_ref, query_ref, key_out_ref, value_ref, far_query_ref, far_key_ref, far_value_ref,
+    cross_ref, core_ref, query_ref, key_out_ref, value_ref, far_query_ref, far_key_ref, far_value_ref, early_ref,
 ):
     half, rows = query_ref.shape
     middle, slots = rows // 2, arrived_ref.shape[0]
@@ -174,72 +246,23 @@
     query_ref[...] = queries[:half]
     far_query_ref[...] = queries[half:]
 
-
-def attend(queries_ref, sides, out_ref, out_start):
-    channels, rows = queries_ref.shape
-    heads = channels // HEAD_DIM
-
-    def sums(expanded):
-        return jnp.sum(expanded, axis=0, keepdims=True)
-
-    def scores(item):
-        head, (keys, _, begin, end) = item
-        group, place = divmod(head, GROUP)
-        parts = [queries_ref[head * HEAD_DIM : (head + 1) * HEAD_DIM, begin:end]]
-        if place > 0:
-            parts.insert(0, jnp.zeros((HEAD_DIM * place, end - begin), BF16))
-        if place < GROUP - 1:
-            parts.append(jnp.zeros((HEAD_DIM * (GROUP - 1 - place), end - begin), BF16))
-        return dot(keys[:, group * LANES : (group + 1) * LANES], jnp.concatenate(parts, axis=0))
-
-    def store(item, weights):
-        head, (_, values, begin, end) = item
-        mixed = dot(values[head * HEAD_DIM : (head + 1) * HEAD_DIM, :], weights)
-        start = out_start + head * HEAD_DIM
-        out_ref[start : start + HEAD_DIM, begin:end] = mixed.astype(BF16)
-
-    items = [(head, side) for head in range(heads) for side in sides]
-    ahead = [scores(item) for item in items[:2]]
-    previous = None
-    least = most = None
-    for index, item in enumerate(items):
-        if index + 2 < len(items):
-            ahead.append(scores(items[index + 2]))
-        expanded = jnp.exp2(ahead.pop(0) * SCALE)
-        total = sums(expanded)
-        least = total if least is None else jnp.minimum(least, total)
-        most = total if most is None else jnp.maximum(most, total)
-        weights = (expanded * (1.0 / total)).astype(BF16)
-        if previous is not None:
-            store(items[index - 1], previous)
-        previous = weights
-    store(items[-1], previous)
-    in_range = jnp.logical_and(jnp.min(least) >= SUM_LOW, jnp.max(most) <= SUM_HIGH)
-
-    @pl.when(jnp.logical_not(in_range))
+    @pl.when(odd_device() == 1)
     def _():
-        def one_head(head, carry):
-            group = head // GROUP
-            start = pl.multiple_of(group * LANES, LANES)
-            base = pl.multiple_of(head * HEAD_DIM, HEAD_DIM)
-            for keys, values, begin, end in sides:
-                inside = jnp.right_shift(iota((LANES, end - begin), 0), 4) == head - group * GROUP
-                query = queries_ref[pl.ds(start, LANES), begin:end]
-                part = dot(keys[:, pl.ds(start, LANES)], jnp.where(inside, query, jnp.zeros((), BF16)))
-                expanded = jnp.exp2((part - jnp.max(part, axis=0, keepdims=True)) * SCALE)
-                weights = (expanded * (1.0 / sums(expanded))).astype(BF16)
-                mixed = dot(values[pl.ds(base, HEAD_DIM), :], weights)
-                out_ref[pl.ds(out_start + base, HEAD_DIM), begin:end] = mixed.astype(BF16)
-            return carry
-
-        lax.fori_loop(0, heads, one_head, 0)
-
-
-def near_kernel(query_ref, key_ref, value_ref, attended_ref):
-    rows = query_ref.shape[1]
-    middle = rows // 2
-    sides = [(key_ref, value_ref, 0, middle), (key_ref, value_ref, middle, rows)]
-    attend(query_ref, sides, attended_ref, 0)
+        attend_near(query_ref, key_out_ref, value_ref, 0, early_ref, 0)
+
+
+def near_kernel(query_ref, key_ref, value_ref, early_ref, attended_ref):
+    odd = odd_device()
+
+    @pl.when(odd == 1)
+    def _():
+        attended_ref[:LANES] = early_ref[...]
+
+    @pl.when(odd == 0)
+    def _():
+        attend_near(query_ref, key_ref, value_ref, 0, attended_ref, 0)
+
+    attend_near(query_ref, key_ref, value_ref, LANES, attended_ref, LANES)
 
 
 def extend(received_ref, own, far_key_ref, far_value_ref, key_s, value_s):
@@ -347,12 +370,13 @@
     )(order.reshape(1, rows), qkv_weight, qkv_bias.reshape(1, 3 * width), proj_weight, proj_bias.reshape(1, width))
     halves = shape((middle, width), BF16)
     wide, tall = shape((half, rows), BF16), shape((rows, half), BF16)
-    cross, core, query, key, value, far_query, far_key, far_value = call(
-        arrange_kernel, [halves, halves, wide, tall, wide, wide, tall, wide], 6
+    early_heads = shape((LANES, rows), BF16)
+    cross, core, query, key, value, far_query, far_key, far_value, early = call(
+        arrange_kernel, [halves, halves, wide, tall, wide, wide, tall, wide, early_heads], 6
     )(arrived.reshape(slots, width), columns, query_t, key_weight, value_t, key_bias)
     cross = lax.ppermute(cross, "seq", [(i, (i + 2 * (i % 2) - 1) % peers) for i in range(peers)])
     core = lax.ppermute(core, "seq", [(i, i + 1 - 2 * (i % 2)) for i in range(peers)])
-    near = call(near_kernel, [wide], 3, flops=6_000_000_000)(query, key, value)
+    near = call(near_kernel, [wide], 4, flops=6_000_000_000)(query, key, value, early)
     patch_s = [pltpu.VMEM((rows, half), BF16), pltpu.VMEM((half, rows), BF16)]
     core_attended = call(
         core_kernel,

time: 161 us -> 171 us (1.062)
  starting transfers between devices: 37.8 us -> 47.4 us
    all_to_all x1, starting transfers between devices: 8 us -> 18 us  [per_device(): lax.all_to_all(outgoing.reshape(peers, CAPACITY, width), 'seq', split_axi...]
    ppermute x1, starting transfers between devices: 3.68 us -> 1.93 us  [per_device(): lax.ppermute(cross, 'seq', [(i, (i + 2 * (i % 2) - 1) % peers) for i in r...]
  transfers between devices with their start and end apart: 5 -> 5, of which waited for: 3 -> 3; matrix products, arithmetic and copies ran while one was open for 0% -> 0% of each run, Pallas kernels for 20% -> 14%
where the time goes in v8:
time: 171 us; the launch traced here: 170 us
  waiting for transfers between devices  64.7 us (38%)
  Pallas kernels  52.2 us (31%)
  starting transfers between devices  47.4 us (28%)
  local copies, waits for them, and re-layouts  5.63 us (3%)
    all_to_all x1, waiting for transfers between devices, per_device(): lax.all_to_all(outgoing.reshape(peers, CAPACITY, width), 'seq', split_axi...  29.8 us
    all_to_all x1, waiting for transfers between devices, per_device(): lax.all_to_all(picked.reshape(peers, CAPACITY, width), 'seq', split_axis=...  26.3 us
    all_to_all x1, starting transfers between devices, per_device(): lax.all_to_all(wanted, 'seq', split_axis=0, concat_axis=0, tiled=True)  18.4 us
    all_to_all x1, starting transfers between devices, per_device(): lax.all_to_all(outgoing.reshape(peers, CAPACITY, width), 'seq', split_axi...  18 us
    pallas_call x1, Pallas kernels, per_device(): call(cross_kernel, [shape((slots, width), BF16)], 9, [pltpu.VMEM((width,...  12.6 us
    pallas_call x1, Pallas kernels, per_device(): call(arrange_kernel, [halves, halves, wide, tall, wide, wide, tall, wide,...  11.8 us
    pallas_call x1, Pallas kernels, per_device(): call(core_kernel, [shape((half, middle), BF16)], 4, [pltpu.VMEM((half, mi...  10.7 us
    pallas_call x1, Pallas kernels, per_device(): call(near_kernel, [wide], 4, flops=6000000000)(query, key, value, early)  10.4 us
  transfers between devices with their start and end apart: 5, of which 3 were waited for; matrix products, arithmetic and copies ran while one was open for 0% of the time, Pallas kernels for 14%

profile of v8, /device:TPU:1, one launch (start us, length us, event | category | flops | bytes accessed | tf_op | source)
XLA Modules:
  0.0 170.2 jit_solution(2756612895936093406)
XLA Ops:
  0.0 1.8 %request_kernel.1 = s32[128,128]{1,0:T(8,128)} custom-call(s32[1,512]{1,0:T(1,128)} %bitcast.16), custom_call_target="tpu_custom_call" | custom-call | bytes 4194304 | tf_op jit(solution)/shard_map/request_kernel/pallas_call | solution.py:334
  1.8 18.4 %all-to-all-start = ((s32[128,1,128]{2,1,0:T(1,128)}), s32[128,1,128]{2,1,0:T(1,128)S(1)}, u32[]{:S(2)}, u32[]{:S(2)}) async-start(s32[128,1,128]{2,1,0:T(1,128)} %bitcast.21), calls=%async_computation | async-start | bytes 131072 | tf_op jit(solution)/shard_map/all_to_all | solution.py:342
  20.3 1.0 copy-done.2
  21.3 0.7 copy-done.4
  22.0 0.7 copy-done.5
  22.7 0.4 norm_kernel.1.normed_ref
  23.1 8.6 %all-to-all-done.asked_ref = s32[128,1,128]{2,1,0:T(1,128)S(1)} async-done(((s32[128,1,128]{2,1,0:T(1,128)}), s32[128,1,128]{2,1,0:T(1,128)S(1)}, u32[]{:S(2)}, u32[]{:S(2)}) %all-to-all-start) | async-done | bytes 65568 | tf_op jit(solution)/shard_map/all_to_all | solution.py:342
  31.7 1.5 pick_kernel.1
  33.2 5.7 %all-to-all-start.1 = ((bf16[128,8,512]{2,1,0:T(8,128)(2,1)}), bf16[128,8,512]{2,1,0:T(8,128)(2,1)S(1)}, u32[]{:S(2)}, u32[]{:S(2)}) async-start(bf16[128,8,512]{2,1,0:T(8,128)(2,1)} %bitcast.5), calls=%async_computation.1 | async-start | bytes 2097152 | tf_op jit(solution)/shard_map/all_to_all | solution.py:358
  39.0 1.4 copy-done.1
  40.4 0.9 setup_kernel.1
  41.3 1.0 copy-done.7
  42.3 0.8 copy-done.9
  43.1 26.3 %all-to-all-done.1 = bf16[128,8,512]{2,1,0:T(8,128)(2,1)S(1)} async-done(((bf16[128,8,512]{2,1,0:T(8,128)(2,1)}), bf16[128,8,512]{2,1,0:T(8,128)(2,1)S(1)}, u32[]{:S(2)}, u32[]{:S(2)}) %all-to-all-start.1) | async-done | bytes 1048608 | tf_op jit(solution)/shard_map/all_to_all | solution.py:358
  69.4 11.8 %arrange_kernel.1 = (bf16[256,512]{1,0:T(8,128)(2,1)S(1)}, bf16[256,512]{1,0:T(8,128)(2,1)S(1)}, bf16[256,512]{1,0:T(8,128)(2,1)S(1)}, bf16[512,256]{1,0:T(8,128...) custom-call(bf16[1024,512]{1,0:T(8,128)(2,1)S(1)} %bitcast.13, ...), custom_call_target="tpu_custom_call" | custom-call | bytes 4194304 | tf_op jit(solution)/shard_map/arrange_kernel/pallas_call | solution.py:374
  81.2 1.9 %collective-permute-start = (bf16[256,512]{1,0:T(8,128)(2,1)S(1)}, bf16[256,512]{1,0:T(8,128)(2,1)S(1)}, u32[]{:S(2)}, u32[]{:S(2)}) collective-permute-start(bf16[256,512]{1,0:T(8,128)(2,1)S(1)} %get-tuple-element.40), channel_id=1, source_target_pairs={{0,127},{1,2},{2,1},{3,4},{4,3},{5,6},{6,5},{7,8},{8,7},{9,10},{10... | collective-permute-start | bytes 786440 | tf_op jit(solution)/shard_map/ppermute | solution.py:377
  83.1 3.3 %collective-permute-start.1 = (bf16[256,512]{1,0:T(8,128)(2,1)S(1)}, bf16[256,512]{1,0:T(8,128)(2,1)S(1)}, u32[]{:S(2)}, u32[]{:S(2)}) collective-permute-start(bf16[256,512]{1,0:T(8,128)(2,1)S(1)} %get-tuple-element.45), channel_id=1, source_target_pairs={{0,1},{1,0},{2,3},{3,2},{4,5},{5,4},{6,7},{7,6},{8,9},{9,8},{10,11... | collective-permute-start | bytes 786440 | tf_op jit(solution)/shard_map/ppermute | solution.py:378
  86.4 10.4 %near_kernel.1.near_ref = bf16[256,512]{1,0:T(8,128)(2,1)S(1)} custom-call(bf16[256,512]{1,0:T(8,128)(2,1)S(1)} %get-tuple-element.41.query_ref, bf16[512,256]{1,0:T(8,128)(2,1)S(1)} %get-tuple-element.42.key_ref, bf16[256,512]{1,0:T(8,128)(2,1)S(1)} %get-tuple-element.43.value_ref, bf16[128,512]{1,0:T(8,128)(2,1)S(1)} %get-tuple-element.44.early_ref), custom_call_target="tpu_custom_call" | custom-call | flops 6000000000 | bytes 4194304 | tf_op jit(solution)/shard_map/near_kernel/pallas_call | solution.py:379
  96.9 10.7 %core_kernel.1.core_ref = bf16[256,256]{1,0:T(8,128)(2,1)S(1)} custom-call(bf16[256,512]{1,0:T(8,128)(2,1)S(1)} %collective-permute-done.1.received_ref, bf16[256,512]{1,0:T(8,128)(2,1)S(1)} %get-tuple-element.46.far_query_ref, bf16[512,256]{1,0:T(8,128)(2,1)S(1)} %get-tuple-element.47.far_key_ref, bf16[256,512]{1,0:T(8,128)(2,1)S(1)} %get-tuple-element.48.far_value_ref), custom_call_target="tpu_custom_call" | custom-call | flops 3000000000 | bytes 4194304 | tf_op jit(solution)/shard_map/core_kernel/pallas_call | solution.py:381
  107.6 12.6 %cross_kernel.1 = bf16[1024,512]{1,0:T(8,128)(2,1)} custom-call(bf16[256,512]{1,0:T(8,128)(2,1)S(1)} %collective-permute-done.received_ref, bf16[256,512]{1,0:T(8,128)(2,1)S(1)} %near_kernel.1.near_ref, bf16[256,256]{1,0:T(8,128)(2,1)S(1)} %core_kernel.1.core_ref, bf16[256,512]{1,0:T(8,128)(2,1)S(1)} %get-tuple-element.46.far_query_ref, ...), custom_call_target="tpu_custom_call" | custom-call | flops 6000000000 | bytes 4194304 | tf_op jit(solution)/shard_map/cross_kernel/pallas_call | solution.py:388
  120.2 18.0 %all-to-all-start.2 = ((bf16[128,8,512]{2,1,0:T(8,128)(2,1)}), bf16[128,8,512]{2,1,0:T(8,128)(2,1)S(1)}, u32[]{:S(2)}, u32[]{:S(2)}) async-start(bf16[128,8,512]{2,1,0:T(8,128)(2,1)} %bitcast.10), calls=%async_computation.2 | async-start | bytes 2097152 | tf_op jit(solution)/shard_map/all_to_all | solution.py:398
  138.2 0.6 place_setup_kernel.1.onehot_ref
  138.8 29.8 %all-to-all-done.2 = bf16[128,8,512]{2,1,0:T(8,128)(2,1)S(1)} async-done(((bf16[128,8,512]{2,1,0:T(8,128)(2,1)}), bf16[128,8,512]{2,1,0:T(8,128)(2,1)S(1)}, u32[]{:S(2)}, u32[]{:S(2)}) %all-to-all-start.2) | async-done | bytes 1048608 | tf_op jit(solution)/shard_map/all_to_all | solution.py:398
  168.7 1.4 place_kernel.1
  (21 shorter events, 0.1 us)
Async XLA Ops:
  1.8 29.9 %all-to-all-start = ((s32[128,1,128]{2,1,0:T(1,128)}), s32[128,1,128]{2,1,0:T(1,128)S(1)}, u32[]{:S(2)}, u32[]{:S(2)}) async-start(s32[128,1,128]{2,1,0:T(1,128)} %bitcast.21), calls=%async_computation | async-start | bytes 131072 | tf_op jit(solution)/shard_map/all_to_all | solution.py:342
  20.2 1.0 copy-start.2
  21.3 0.7 copy-start.4
  22.0 0.7 copy-start.5
  23.1 15.9 %copy-start.11 = (f32[1536]{0:T(1024)S(1)}, f32[1536]{0:T(1024)}, u32[]{:S(2)}) copy-start(f32[1536]{0:T(1024)} %param.13) | copy-start | bytes 18436
  23.1 15.9 %copy-start = (s32[512]{0:T(512)S(1)}, s32[512]{0:T(512)}, u32[]{:S(2)}) copy-start(s32[512]{0:T(512)} %param.9) | copy-start | bytes 6148
  23.1 15.9 %copy-start.3 = (bf16[512,512]{1,0:T(8,128)(2,1)S(1)}, bf16[512,512]{1,0:T(8,128)(2,1)}, u32[]{:S(2)}) copy-start(bf16[512,512]{1,0:T(8,128)(2,1)} %proj_weight_ref) | copy-start | bytes 1572868
  23.1 15.9 %copy-start.6 = (f32[512]{0:T(512)S(1)}, f32[512]{0:T(512)}, u32[]{:S(2)}) copy-start(f32[512]{0:T(512)} %param.15) | copy-start | bytes 6148
  33.2 36.2 %all-to-all-start.1 = ((bf16[128,8,512]{2,1,0:T(8,128)(2,1)}), bf16[128,8,512]{2,1,0:T(8,128)(2,1)S(1)}, u32[]{:S(2)}, u32[]{:S(2)}) async-start(bf16[128,8,512]{2,1,0:T(8,128)(2,1)} %bitcast.5), calls=%async_computation.1 | async-start | bytes 2097152 | tf_op jit(solution)/shard_map/all_to_all | solution.py:358
  39.0 1.4 copy-start.1
  41.3 1.0 copy-start.7
  42.3 0.8 copy-start.9
  81.2 26.4 %collective-permute-start = (bf16[256,512]{1,0:T(8,128)(2,1)S(1)}, bf16[256,512]{1,0:T(8,128)(2,1)S(1)}, u32[]{:S(2)}, u32[]{:S(2)}) collective-permute-start(bf16[256,512]{1,0:T(8,128)(2,1)S(1)} %get-tuple-element.40), channel_id=1, source_target_pairs={{0,127},{1,2},{2,1},{3,4},{4,3},{5,6},{6,5},{7,8},{8,7},{9,10},{10... | collective-permute-start | bytes 786440 | tf_op jit(solution)/shard_map/ppermute | solution.py:377
  83.1 13.7 %collective-permute-start.1 = (bf16[256,512]{1,0:T(8,128)(2,1)S(1)}, bf16[256,512]{1,0:T(8,128)(2,1)S(1)}, u32[]{:S(2)}, u32[]{:S(2)}) collective-permute-start(bf16[256,512]{1,0:T(8,128)(2,1)S(1)} %get-tuple-element.45), channel_id=1, source_target_pairs={{0,1},{1,0},{2,3},{3,2},{4,5},{5,4},{6,7},{7,6},{8,9},{9,8},{10,11... | collective-permute-start | bytes 786440 | tf_op jit(solution)/shard_map/ppermute | solution.py:378
  96.8 10.7 %copy-start.8 = (bf16[1024,512]{1,0:T(8,128)(2,1)S(1)}, bf16[1024,512]{1,0:T(8,128)(2,1)}, u32[]{:S(2)}) copy-start(bf16[1024,512]{1,0:T(8,128)(2,1)} %copy-done.7) | copy-start | bytes 3145732
  96.8 10.7 %copy-start.10 = (bf16[512,512]{1,0:T(8,128)(2,1)S(1)}, bf16[512,512]{1,0:T(8,128)(2,1)}, u32[]{:S(2)}) copy-start(bf16[512,512]{1,0:T(8,128)(2,1)} %copy-done.9) | copy-start | bytes 1572868
  120.2 48.5 %all-to-all-start.2 = ((bf16[128,8,512]{2,1,0:T(8,128)(2,1)}), bf16[128,8,512]{2,1,0:T(8,128)(2,1)S(1)}, u32[]{:S(2)}, u32[]{:S(2)}) async-start(bf16[128,8,512]{2,1,0:T(8,128)(2,1)} %bitcast.10), calls=%async_computation.2 | async-start | bytes 2097152 | tf_op jit(solution)/shard_map/all_to_all | solution.py:398

commit v9 on v7

--- a/solution.py
+++ b/solution.py
@@ -52,10 +52,11 @@
     order_row = order_s[...]
     _, mine_bf, rank_row = ranks(order_row, peers, before)
     local = jnp.bitwise_and(order_row, rows - 1) + 1
-    chosen = iota((LANES, rows), 0) == rank_row
+    chosen = iota((2 * CAPACITY, rows), 0) == rank_row
     high = jnp.where(chosen, jnp.right_shift(local, 4).astype(F32), 0.0).astype(BF16)
     low = jnp.where(chosen, jnp.bitwise_and(local, 15).astype(F32), 0.0).astype(BF16)
-    wanted_ref[...] = (dot_nt(mine_bf, high) * 16.0 + dot_nt(mine_bf, low)).astype(jnp.int32)
+    wanted = (dot_nt(mine_bf, high) * 16.0 + dot_nt(mine_bf, low)).astype(jnp.int32)
+    wanted_ref[...] = jnp.concatenate([wanted, jnp.zeros((peers, LANES - wanted.shape[1]), jnp.int32)], axis=1)
 
 
 def column(row, count):
@@ -150,10 +151,9 @@
 
 
 def arrange_kernel(
-    arrived_ref, columns_ref, query_t_ref, key_ref, value_t_ref, key_bias_ref,
-    cross_ref, core_ref, query_ref, key_out_ref, value_ref, far_query_ref, far_key_ref, far_value_ref,
+    arrived_ref, columns_ref, key_ref, value_t_ref, key_bias_ref, cross_ref, core_ref, seq_ref, far_key_ref, far_value_ref,
 ):
-    half, rows = query_ref.shape
+    rows, half = far_key_ref.shape
     middle, slots = rows // 2, arrived_ref.shape[0]
     arrived = arrived_ref[...]
     parts = []
@@ -161,18 +161,14 @@
         slot = columns_ref[part, 3:4].astype(jnp.int32)
         parts.append(dot(onehot_of(slot == iota((middle, slots), 1)), arrived).astype(BF16))
     seq = jnp.concatenate(parts, axis=0)
-    keys = (dot(seq, key_ref[...]) + key_bias_ref[...]).astype(BF16)
-    values = (dot_nt(value_t_ref[...], seq) + columns_ref[:, 1:2]).astype(BF16)
+    seq_ref[...] = seq
+    keys = (dot(seq, key_ref[:, half:]) + key_bias_ref[:, half:]).astype(BF16)
+    values = (dot_nt(value_t_ref[half:], seq) + columns_ref[half:, 1:2]).astype(BF16)
     for ref, part in ((cross_ref, slice(0, middle)), (core_ref, slice(middle, rows))):
-        ref[:, :half] = keys[part, half:]
-        ref[:, half:] = values[half:, part]
-    key_out_ref[...] = keys[:, :half]
-    far_key_ref[...] = keys[:, half:]
-    value_ref[...] = values[:half]
-    far_value_ref[...] = values[half:]
-    queries = (dot_nt(query_t_ref[...], seq) + columns_ref[:, 0:1]).astype(BF16)
-    query_ref[...] = queries[:half]
-    far_query_ref[...] = queries[half:]
+        ref[:, :half] = keys[part]
+        ref[:, half:] = values[:, part]
+    far_key_ref[...] = keys
+    far_value_ref[...] = values
 
 
 def attend(queries_ref, sides, out_ref, out_start):
@@ -235,11 +231,20 @@
         lax.fori_loop(0, heads, one_head, 0)
 
 
-def near_kernel(query_ref, key_ref, value_ref, attended_ref):
-    rows = query_ref.shape[1]
+def near_kernel(
+    seq_ref, columns_ref, query_t_ref, key_ref, value_t_ref, key_bias_ref,
+    attended_ref, far_query_ref, query_s, key_s, value_s,
+):
+    half, rows = query_s.shape
     middle = rows // 2
-    sides = [(key_ref, value_ref, 0, middle), (key_ref, value_ref, middle, rows)]
-    attend(query_ref, sides, attended_ref, 0)
+    seq = seq_ref[...]
+    queries = (dot_nt(query_t_ref[...], seq) + columns_ref[:, 0:1]).astype(BF16)
+    query_s[...] = queries[:half]
+    far_query_ref[...] = queries[half:]
+    key_s[...] = (dot(seq, key_ref[:, :half]) + key_bias_ref[:, :half]).astype(BF16)
+    value_s[...] = (dot_nt(value_t_ref[:half], seq) + columns_ref[:half, 1:2]).astype(BF16)
+    sides = [(key_s, value_s, 0, middle), (key_s, value_s, middle, rows)]
+    attend(query_s, sides, attended_ref, 0)
 
 
 def extend(received_ref, own, far_key_ref, far_value_ref, key_s, value_s):
@@ -347,13 +352,15 @@
     )(order.reshape(1, rows), qkv_weight, qkv_bias.reshape(1, 3 * width), proj_weight, proj_bias.reshape(1, width))
     halves = shape((middle, width), BF16)
     wide, tall = shape((half, rows), BF16), shape((rows, half), BF16)
-    cross, core, query, key, value, far_query, far_key, far_value = call(
-        arrange_kernel, [halves, halves, wide, tall, wide, wide, tall, wide], 6
-    )(arrived.reshape(slots, width), columns, query_t, key_weight, value_t, key_bias)
+    cross, core, seq, far_key, far_value = call(
+        arrange_kernel, [halves, halves, shape((rows, width), BF16), tall, wide], 5
+    )(arrived.reshape(slots, width), columns, key_weight, value_t, key_bias)
     cross = lax.ppermute(cross, "seq", [(i, (i + 2 * (i % 2) - 1) % peers) for i in range(peers)])
     core = lax.ppermute(core, "seq", [(i, i + 1 - 2 * (i % 2)) for i in range(peers)])
-    near = call(near_kernel, [wide], 3, flops=6_000_000_000)(query, key, value)
     patch_s = [pltpu.VMEM((rows, half), BF16), pltpu.VMEM((half, rows), BF16)]
+    near, far_query = call(
+        near_kernel, [wide, wide], 6, [pltpu.VMEM((half, rows), BF16), *patch_s], flops=6_000_000_000
+    )(seq, columns, query_t, key_weight, value_t, key_bias)
     core_attended = call(
         core_kernel,
         [shape((half, middle), BF16)],

time: 161 us -> 161 us (level)
  transfers between devices with their start and end apart: 5 -> 5, of which waited for: 3 -> 3; matrix products, arithmetic and copies ran while one was open for 0% -> 0% of each run, Pallas kernels for 20% -> 21%
where the time goes in v9:
time: 161 us; the launch traced here: 160 us
  waiting for transfers between devices  64.7 us (40%)
  Pallas kernels  51.8 us (32%)
  starting transfers between devices  37.8 us (23%)
  local copies, waits for them, and re-layouts  5.6 us (3%)
    all_to_all x1, waiting for transfers between devices, per_device(): lax.all_to_all(outgoing.reshape(peers, CAPACITY, width), 'seq', split_axi...  29.8 us
    all_to_all x1, waiting for transfers between devices, per_device(): lax.all_to_all(picked.reshape(peers, CAPACITY, width), 'seq', split_axis=...  26.3 us
    pallas_call x1, Pallas kernels, per_device(): call(near_kernel, [wide, wide], 6, [pltpu.VMEM((half, rows), BF16), *patc...  20.8 us
    all_to_all x1, starting transfers between devices, per_device(): lax.all_to_all(wanted, 'seq', split_axis=0, concat_axis=0, tiled=True)  18.4 us
    pallas_call x1, Pallas kernels, per_device(): call(cross_kernel, [shape((slots, width), BF16)], 9, [pltpu.VMEM((width,...  12.6 us
    pallas_call x1, Pallas kernels, per_device(): call(core_kernel, [shape((half, middle), BF16)], 4, [pltpu.VMEM((half, mi...  10.7 us
    all_to_all x1, waiting for transfers between devices, per_device(): lax.all_to_all(wanted, 'seq', split_axis=0, concat_axis=0, tiled=True)  8.57 us
    all_to_all x1, starting transfers between devices, per_device(): lax.all_to_all(outgoing.reshape(peers, CAPACITY, width), 'seq', split_axi...  7.99 us
  transfers between devices with their start and end apart: 5, of which 3 were waited for; matrix products, arithmetic and copies ran while one was open for 0% of the time, Pallas kernels for 21%

profile of v9, /device:TPU:1, one launch (start us, length us, event | category | flops | bytes accessed | tf_op | source)
XLA Modules:
  0.0 160.3 jit_solution(16793111027475563247)
XLA Ops:
  0.0 1.8 %request_kernel.1 = s32[128,128]{1,0:T(8,128)} custom-call(s32[1,512]{1,0:T(1,128)} %bitcast.16), custom_call_target="tpu_custom_call" | custom-call | bytes 4194304 | tf_op jit(solution)/shard_map/request_kernel/pallas_call | solution.py:316
  1.8 18.4 %all-to-all-start = ((s32[128,1,128]{2,1,0:T(1,128)}), s32[128,1,128]{2,1,0:T(1,128)S(1)}, u32[]{:S(2)}, u32[]{:S(2)}) async-start(s32[128,1,128]{2,1,0:T(1,128)} %bitcast.21), calls=%async_computation | async-start | bytes 131072 | tf_op jit(solution)/shard_map/all_to_all | solution.py:324
  20.2 1.0 copy-done.2
  21.3 0.7 copy-done.4
  21.9 0.7 copy-done.5
  22.6 0.4 norm_kernel.1.normed_ref
  23.1 8.6 %all-to-all-done.asked_ref = s32[128,1,128]{2,1,0:T(1,128)S(1)} async-done(((s32[128,1,128]{2,1,0:T(1,128)}), s32[128,1,128]{2,1,0:T(1,128)S(1)}, u32[]{:S(2)}, u32[]{:S(2)}) %all-to-all-start) | async-done | bytes 65568 | tf_op jit(solution)/shard_map/all_to_all | solution.py:324
  31.7 1.5 pick_kernel.1
  33.2 5.7 %all-to-all-start.1 = ((bf16[128,8,512]{2,1,0:T(8,128)(2,1)}), bf16[128,8,512]{2,1,0:T(8,128)(2,1)S(1)}, u32[]{:S(2)}, u32[]{:S(2)}) async-start(bf16[128,8,512]{2,1,0:T(8,128)(2,1)} %bitcast.5), calls=%async_computation.1 | async-start | bytes 2097152 | tf_op jit(solution)/shard_map/all_to_all | solution.py:340
  39.0 1.4 copy-done.1
  40.4 0.9 setup_kernel.1
  41.3 1.0 copy-done.7
  42.3 0.8 copy-done.9
  43.1 26.3 %all-to-all-done.1 = bf16[128,8,512]{2,1,0:T(8,128)(2,1)S(1)} async-done(((bf16[128,8,512]{2,1,0:T(8,128)(2,1)}), bf16[128,8,512]{2,1,0:T(8,128)(2,1)S(1)}, u32[]{:S(2)}, u32[]{:S(2)}) %all-to-all-start.1) | async-done | bytes 1048608 | tf_op jit(solution)/shard_map/all_to_all | solution.py:340
  69.4 1.1 arrange_kernel.1
  70.4 3.7 %collective-permute-start = (bf16[256,512]{1,0:T(8,128)(2,1)S(1)}, bf16[256,512]{1,0:T(8,128)(2,1)S(1)}, u32[]{:S(2)}, u32[]{:S(2)}) collective-permute-start(bf16[256,512]{1,0:T(8,128)(2,1)S(1)} %get-tuple-element.37), channel_id=1, source_target_pairs={{0,127},{1,2},{2,1},{3,4},{4,3},{5,6},{6,5},{7,8},{8,7},{9,10},{10... | collective-permute-start | bytes 786440 | tf_op jit(solution)/shard_map/ppermute | solution.py:358
  74.1 1.9 %collective-permute-start.1 = (bf16[256,512]{1,0:T(8,128)(2,1)S(1)}, bf16[256,512]{1,0:T(8,128)(2,1)S(1)}, u32[]{:S(2)}, u32[]{:S(2)}) collective-permute-start(bf16[256,512]{1,0:T(8,128)(2,1)S(1)} %get-tuple-element.41), channel_id=1, source_target_pairs={{0,1},{1,0},{2,3},{3,2},{4,5},{5,4},{6,7},{7,6},{8,9},{9,8},{10,11... | collective-permute-start | bytes 786440 | tf_op jit(solution)/shard_map/ppermute | solution.py:359
  76.1 20.8 %near_kernel.1 = (bf16[256,512]{1,0:T(8,128)(2,1)S(1)}, bf16[256,512]{1,0:T(8,128)(2,1)S(1)}) custom-call(bf16[512,512]{1,0:T(8,128)(2,1)S(1)} %get-tuple-element.38.seq_ref, f32[512,128]{1,0:T(8,128)S(1)} %get-tuple-element.33.columns_ref, bf16[512,512]{1,0:T(8,128)(2,1)S(1)} %copy-done.10, bf16[512,512]{1,0:T(8,128)(2,1)S(1)} %get-tuple-element.34.key_ref, ...), custom_call_target="tpu_custom_call" | custom-call | flops 6000000000 | bytes 4194304 | tf_op jit(solution)/shard_map/near_kernel/pallas_call | solution.py:361
  96.9 10.7 %core_kernel.1.core_ref = bf16[256,256]{1,0:T(8,128)(2,1)S(1)} custom-call(bf16[256,512]{1,0:T(8,128)(2,1)S(1)} %collective-permute-done.1.received_ref, bf16[256,512]{1,0:T(8,128)(2,1)S(1)} %get-tuple-element.42.far_query_ref, bf16[512,256]{1,0:T(8,128)(2,1)S(1)} %get-tuple-element.43.far_key_ref, bf16[256,512]{1,0:T(8,128)(2,1)S(1)} %get-tuple-element.44.far_value_ref), custom_call_target="tpu_custom_call" | custom-call | flops 3000000000 | bytes 4194304 | tf_op jit(solution)/shard_map/core_kernel/pallas_call | solution.py:364
  107.6 12.6 %cross_kernel.1 = bf16[1024,512]{1,0:T(8,128)(2,1)} custom-call(bf16[256,512]{1,0:T(8,128)(2,1)S(1)} %collective-permute-done.received_ref, bf16[256,512]{1,0:T(8,128)(2,1)S(1)} %get-tuple-element.40.near_ref, bf16[256,256]{1,0:T(8,128)(2,1)S(1)} %core_kernel.1.core_ref, bf16[256,512]{1,0:T(8,128)(2,1)S(1)} %get-tuple-element.42.far_query_ref, ...), custom_call_target="tpu_custom_call" | custom-call | flops 6000000000 | bytes 4194304 | tf_op jit(solution)/shard_map/cross_kernel/pallas_call | solution.py:371
  120.2 8.0 %all-to-all-start.2 = ((bf16[128,8,512]{2,1,0:T(8,128)(2,1)}), bf16[128,8,512]{2,1,0:T(8,128)(2,1)S(1)}, u32[]{:S(2)}, u32[]{:S(2)}) async-start(bf16[128,8,512]{2,1,0:T(8,128)(2,1)} %bitcast.10), calls=%async_computation.2 | async-start | bytes 2097152 | tf_op jit(solution)/shard_map/all_to_all | solution.py:381
  128.2 0.6 place_setup_kernel.1.onehot_ref
  128.9 29.8 %all-to-all-done.2 = bf16[128,8,512]{2,1,0:T(8,128)(2,1)S(1)} async-done(((bf16[128,8,512]{2,1,0:T(8,128)(2,1)}), bf16[128,8,512]{2,1,0:T(8,128)(2,1)S(1)}, u32[]{:S(2)}, u32[]{:S(2)}) %all-to-all-start.2) | async-done | bytes 1048608 | tf_op jit(solution)/shard_map/all_to_all | solution.py:381
  158.7 1.4 place_kernel.1
  (21 shorter events, 0.1 us)
Async XLA Ops:
  1.8 29.9 %all-to-all-start = ((s32[128,1,128]{2,1,0:T(1,128)}), s32[128,1,128]{2,1,0:T(1,128)S(1)}, u32[]{:S(2)}, u32[]{:S(2)}) async-start(s32[128,1,128]{2,1,0:T(1,128)} %bitcast.21), calls=%async_computation | async-start | bytes 131072 | tf_op jit(solution)/shard_map/all_to_all | solution.py:324
  20.2 1.0 copy-start.2
  21.3 0.7 copy-start.4
  21.9 0.7 copy-start.5
  23.0 15.9 %copy-start.11 = (f32[1536]{0:T(1024)S(1)}, f32[1536]{0:T(1024)}, u32[]{:S(2)}) copy-start(f32[1536]{0:T(1024)} %param.13) | copy-start | bytes 18436
  23.1 15.9 %copy-start = (s32[512]{0:T(512)S(1)}, s32[512]{0:T(512)}, u32[]{:S(2)}) copy-start(s32[512]{0:T(512)} %param.9) | copy-start | bytes 6148
  23.1 15.9 %copy-start.3 = (bf16[512,512]{1,0:T(8,128)(2,1)S(1)}, bf16[512,512]{1,0:T(8,128)(2,1)}, u32[]{:S(2)}) copy-start(bf16[512,512]{1,0:T(8,128)(2,1)} %proj_weight_ref) | copy-start | bytes 1572868
  23.1 15.9 %copy-start.6 = (f32[512]{0:T(512)S(1)}, f32[512]{0:T(512)}, u32[]{:S(2)}) copy-start(f32[512]{0:T(512)} %param.15) | copy-start | bytes 6148
  33.2 36.2 %all-to-all-start.1 = ((bf16[128,8,512]{2,1,0:T(8,128)(2,1)}), bf16[128,8,512]{2,1,0:T(8,128)(2,1)S(1)}, u32[]{:S(2)}, u32[]{:S(2)}) async-start(bf16[128,8,512]{2,1,0:T(8,128)(2,1)} %bitcast.5), calls=%async_computation.1 | async-start | bytes 2097152 | tf_op jit(solution)/shard_map/all_to_all | solution.py:340
  39.0 1.4 copy-start.1
  41.3 1.0 copy-start.7
  42.3 0.8 copy-start.9
  69.4 6.7 %copy-start.10 = (bf16[512,512]{1,0:T(8,128)(2,1)S(1)}, bf16[512,512]{1,0:T(8,128)(2,1)}, u32[]{:S(2)}) copy-start(bf16[512,512]{1,0:T(8,128)(2,1)} %copy-done.9) | copy-start | bytes 1572868
  70.4 37.2 %collective-permute-start = (bf16[256,512]{1,0:T(8,128)(2,1)S(1)}, bf16[256,512]{1,0:T(8,128)(2,1)S(1)}, u32[]{:S(2)}, u32[]{:S(2)}) collective-permute-start(bf16[256,512]{1,0:T(8,128)(2,1)S(1)} %get-tuple-element.37), channel_id=1, source_target_pairs={{0,127},{1,2},{2,1},{3,4},{4,3},{5,6},{6,5},{7,8},{8,7},{9,10},{10... | collective-permute-start | bytes 786440 | tf_op jit(solution)/shard_map/ppermute | solution.py:358
  74.1 22.7 %collective-permute-start.1 = (bf16[256,512]{1,0:T(8,128)(2,1)S(1)}, bf16[256,512]{1,0:T(8,128)(2,1)S(1)}, u32[]{:S(2)}, u32[]{:S(2)}) collective-permute-start(bf16[256,512]{1,0:T(8,128)(2,1)S(1)} %get-tuple-element.41), channel_id=1, source_target_pairs={{0,1},{1,0},{2,3},{3,2},{4,5},{5,4},{6,7},{7,6},{8,9},{9,8},{10,11... | collective-permute-start | bytes 786440 | tf_op jit(solution)/shard_map/ppermute | solution.py:359
  96.9 10.7 %copy-start.8 = (bf16[1024,512]{1,0:T(8,128)(2,1)S(1)}, bf16[1024,512]{1,0:T(8,128)(2,1)}, u32[]{:S(2)}) copy-start(bf16[1024,512]{1,0:T(8,128)(2,1)} %copy-done.7) | copy-start | bytes 3145732
  120.2 38.4 %all-to-all-start.2 = ((bf16[128,8,512]{2,1,0:T(8,128)(2,1)}), bf16[128,8,512]{2,1,0:T(8,128)(2,1)S(1)}, u32[]{:S(2)}, u32[]{:S(2)}) async-start(bf16[128,8,512]{2,1,0:T(8,128)(2,1)} %bitcast.10), calls=%async_computation.2 | async-start | bytes 2097152 | tf_op jit(solution)/shard_map/all_to_all | solution.py:381

commit v10 on v9

--- a/solution.py
+++ b/solution.py
@@ -115,7 +115,8 @@
 
 def setup_kernel(
     order_ref, qkv_weight_ref, qkv_bias_ref, proj_weight_ref, proj_bias_ref,
-    send_ref, query_t_ref, key_ref, value_t_ref, proj_t_ref, columns_ref, key_bias_ref,
+    arrange_ref, send_ref, query_t_ref, near_key_ref, far_key_ref, near_value_t_ref, far_value_t_ref, proj_t_ref,
+    columns_ref, key_bias_ref,
 ):
     slots, rows = send_ref.shape
     peers = slots // CAPACITY
@@ -125,16 +126,20 @@
     swapped = jnp.concatenate([slot[:, rows // 2 :], slot[:, : rows // 2]], axis=1)
     slot = jnp.where(jnp.bitwise_and(lax.axis_index("seq"), 1) == 1, swapped, slot)
     send_ref[...] = onehot_of(iota((slots, rows), 0) == slot)
+    slot_col = column(slot.astype(F32), rows).astype(jnp.int32)
+    arrange_ref[...] = onehot_of(slot_col[:, :1] == iota((rows, slots), 1))
+    half = width // 2
     query_t_ref[...] = jnp.transpose(qkv_weight_ref[:, :width])
-    key_ref[...] = qkv_weight_ref[:, width : 2 * width]
-    value_t_ref[...] = jnp.transpose(qkv_weight_ref[:, 2 * width :])
+    near_key_ref[...] = qkv_weight_ref[:, width : width + half]
+    far_key_ref[...] = qkv_weight_ref[:, width + half : 2 * width]
+    near_value_t_ref[...] = jnp.transpose(qkv_weight_ref[:, 2 * width : 2 * width + half])
+    far_value_t_ref[...] = jnp.transpose(qkv_weight_ref[:, 2 * width + half :])
     proj_t_ref[...] = jnp.transpose(proj_weight_ref[...])
     key_bias_ref[...] = qkv_bias_ref[:, width : 2 * width]
     place = iota((LANES, width), 0)
     packed = jnp.where(place == 0, qkv_bias_ref[:, :width], 0.0)
     packed = jnp.where(place == 1, qkv_bias_ref[:, 2 * width :], packed)
     packed = jnp.where(place == 2, proj_bias_ref[...], packed)
-    packed = jnp.where(place == 3, slot.astype(F32), packed)
     columns_ref[...] = jnp.transpose(packed)
 
 
@@ -151,19 +156,15 @@
 
 
 def arrange_kernel(
-    arrived_ref, columns_ref, key_ref, value_t_ref, key_bias_ref, cross_ref, core_ref, seq_ref, far_key_ref, far_value_ref,
+    arrived_ref, onehot_ref, columns_ref, key_ref, value_t_ref, key_bias_ref,
+    cross_ref, core_ref, seq_ref, far_key_ref, far_value_ref,
 ):
     rows, half = far_key_ref.shape
-    middle, slots = rows // 2, arrived_ref.shape[0]
-    arrived = arrived_ref[...]
-    parts = []
-    for part in (slice(0, middle), slice(middle, rows)):
-        slot = columns_ref[part, 3:4].astype(jnp.int32)
-        parts.append(dot(onehot_of(slot == iota((middle, slots), 1)), arrived).astype(BF16))
-    seq = jnp.concatenate(parts, axis=0)
+    middle = rows // 2
+    seq = dot(onehot_ref[...], arrived_ref[...]).astype(BF16)
     seq_ref[...] = seq
-    keys = (dot(seq, key_ref[:, half:]) + key_bias_ref[:, half:]).astype(BF16)
-    values = (dot_nt(value_t_ref[half:], seq) + columns_ref[half:, 1:2]).astype(BF16)
+    keys = (dot(seq, key_ref[...]) + key_bias_ref[:, half:]).astype(BF16)
+    values = (dot_nt(value_t_ref[...], seq) + columns_ref[half:, 1:2]).astype(BF16)
     for ref, part in ((cross_ref, slice(0, middle)), (core_ref, slice(middle, rows))):
         ref[:, :half] = keys[part]
         ref[:, half:] = values[:, part]
@@ -241,8 +242,8 @@
     queries = (dot_nt(query_t_ref[...], seq) + columns_ref[:, 0:1]).astype(BF16)
     query_s[...] = queries[:half]
     far_query_ref[...] = queries[half:]
-    key_s[...] = (dot(seq, key_ref[:, :half]) + key_bias_ref[:, :half]).astype(BF16)
-    value_s[...] = (dot_nt(value_t_ref[:half], seq) + columns_ref[:half, 1:2]).astype(BF16)
+    key_s[...] = (dot(seq, key_ref[...]) + key_bias_ref[:, :half]).astype(BF16)
+    value_s[...] = (dot_nt(value_t_ref[...], seq) + columns_ref[:half, 1:2]).astype(BF16)
     sides = [(key_s, value_s, 0, middle), (key_s, value_s, middle, rows)]
     attend(query_s, sides, attended_ref, 0)
 
@@ -341,26 +342,27 @@
         picked.reshape(peers, CAPACITY, width), "seq", split_axis=0, concat_axis=0, tiled=True
     )
     square = shape((width, width), BF16)
-    send, query_t, key_weight, value_t, proj_t, columns, key_bias = call(
+    wide, tall = shape((half, rows), BF16), shape((rows, half), BF16)
+    key_shape, value_shape = shape((width, half), BF16), shape((half, width), BF16)
+    arrange, send, query_t, near_key, key_weight, near_value_t, value_t, proj_t, columns, key_bias = call(
         setup_kernel,
         [
-            shape((slots, rows), BF16), square, square, square, square, shape((width, LANES), F32),
-            shape((1, width), F32),
+            shape((rows, slots), BF16), shape((slots, rows), BF16), square, key_shape, key_shape, value_shape,
+            value_shape, square, shape((width, LANES), F32), shape((1, width), F32),
         ],
         5,
         flops=8_000_000_000,
     )(order.reshape(1, rows), qkv_weight, qkv_bias.reshape(1, 3 * width), proj_weight, proj_bias.reshape(1, width))
     halves = shape((middle, width), BF16)
-    wide, tall = shape((half, rows), BF16), shape((rows, half), BF16)
     cross, core, seq, far_key, far_value = call(
-        arrange_kernel, [halves, halves, shape((rows, width), BF16), tall, wide], 5
-    )(arrived.reshape(slots, width), columns, key_weight, value_t, key_bias)
+        arrange_kernel, [halves, halves, shape((rows, width), BF16), tall, wide], 6
+    )(arrived.reshape(slots, width), arrange, columns, key_weight, value_t, key_bias)
     cross = lax.ppermute(cross, "seq", [(i, (i + 2 * (i % 2) - 1) % peers) for i in range(peers)])
     core = lax.ppermute(core, "seq", [(i, i + 1 - 2 * (i % 2)) for i in range(peers)])
     patch_s = [pltpu.VMEM((rows, half), BF16), pltpu.VMEM((half, rows), BF16)]
     near, far_query = call(
         near_kernel, [wide, wide], 6, [pltpu.VMEM((half, rows), BF16), *patch_s], flops=6_000_000_000
-    )(seq, columns, query_t, key_weight, value_t, key_bias)
+    )(seq, columns, query_t, near_key, near_value_t, key_bias)
     core_attended = call(
         core_kernel,
         [shape((half, middle), BF16)],

time: 161 us -> 161 us (level)
  waiting for transfers between devices: 64.7 us -> 61.9 us
  local copies, waits for them, and re-layouts: 5.6 us -> 7.92 us
    all_to_all x1, waiting for transfers between devices: 26.3 us -> 23.5 us  [per_device(): lax.all_to_all(picked.reshape(peers, CAPACITY, width), 'seq', split_axis=...]
    unnamed x24 -> x36, local copies, waits for them, and re-layouts: 5.59 us -> 7.92 us
where the time goes in v10:
time: 161 us; the launch traced here: 160 us
  waiting for transfers between devices  61.9 us (38%)
  Pallas kernels  52.2 us (32%)
  starting transfers between devices  37.8 us (23%)
  local copies, waits for them, and re-layouts  7.92 us (5%)
    all_to_all x1, waiting for transfers between devices, per_device(): lax.all_to_all(outgoing.reshape(peers, CAPACITY, width), 'seq', split_axi...  29.8 us
    all_to_all x1, waiting for transfers between devices, per_device(): lax.all_to_all(picked.reshape(peers, CAPACITY, width), 'seq', split_axis=...  23.5 us
    pallas_call x1, Pallas kernels, per_device(): call(near_kernel, [wide, wide], 6, [pltpu.VMEM((half, rows), BF16), *patc...  20.8 us
    all_to_all x1, starting transfers between devices, per_device(): lax.all_to_all(wanted, 'seq', split_axis=0, concat_axis=0, tiled=True)  18.4 us
    pallas_call x1, Pallas kernels, per_device(): call(cross_kernel, [shape((slots, width), BF16)], 9, [pltpu.VMEM((width,...  12.6 us
    pallas_call x1, Pallas kernels, per_device(): call(core_kernel, [shape((half, middle), BF16)], 4, [pltpu.VMEM((half, mi...  10.7 us
    all_to_all x1, waiting for transfers between devices, per_device(): lax.all_to_all(wanted, 'seq', split_axis=0, concat_axis=0, tiled=True)  8.57 us
    all_to_all x1, starting transfers between devices, per_device(): lax.all_to_all(outgoing.reshape(peers, CAPACITY, width), 'seq', split_axi...  8 us
  transfers between devices with their start and end apart: 5, of which 3 were waited for; matrix products, arithmetic and copies ran while one was open for 0% of the time, Pallas kernels for 21%

profile of v10, /device:TPU:1, one launch (start us, length us, event | category | flops | bytes accessed | tf_op | source)
XLA Modules:
  0.0 160.2 jit_solution(18275908860473769155)
XLA Ops:
  0.0 1.8 %request_kernel.1 = s32[128,128]{1,0:T(8,128)} custom-call(s32[1,512]{1,0:T(1,128)} %bitcast.16), custom_call_target="tpu_custom_call" | custom-call | bytes 4194304 | tf_op jit(solution)/shard_map/request_kernel/pallas_call | solution.py:317
  1.8 18.4 %all-to-all-start = ((s32[128,1,128]{2,1,0:T(1,128)}), s32[128,1,128]{2,1,0:T(1,128)S(1)}, u32[]{:S(2)}, u32[]{:S(2)}) async-start(s32[128,1,128]{2,1,0:T(1,128)} %bitcast.21), calls=%async_computation | async-start | bytes 131072 | tf_op jit(solution)/shard_map/all_to_all | solution.py:325
  20.2 1.0 copy-done.2
  21.3 0.7 copy-done.4
  23.1 8.6 %all-to-all-done.asked_ref = s32[128,1,128]{2,1,0:T(1,128)S(1)} async-done(((s32[128,1,128]{2,1,0:T(1,128)}), s32[128,1,128]{2,1,0:T(1,128)S(1)}, u32[]{:S(2)}, u32[]{:S(2)}) %all-to-all-start) | async-done | bytes 65568 | tf_op jit(solution)/shard_map/all_to_all | solution.py:325
  31.7 1.5 pick_kernel.1
  33.2 5.7 %all-to-all-start.1 = ((bf16[128,8,512]{2,1,0:T(8,128)(2,1)}), bf16[128,8,512]{2,1,0:T(8,128)(2,1)S(1)}, u32[]{:S(2)}, u32[]{:S(2)}) async-start(bf16[128,8,512]{2,1,0:T(8,128)(2,1)} %bitcast.5), calls=%async_computation.1 | async-start | bytes 2097152 | tf_op jit(solution)/shard_map/all_to_all | solution.py:341
  39.0 1.4 copy-done.1
  40.4 1.4 setup_kernel.1
  41.8 1.0 copy-done.7
  42.8 0.8 copy-done.9
  43.6 0.8 copy-done.11
  44.4 0.7 copy-done.13
  45.1 0.7 copy-done.15
  45.8 23.5 %all-to-all-done.1 = bf16[128,8,512]{2,1,0:T(8,128)(2,1)S(1)} async-done(((bf16[128,8,512]{2,1,0:T(8,128)(2,1)}), bf16[128,8,512]{2,1,0:T(8,128)(2,1)S(1)}, u32[]{:S(2)}, u32[]{:S(2)}) %all-to-all-start.1) | async-done | bytes 1048608 | tf_op jit(solution)/shard_map/all_to_all | solution.py:341
  69.3 1.0 arrange_kernel.1
  70.4 3.7 %collective-permute-start = (bf16[256,512]{1,0:T(8,128)(2,1)S(1)}, bf16[256,512]{1,0:T(8,128)(2,1)S(1)}, u32[]{:S(2)}, u32[]{:S(2)}) collective-permute-start(bf16[256,512]{1,0:T(8,128)(2,1)S(1)} %get-tuple-element.41), channel_id=1, source_target_pairs={{0,127},{1,2},{2,1},{3,4},{4,3},{5,6},{6,5},{7,8},{8,7},{9,10},{10... | collective-permute-start | bytes 786440 | tf_op jit(solution)/shard_map/ppermute | solution.py:360
  74.1 1.9 %collective-permute-start.1 = (bf16[256,512]{1,0:T(8,128)(2,1)S(1)}, bf16[256,512]{1,0:T(8,128)(2,1)S(1)}, u32[]{:S(2)}, u32[]{:S(2)}) collective-permute-start(bf16[256,512]{1,0:T(8,128)(2,1)S(1)} %get-tuple-element.47), channel_id=1, source_target_pairs={{0,1},{1,0},{2,3},{3,2},{4,5},{5,4},{6,7},{7,6},{8,9},{9,8},{10,11... | collective-permute-start | bytes 786440 | tf_op jit(solution)/shard_map/ppermute | solution.py:361
  76.0 20.8 %near_kernel.1 = (bf16[256,512]{1,0:T(8,128)(2,1)S(1)}, bf16[256,512]{1,0:T(8,128)(2,1)S(1)}) custom-call(bf16[512,512]{1,0:T(8,128)(2,1)S(1)} %get-tuple-element.42.seq_ref, f32[512,128]{1,0:T(8,128)S(1)} %get-tuple-element.37.columns_ref, bf16[512,512]{1,0:T(8,128)(2,1)S(1)} %copy-done.12, bf16[512,256]{1,0:T(8,128)(2,1)S(1)} %copy-done.14, ...), custom_call_target="tpu_custom_call" | custom-call | flops 6000000000 | bytes 4194304 | tf_op jit(solution)/shard_map/near_kernel/pallas_call | solution.py:363
  96.9 10.7 %core_kernel.1.core_ref = bf16[256,256]{1,0:T(8,128)(2,1)S(1)} custom-call(bf16[256,512]{1,0:T(8,128)(2,1)S(1)} %collective-permute-done.1.received_ref, bf16[256,512]{1,0:T(8,128)(2,1)S(1)} %get-tuple-element.48.far_query_ref, bf16[512,256]{1,0:T(8,128)(2,1)S(1)} %get-tuple-element.49.far_key_ref, bf16[256,512]{1,0:T(8,128)(2,1)S(1)} %get-tuple-element.50.far_value_ref), custom_call_target="tpu_custom_call" | custom-call | flops 3000000000 | bytes 4194304 | tf_op jit(solution)/shard_map/core_kernel/pallas_call | solution.py:366
  107.6 12.6 %cross_kernel.1 = bf16[1024,512]{1,0:T(8,128)(2,1)} custom-call(bf16[256,512]{1,0:T(8,128)(2,1)S(1)} %collective-permute-done.received_ref, bf16[256,512]{1,0:T(8,128)(2,1)S(1)} %get-tuple-element.46.near_ref, bf16[256,256]{1,0:T(8,128)(2,1)S(1)} %core_kernel.1.core_ref, bf16[256,512]{1,0:T(8,128)(2,1)S(1)} %get-tuple-element.48.far_query_ref, ...), custom_call_target="tpu_custom_call" | custom-call | flops 6000000000 | bytes 4194304 | tf_op jit(solution)/shard_map/cross_kernel/pallas_call | solution.py:373
  120.2 8.0 %all-to-all-start.2 = ((bf16[128,8,512]{2,1,0:T(8,128)(2,1)}), bf16[128,8,512]{2,1,0:T(8,128)(2,1)S(1)}, u32[]{:S(2)}, u32[]{:S(2)}) async-start(bf16[128,8,512]{2,1,0:T(8,128)(2,1)} %bitcast.10), calls=%async_computation.2 | async-start | bytes 2097152 | tf_op jit(solution)/shard_map/all_to_all | solution.py:383
  128.8 29.8 %all-to-all-done.2 = bf16[128,8,512]{2,1,0:T(8,128)(2,1)S(1)} async-done(((bf16[128,8,512]{2,1,0:T(8,128)(2,1)}), bf16[128,8,512]{2,1,0:T(8,128)(2,1)S(1)}, u32[]{:S(2)}, u32[]{:S(2)}) %all-to-all-start.2) | async-done | bytes 1048608 | tf_op jit(solution)/shard_map/all_to_all | solution.py:383
  158.7 1.4 place_kernel.1
  (33 shorter events, 1.8 us)
Async XLA Ops:
  1.8 29.9 %all-to-all-start = ((s32[128,1,128]{2,1,0:T(1,128)}), s32[128,1,128]{2,1,0:T(1,128)S(1)}, u32[]{:S(2)}, u32[]{:S(2)}) async-start(s32[128,1,128]{2,1,0:T(1,128)} %bitcast.21), calls=%async_computation | async-start | bytes 131072 | tf_op jit(solution)/shard_map/all_to_all | solution.py:325
  20.2 1.0 copy-start.2
  21.3 0.7 copy-start.4
  21.9 0.7 copy-start.5
  23.0 15.9 %copy-start.17 = (f32[1536]{0:T(1024)S(1)}, f32[1536]{0:T(1024)}, u32[]{:S(2)}) copy-start(f32[1536]{0:T(1024)} %param.13) | copy-start | bytes 18436
  23.1 15.9 %copy-start = (s32[512]{0:T(512)S(1)}, s32[512]{0:T(512)}, u32[]{:S(2)}) copy-start(s32[512]{0:T(512)} %param.9) | copy-start | bytes 6148
  23.1 15.9 %copy-start.3 = (bf16[512,512]{1,0:T(8,128)(2,1)S(1)}, bf16[512,512]{1,0:T(8,128)(2,1)}, u32[]{:S(2)}) copy-start(bf16[512,512]{1,0:T(8,128)(2,1)} %proj_weight_ref) | copy-start | bytes 1572868
  23.1 15.9 %copy-start.6 = (f32[512]{0:T(512)S(1)}, f32[512]{0:T(512)}, u32[]{:S(2)}) copy-start(f32[512]{0:T(512)} %param.15) | copy-start | bytes 6148
  33.2 36.2 %all-to-all-start.1 = ((bf16[128,8,512]{2,1,0:T(8,128)(2,1)}), bf16[128,8,512]{2,1,0:T(8,128)(2,1)S(1)}, u32[]{:S(2)}, u32[]{:S(2)}) async-start(bf16[128,8,512]{2,1,0:T(8,128)(2,1)} %bitcast.5), calls=%async_computation.1 | async-start | bytes 2097152 | tf_op jit(solution)/shard_map/all_to_all | solution.py:341
  39.0 1.4 copy-start.1
  41.8 1.0 copy-start.7
  42.8 0.8 copy-start.9
  43.6 0.8 copy-start.11
  44.4 0.7 copy-start.13
  45.1 0.7 copy-start.15
  69.3 6.7 %copy-start.12 = (bf16[512,512]{1,0:T(8,128)(2,1)S(1)}, bf16[512,512]{1,0:T(8,128)(2,1)}, u32[]{:S(2)}) copy-start(bf16[512,512]{1,0:T(8,128)(2,1)} %copy-done.11) | copy-start | bytes 1572868
  69.3 6.7 %copy-start.14 = (bf16[512,256]{1,0:T(8,128)(2,1)S(1)}, bf16[512,256]{1,0:T(8,128)(2,1)}, u32[]{:S(2)}) copy-start(bf16[512,256]{1,0:T(8,128)(2,1)} %copy-done.13) | copy-start | bytes 786436
  69.3 6.7 %copy-start.16 = (bf16[256,512]{1,0:T(8,128)(2,1)S(1)}, bf16[256,512]{1,0:T(8,128)(2,1)}, u32[]{:S(2)}) copy-start(bf16[256,512]{1,0:T(8,128)(2,1)} %copy-done.15) | copy-start | bytes 786436
  70.4 37.2 %collective-permute-start = (bf16[256,512]{1,0:T(8,128)(2,1)S(1)}, bf16[256,512]{1,0:T(8,128)(2,1)S(1)}, u32[]{:S(2)}, u32[]{:S(2)}) collective-permute-start(bf16[256,512]{1,0:T(8,128)(2,1)S(1)} %get-tuple-element.41), channel_id=1, source_target_pairs={{0,127},{1,2},{2,1},{3,4},{4,3},{5,6},{6,5},{7,8},{8,7},{9,10},{10... | collective-permute-start | bytes 786440 | tf_op jit(solution)/shard_map/ppermute | solution.py:360
  74.1 22.8 %collective-permute-start.1 = (bf16[256,512]{1,0:T(8,128)(2,1)S(1)}, bf16[256,512]{1,0:T(8,128)(2,1)S(1)}, u32[]{:S(2)}, u32[]{:S(2)}) collective-permute-start(bf16[256,512]{1,0:T(8,128)(2,1)S(1)} %get-tuple-element.47), channel_id=1, source_target_pairs={{0,1},{1,0},{2,3},{3,2},{4,5},{5,4},{6,7},{7,6},{8,9},{9,8},{10,11... | collective-permute-start | bytes 786440 | tf_op jit(solution)/shard_map/ppermute | solution.py:361
  96.8 10.7 %copy-start.8 = (bf16[1024,512]{1,0:T(8,128)(2,1)S(1)}, bf16[1024,512]{1,0:T(8,128)(2,1)}, u32[]{:S(2)}) copy-start(bf16[1024,512]{1,0:T(8,128)(2,1)} %copy-done.7) | copy-start | bytes 3145732
  96.8 10.7 %copy-start.10 = (bf16[512,512]{1,0:T(8,128)(2,1)S(1)}, bf16[512,512]{1,0:T(8,128)(2,1)}, u32[]{:S(2)}) copy-start(bf16[512,512]{1,0:T(8,128)(2,1)} %copy-done.9) | copy-start | bytes 1572868
  120.2 38.4 %all-to-all-start.2 = ((bf16[128,8,512]{2,1,0:T(8,128)(2,1)}), bf16[128,8,512]{2,1,0:T(8,128)(2,1)S(1)}, u32[]{:S(2)}, u32[]{:S(2)}) async-start(bf16[128,8,512]{2,1,0:T(8,128)(2,1)} %bitcast.10), calls=%async_computation.2 | async-start | bytes 2097152 | tf_op jit(solution)/shard_map/all_to_all | solution.py:383

commit v11 on v10

--- a/solution.py
+++ b/solution.py
@@ -256,27 +256,38 @@
     value_s[:, middle:] = far_value_ref[:, own]
 
 
-def core_kernel(received_ref, far_query_ref, far_key_ref, far_value_ref, attended_ref, query_s, key_s, value_s):
+def project(near, far, proj_t_ref, columns_ref):
+    half = near.shape[0]
+    total = dot(proj_t_ref[:, :half], near) + dot(proj_t_ref[:, half:], far)
+    return (total + columns_ref[:, 2:3]).astype(BF16)
+
+
+def core_kernel(
+    received_ref, near_ref, far_query_ref, far_key_ref, far_value_ref, proj_t_ref, columns_ref, send_ref,
+    slots_ref, attended_s, query_s, key_s, value_s,
+):
     middle = received_ref.shape[0]
     own = slice(middle, 2 * middle)
     extend(received_ref, own, far_key_ref, far_value_ref, key_s, value_s)
     query_s[...] = far_query_ref[:, own]
-    attend(query_s, [(key_s, value_s, 0, middle)], attended_ref, 0)
+    attend(query_s, [(key_s, value_s, 0, middle)], attended_s, 0)
+    update = project(near_ref[:, own], attended_s[...], proj_t_ref, columns_ref)
+    slots_ref[...] = dot_nt(send_ref[:, own], update).astype(BF16)
 
 
 def cross_kernel(
     received_ref, near_ref, core_ref, far_query_ref, far_key_ref, far_value_ref, proj_t_ref, columns_ref, send_ref,
     outgoing_ref, attended_s, key_s, value_s, stage, sems,
 ):
-    middle, half = received_ref.shape[0], near_ref.shape[0]
-    extend(received_ref, slice(0, middle), far_key_ref, far_value_ref, key_s, value_s)
-    attended_s[:half] = near_ref[...]
-    attended_s[half:, middle:] = core_ref[...]
-    attend(far_query_ref, [(key_s, value_s, 0, middle)], attended_s, half)
-    update = (dot(proj_t_ref[...], attended_s[...]) + columns_ref[:, 2:3]).astype(BF16)
+    middle = received_ref.shape[0]
+    own = slice(0, middle)
+    extend(received_ref, own, far_key_ref, far_value_ref, key_s, value_s)
+    attend(far_query_ref, [(key_s, value_s, 0, middle)], attended_s, 0)
+    update = project(near_ref[:, own], attended_s[...], proj_t_ref, columns_ref)
 
     def make(chunk, size):
-        return dot_nt(send_ref[chunk * size : (chunk + 1) * size], update).astype(BF16)
+        part = slice(chunk * size, (chunk + 1) * size)
+        return (dot_nt(send_ref[part, own], update) + core_ref[part].astype(F32)).astype(BF16)
 
     send_chunks(make, outgoing_ref, stage, sems)
 
@@ -363,21 +374,22 @@
     near, far_query = call(
         near_kernel, [wide, wide], 6, [pltpu.VMEM((half, rows), BF16), *patch_s], flops=6_000_000_000
     )(seq, columns, query_t, near_key, near_value_t, key_bias)
-    core_attended = call(
+    quarter_s = pltpu.VMEM((half, middle), BF16)
+    core_slots = call(
         core_kernel,
-        [shape((half, middle), BF16)],
-        4,
-        [pltpu.VMEM((half, middle), BF16), *patch_s],
+        [shape((slots, width), BF16)],
+        8,
+        [quarter_s, quarter_s, *patch_s],
         flops=3_000_000_000,
-    )(core, far_query, far_key, far_value)
+    )(core, near, far_query, far_key, far_value, proj_t, columns, send)
     outgoing = call(
         cross_kernel,
         [shape((slots, width), BF16)],
         9,
-        [pltpu.VMEM((width, rows), BF16), *patch_s, *staging],
+        [quarter_s, *patch_s, *staging],
         flops=6_000_000_000,
         out_hbm=True,
-    )(cross, near, core_attended, far_query, far_key, far_value, proj_t, columns, send)
+    )(cross, near, core_slots, far_query, far_key, far_value, proj_t, columns, send)
     outgoing, asked = lax.optimization_barrier((outgoing, asked))
     place = call(place_setup_kernel, [shape((rows, slots), BF16)], 1, flops=2_000_000_000)(asked)
     returned = lax.all_to_all(

time: 161 us -> 161 us (level)
  transfers between devices with their start and end apart: 5 -> 5, of which waited for: 3 -> 3; matrix products, arithmetic and copies ran while one was open for 0% -> 0% of each run, Pallas kernels for 21% -> 22%
where the time goes in v11:
time: 161 us
  waiting for transfers between devices  61.9 us (38%)
  Pallas kernels  52.7 us (33%)
  starting transfers between devices  37.8 us (23%)
  local copies, waits for them, and re-layouts  7.92 us (5%)
    all_to_all x1, waiting for transfers between devices, per_device(): lax.all_to_all(outgoing.reshape(peers, CAPACITY, width), 'seq', split_axi...  29.8 us
    all_to_all x1, waiting for transfers between devices, per_device(): lax.all_to_all(picked.reshape(peers, CAPACITY, width), 'seq', split_axis=...  23.5 us
    pallas_call x1, Pallas kernels, per_device(): call(near_kernel, [wide, wide], 6, [pltpu.VMEM((half, rows), BF16), *patc...  20.8 us
    all_to_all x1, starting transfers between devices, per_device(): lax.all_to_all(wanted, 'seq', split_axis=0, concat_axis=0, tiled=True)  18.4 us
    pallas_call x1, Pallas kernels, per_device(): call(cross_kernel, [shape((slots, width), BF16)], 9, [quarter_s, *patch_s...  12.4 us
    pallas_call x1, Pallas kernels, per_device(): call(core_kernel, [shape((slots, width), BF16)], 8, [quarter_s, quarter_s...  11.4 us
    all_to_all x1, waiting for transfers between devices, per_device(): lax.all_to_all(wanted, 'seq', split_axis=0, concat_axis=0, tiled=True)  8.57 us
    all_to_all x1, starting transfers between devices, per_device(): lax.all_to_all(outgoing.reshape(peers, CAPACITY, width), 'seq', split_axi...  7.99 us
  transfers between devices with their start and end apart: 5, of which 3 were waited for; matrix products, arithmetic and copies ran while one was open for 0% of the time, Pallas kernels for 22%

profile of v11, /device:TPU:1, one launch (start us, length us, event | category | flops | bytes accessed | tf_op | source)
XLA Modules:
  0.0 160.8 jit_solution(10326889977625465980)
XLA Ops:
  0.0 1.8 %request_kernel.1 = s32[128,128]{1,0:T(8,128)} custom-call(s32[1,512]{1,0:T(1,128)} %bitcast.16), custom_call_target="tpu_custom_call" | custom-call | bytes 4194304 | tf_op jit(solution)/shard_map/request_kernel/pallas_call | solution.py:328
  1.8 18.4 %all-to-all-start = ((s32[128,1,128]{2,1,0:T(1,128)}), s32[128,1,128]{2,1,0:T(1,128)S(1)}, u32[]{:S(2)}, u32[]{:S(2)}) async-start(s32[128,1,128]{2,1,0:T(1,128)} %bitcast.21), calls=%async_computation | async-start | bytes 131072 | tf_op jit(solution)/shard_map/all_to_all | solution.py:336
  20.2 1.0 copy-done.2
  21.3 0.7 copy-done.4
  23.1 8.6 %all-to-all-done.asked_ref = s32[128,1,128]{2,1,0:T(1,128)S(1)} async-done(((s32[128,1,128]{2,1,0:T(1,128)}), s32[128,1,128]{2,1,0:T(1,128)S(1)}, u32[]{:S(2)}, u32[]{:S(2)}) %all-to-all-start) | async-done | bytes 65568 | tf_op jit(solution)/shard_map/all_to_all | solution.py:336
  31.7 1.5 pick_kernel.1
  33.2 5.7 %all-to-all-start.1 = ((bf16[128,8,512]{2,1,0:T(8,128)(2,1)}), bf16[128,8,512]{2,1,0:T(8,128)(2,1)S(1)}, u32[]{:S(2)}, u32[]{:S(2)}) async-start(bf16[128,8,512]{2,1,0:T(8,128)(2,1)} %bitcast.5), calls=%async_computation.1 | async-start | bytes 2097152 | tf_op jit(solution)/shard_map/all_to_all | solution.py:352
  39.0 1.4 copy-done.1
  40.4 1.4 setup_kernel.1
  41.8 1.0 copy-done.7
  42.8 0.8 copy-done.9
  43.6 0.8 copy-done.11
  44.4 0.7 copy-done.13
  45.1 0.7 copy-done.15
  45.8 23.5 %all-to-all-done.1 = bf16[128,8,512]{2,1,0:T(8,128)(2,1)S(1)} async-done(((bf16[128,8,512]{2,1,0:T(8,128)(2,1)}), bf16[128,8,512]{2,1,0:T(8,128)(2,1)S(1)}, u32[]{:S(2)}, u32[]{:S(2)}) %all-to-all-start.1) | async-done | bytes 1048608 | tf_op jit(solution)/shard_map/all_to_all | solution.py:352
  69.3 1.0 arrange_kernel.1
  70.4 3.7 %collective-permute-start = (bf16[256,512]{1,0:T(8,128)(2,1)S(1)}, bf16[256,512]{1,0:T(8,128)(2,1)S(1)}, u32[]{:S(2)}, u32[]{:S(2)}) collective-permute-start(bf16[256,512]{1,0:T(8,128)(2,1)S(1)} %get-tuple-element.41), channel_id=1, source_target_pairs={{0,127},{1,2},{2,1},{3,4},{4,3},{5,6},{6,5},{7,8},{8,7},{9,10},{10... | collective-permute-start | bytes 786440 | tf_op jit(solution)/shard_map/ppermute | solution.py:371
  74.1 1.9 %collective-permute-start.1 = (bf16[256,512]{1,0:T(8,128)(2,1)S(1)}, bf16[256,512]{1,0:T(8,128)(2,1)S(1)}, u32[]{:S(2)}, u32[]{:S(2)}) collective-permute-start(bf16[256,512]{1,0:T(8,128)(2,1)S(1)} %get-tuple-element.47), channel_id=1, source_target_pairs={{0,1},{1,0},{2,3},{3,2},{4,5},{5,4},{6,7},{7,6},{8,9},{9,8},{10,11... | collective-permute-start | bytes 786440 | tf_op jit(solution)/shard_map/ppermute | solution.py:372
  76.0 20.8 %near_kernel.1 = (bf16[256,512]{1,0:T(8,128)(2,1)S(1)}, bf16[256,512]{1,0:T(8,128)(2,1)S(1)}) custom-call(bf16[512,512]{1,0:T(8,128)(2,1)S(1)} %get-tuple-element.42.seq_ref, f32[512,128]{1,0:T(8,128)S(1)} %get-tuple-element.37.columns_ref, bf16[512,512]{1,0:T(8,128)(2,1)S(1)} %copy-done.12, bf16[512,256]{1,0:T(8,128)(2,1)S(1)} %copy-done.14, ...), custom_call_target="tpu_custom_call" | custom-call | flops 6000000000 | bytes 4194304 | tf_op jit(solution)/shard_map/near_kernel/pallas_call | solution.py:374
  96.9 11.4 %core_kernel.1.core_ref = bf16[1024,512]{1,0:T(8,128)(2,1)S(1)} custom-call(bf16[256,512]{1,0:T(8,128)(2,1)S(1)} %collective-permute-done.1.received_ref, bf16[256,512]{1,0:T(8,128)(2,1)S(1)} %get-tuple-element.46.near_ref, bf16[256,512]{1,0:T(8,128)(2,1)S(1)} %get-tuple-element.48.far_query_ref, bf16[512,256]{1,0:T(8,128)(2,1)S(1)} %get-tuple-element.49.far_key_ref, ...), custom_call_target="tpu_custom_call" | custom-call | flops 3000000000 | bytes 4194304 | tf_op jit(solution)/shard_map/core_kernel/pallas_call | solution.py:378
  108.3 12.4 %cross_kernel.1 = bf16[1024,512]{1,0:T(8,128)(2,1)} custom-call(bf16[256,512]{1,0:T(8,128)(2,1)S(1)} %collective-permute-done.received_ref, bf16[256,512]{1,0:T(8,128)(2,1)S(1)} %get-tuple-element.46.near_ref, bf16[1024,512]{1,0:T(8,128)(2,1)S(1)} %core_kernel.1.core_ref, bf16[256,512]{1,0:T(8,128)(2,1)S(1)} %get-tuple-element.48.far_query_ref, ...), custom_call_target="tpu_custom_call" | custom-call | flops 6000000000 | bytes 4194304 | tf_op jit(solution)/shard_map/cross_kernel/pallas_call | solution.py:385
  120.8 8.0 %all-to-all-start.2 = ((bf16[128,8,512]{2,1,0:T(8,128)(2,1)}), bf16[128,8,512]{2,1,0:T(8,128)(2,1)S(1)}, u32[]{:S(2)}, u32[]{:S(2)}) async-start(bf16[128,8,512]{2,1,0:T(8,128)(2,1)} %bitcast.10), calls=%async_computation.2 | async-start | bytes 2097152 | tf_op jit(solution)/shard_map/all_to_all | solution.py:395
  129.4 29.8 %all-to-all-done.2 = bf16[128,8,512]{2,1,0:T(8,128)(2,1)S(1)} async-done(((bf16[128,8,512]{2,1,0:T(8,128)(2,1)}), bf16[128,8,512]{2,1,0:T(8,128)(2,1)S(1)}, u32[]{:S(2)}, u32[]{:S(2)}) %all-to-all-start.2) | async-done | bytes 1048608 | tf_op jit(solution)/shard_map/all_to_all | solution.py:395
  159.2 1.4 place_kernel.1
  (33 shorter events, 1.8 us)
Async XLA Ops:
  1.8 29.9 %all-to-all-start = ((s32[128,1,128]{2,1,0:T(1,128)}), s32[128,1,128]{2,1,0:T(1,128)S(1)}, u32[]{:S(2)}, u32[]{:S(2)}) async-start(s32[128,1,128]{2,1,0:T(1,128)} %bitcast.21), calls=%async_computation | async-start | bytes 131072 | tf_op jit(solution)/shard_map/all_to_all | solution.py:336
  20.2 1.0 copy-start.2
  21.3 0.7 copy-start.4
  21.9 0.7 copy-start.5
  23.0 15.9 %copy-start.17 = (f32[1536]{0:T(1024)S(1)}, f32[1536]{0:T(1024)}, u32[]{:S(2)}) copy-start(f32[1536]{0:T(1024)} %param.13) | copy-start | bytes 18436
  23.1 15.9 %copy-start = (s32[512]{0:T(512)S(1)}, s32[512]{0:T(512)}, u32[]{:S(2)}) copy-start(s32[512]{0:T(512)} %param.9) | copy-start | bytes 6148
  23.1 15.9 %copy-start.3 = (bf16[512,512]{1,0:T(8,128)(2,1)S(1)}, bf16[512,512]{1,0:T(8,128)(2,1)}, u32[]{:S(2)}) copy-start(bf16[512,512]{1,0:T(8,128)(2,1)} %proj_weight_ref) | copy-start | bytes 1572868
  23.1 15.9 %copy-start.6 = (f32[512]{0:T(512)S(1)}, f32[512]{0:T(512)}, u32[]{:S(2)}) copy-start(f32[512]{0:T(512)} %param.15) | copy-start | bytes 6148
  33.2 36.2 %all-to-all-start.1 = ((bf16[128,8,512]{2,1,0:T(8,128)(2,1)}), bf16[128,8,512]{2,1,0:T(8,128)(2,1)S(1)}, u32[]{:S(2)}, u32[]{:S(2)}) async-start(bf16[128,8,512]{2,1,0:T(8,128)(2,1)} %bitcast.5), calls=%async_computation.1 | async-start | bytes 2097152 | tf_op jit(solution)/shard_map/all_to_all | solution.py:352
  39.0 1.4 copy-start.1
  41.8 1.0 copy-start.7
  42.8 0.8 copy-start.9
  43.6 0.8 copy-start.11
  44.4 0.7 copy-start.13
  45.1 0.7 copy-start.15
  69.3 6.7 %copy-start.12 = (bf16[512,512]{1,0:T(8,128)(2,1)S(1)}, bf16[512,512]{1,0:T(8,128)(2,1)}, u32[]{:S(2)}) copy-start(bf16[512,512]{1,0:T(8,128)(2,1)} %copy-done.11) | copy-start | bytes 1572868
  69.3 6.7 %copy-start.14 = (bf16[512,256]{1,0:T(8,128)(2,1)S(1)}, bf16[512,256]{1,0:T(8,128)(2,1)}, u32[]{:S(2)}) copy-start(bf16[512,256]{1,0:T(8,128)(2,1)} %copy-done.13) | copy-start | bytes 786436
  69.3 6.7 %copy-start.16 = (bf16[256,512]{1,0:T(8,128)(2,1)S(1)}, bf16[256,512]{1,0:T(8,128)(2,1)}, u32[]{:S(2)}) copy-start(bf16[256,512]{1,0:T(8,128)(2,1)} %copy-done.15) | copy-start | bytes 786436
  70.4 38.0 %collective-permute-start = (bf16[256,512]{1,0:T(8,128)(2,1)S(1)}, bf16[256,512]{1,0:T(8,128)(2,1)S(1)}, u32[]{:S(2)}, u32[]{:S(2)}) collective-permute-start(bf16[256,512]{1,0:T(8,128)(2,1)S(1)} %get-tuple-element.41), channel_id=1, source_target_pairs={{0,127},{1,2},{2,1},{3,4},{4,3},{5,6},{6,5},{7,8},{8,7},{9,10},{10... | collective-permute-start | bytes 786440 | tf_op jit(solution)/shard_map/ppermute | solution.py:371
  74.1 22.8 %collective-permute-start.1 = (bf16[256,512]{1,0:T(8,128)(2,1)S(1)}, bf16[256,512]{1,0:T(8,128)(2,1)S(1)}, u32[]{:S(2)}, u32[]{:S(2)}) collective-permute-start(bf16[256,512]{1,0:T(8,128)(2,1)S(1)} %get-tuple-element.47), channel_id=1, source_target_pairs={{0,1},{1,0},{2,3},{3,2},{4,5},{5,4},{6,7},{7,6},{8,9},{9,8},{10,11... | collective-permute-start | bytes 786440 | tf_op jit(solution)/shard_map/ppermute | solution.py:372
  76.0 20.8 %copy-start.8 = (bf16[1024,512]{1,0:T(8,128)(2,1)S(1)}, bf16[1024,512]{1,0:T(8,128)(2,1)}, u32[]{:S(2)}) copy-start(bf16[1024,512]{1,0:T(8,128)(2,1)} %copy-done.7) | copy-start | bytes 3145732
  76.0 20.9 %copy-start.10 = (bf16[512,512]{1,0:T(8,128)(2,1)S(1)}, bf16[512,512]{1,0:T(8,128)(2,1)}, u32[]{:S(2)}) copy-start(bf16[512,512]{1,0:T(8,128)(2,1)} %copy-done.9) | copy-start | bytes 1572868
  120.8 38.4 %all-to-all-start.2 = ((bf16[128,8,512]{2,1,0:T(8,128)(2,1)}), bf16[128,8,512]{2,1,0:T(8,128)(2,1)S(1)}, u32[]{:S(2)}, u32[]{:S(2)}) async-start(bf16[128,8,512]{2,1,0:T(8,128)(2,1)} %bitcast.10), calls=%async_computation.2 | async-start | bytes 2097152 | tf_op jit(solution)/shard_map/all_to_all | solution.py:395

commit v12 on v10

--- a/solution.py
+++ b/solution.py
@@ -256,24 +256,21 @@
     value_s[:, middle:] = far_value_ref[:, own]
 
 
-def core_kernel(received_ref, far_query_ref, far_key_ref, far_value_ref, attended_ref, query_s, key_s, value_s):
-    middle = received_ref.shape[0]
-    own = slice(middle, 2 * middle)
-    extend(received_ref, own, far_key_ref, far_value_ref, key_s, value_s)
-    query_s[...] = far_query_ref[:, own]
-    attend(query_s, [(key_s, value_s, 0, middle)], attended_ref, 0)
-
-
-def cross_kernel(
-    received_ref, near_ref, core_ref, far_query_ref, far_key_ref, far_value_ref, proj_t_ref, columns_ref, send_ref,
+def far_kernel(
+    cross_ref, core_ref, near_ref, far_query_ref, far_key_ref, far_value_ref, proj_t_ref, columns_ref, send_ref,
     outgoing_ref, attended_s, key_s, value_s, stage, sems,
 ):
-    middle, half = received_ref.shape[0], near_ref.shape[0]
-    extend(received_ref, slice(0, middle), far_key_ref, far_value_ref, key_s, value_s)
-    attended_s[:half] = near_ref[...]
-    attended_s[half:, middle:] = core_ref[...]
-    attend(far_query_ref, [(key_s, value_s, 0, middle)], attended_s, half)
-    update = (dot(proj_t_ref[...], attended_s[...]) + columns_ref[:, 2:3]).astype(BF16)
+    half, rows = far_query_ref.shape
+    middle = rows // 2
+    sides = []
+    for side, received_ref in enumerate((cross_ref, core_ref)):
+        begin, end = side * middle, (side + 1) * middle
+        keys, values = key_s.at[side], value_s.at[side]
+        extend(received_ref, slice(begin, end), far_key_ref, far_value_ref, keys, values)
+        sides.append((keys, values, begin, end))
+    attend(far_query_ref, sides, attended_s, 0)
+    total = dot(proj_t_ref[:, :half], near_ref[...]) + dot(proj_t_ref[:, half:], attended_s[...])
+    update = (total + columns_ref[:, 2:3]).astype(BF16)
 
     def make(chunk, size):
         return dot_nt(send_ref[chunk * size : (chunk + 1) * size], update).astype(BF16)
@@ -363,21 +360,17 @@
     near, far_query = call(
         near_kernel, [wide, wide], 6, [pltpu.VMEM((half, rows), BF16), *patch_s], flops=6_000_000_000
     )(seq, columns, query_t, near_key, near_value_t, key_bias)
-    core_attended = call(
-        core_kernel,
-        [shape((half, middle), BF16)],
-        4,
-        [pltpu.VMEM((half, middle), BF16), *patch_s],
-        flops=3_000_000_000,
-    )(core, far_query, far_key, far_value)
     outgoing = call(
-        cross_kernel,
+        far_kernel,
         [shape((slots, width), BF16)],
         9,
-        [pltpu.VMEM((width, rows), BF16), *patch_s, *staging],
+        [
+            pltpu.VMEM((half, rows), BF16), pltpu.VMEM((2, rows, half), BF16), pltpu.VMEM((2, half, rows), BF16),
+            *staging,
+        ],
         flops=6_000_000_000,
         out_hbm=True,
-    )(cross, near, core_attended, far_query, far_key, far_value, proj_t, columns, send)
+    )(cross, core, near, far_query, far_key, far_value, proj_t, columns, send)
     outgoing, asked = lax.optimization_barrier((outgoing, asked))
     place = call(place_setup_kernel, [shape((rows, slots), BF16)], 1, flops=2_000_000_000)(asked)
     returned = lax.all_to_all(

time: 161 us -> 159 us (0.988)
    pallas_call x2 -> x1, Pallas kernels: 23.3 us -> 22 us  [per_device(): call(far_kernel, [shape((slots, width), BF16)], 9, [pltpu.VMEM((half, row...]
  transfers between devices with their start and end apart: 5 -> 5, of which waited for: 3 -> 3; matrix products, arithmetic and copies ran while one was open for 0% -> 0% of each run, Pallas kernels for 21% -> 15%
where the time goes in v12:
time: 159 us
  waiting for transfers between devices  61.9 us (39%)
  Pallas kernels  50.9 us (32%)
  starting transfers between devices  37.8 us (24%)
  local copies, waits for them, and re-layouts  7.91 us (5%)
    all_to_all x1, waiting for transfers between devices, per_device(): lax.all_to_all(outgoing.reshape(peers, CAPACITY, width), 'seq', split_axi...  29.8 us
    all_to_all x1, waiting for transfers between devices, per_device(): lax.all_to_all(picked.reshape(peers, CAPACITY, width), 'seq', split_axis=...  23.5 us
    pallas_call x1, Pallas kernels, per_device(): call(far_kernel, [shape((slots, width), BF16)], 9, [pltpu.VMEM((half, row...  22 us
    pallas_call x1, Pallas kernels, per_device(): call(near_kernel, [wide, wide], 6, [pltpu.VMEM((half, rows), BF16), *patc...  20.8 us
    all_to_all x1, starting transfers between devices, per_device(): lax.all_to_all(wanted, 'seq', split_axis=0, concat_axis=0, tiled=True)  18.4 us
    all_to_all x1, waiting for transfers between devices, per_device(): lax.all_to_all(wanted, 'seq', split_axis=0, concat_axis=0, tiled=True)  8.57 us
    all_to_all x1, starting transfers between devices, per_device(): lax.all_to_all(outgoing.reshape(peers, CAPACITY, width), 'seq', split_axi...  7.99 us
    unnamed x36, local copies, waits for them, and re-layouts  7.9 us
  transfers between devices with their start and end apart: 5, of which 3 were waited for; matrix products, arithmetic and copies ran while one was open for 0% of the time, Pallas kernels for 15%

profile of v12, /device:TPU:1, one launch (start us, length us, event | category | flops | bytes accessed | tf_op | source)
XLA Modules:
  0.0 158.9 jit_solution(588357765256331952)
XLA Ops:
  0.0 1.8 %request_kernel.1 = s32[128,128]{1,0:T(8,128)} custom-call(s32[1,512]{1,0:T(1,128)} %bitcast.16), custom_call_target="tpu_custom_call" | custom-call | bytes 4194304 | tf_op jit(solution)/shard_map/request_kernel/pallas_call | solution.py:314
  1.8 18.4 %all-to-all-start = ((s32[128,1,128]{2,1,0:T(1,128)}), s32[128,1,128]{2,1,0:T(1,128)S(1)}, u32[]{:S(2)}, u32[]{:S(2)}) async-start(s32[128,1,128]{2,1,0:T(1,128)} %bitcast.21), calls=%async_computation | async-start | bytes 131072 | tf_op jit(solution)/shard_map/all_to_all | solution.py:322
  20.2 1.0 copy-done.2
  21.3 0.7 copy-done.4
  21.9 0.7 copy-done.5
  23.1 8.6 %all-to-all-done.asked_ref = s32[128,1,128]{2,1,0:T(1,128)S(1)} async-done(((s32[128,1,128]{2,1,0:T(1,128)}), s32[128,1,128]{2,1,0:T(1,128)S(1)}, u32[]{:S(2)}, u32[]{:S(2)}) %all-to-all-start) | async-done | bytes 65568 | tf_op jit(solution)/shard_map/all_to_all | solution.py:322
  31.7 1.5 pick_kernel.1
  33.2 5.7 %all-to-all-start.1 = ((bf16[128,8,512]{2,1,0:T(8,128)(2,1)}), bf16[128,8,512]{2,1,0:T(8,128)(2,1)S(1)}, u32[]{:S(2)}, u32[]{:S(2)}) async-start(bf16[128,8,512]{2,1,0:T(8,128)(2,1)} %bitcast.5), calls=%async_computation.1 | async-start | bytes 2097152 | tf_op jit(solution)/shard_map/all_to_all | solution.py:338
  39.0 1.4 copy-done.1
  40.4 1.4 setup_kernel.1
  41.8 1.0 copy-done.7
  42.8 0.8 copy-done.9
  43.6 0.8 copy-done.11
  44.4 0.7 copy-done.13
  45.1 0.7 copy-done.15
  45.8 23.5 %all-to-all-done.1 = bf16[128,8,512]{2,1,0:T(8,128)(2,1)S(1)} async-done(((bf16[128,8,512]{2,1,0:T(8,128)(2,1)}), bf16[128,8,512]{2,1,0:T(8,128)(2,1)S(1)}, u32[]{:S(2)}, u32[]{:S(2)}) %all-to-all-start.1) | async-done | bytes 1048608 | tf_op jit(solution)/shard_map/all_to_all | solution.py:338
  69.3 1.0 arrange_kernel.1
  70.4 3.7 %collective-permute-start = (bf16[256,512]{1,0:T(8,128)(2,1)S(1)}, bf16[256,512]{1,0:T(8,128)(2,1)S(1)}, u32[]{:S(2)}, u32[]{:S(2)}) collective-permute-start(bf16[256,512]{1,0:T(8,128)(2,1)S(1)} %get-tuple-element.41), channel_id=1, source_target_pairs={{0,127},{1,2},{2,1},{3,4},{4,3},{5,6},{6,5},{7,8},{8,7},{9,10},{10... | collective-permute-start | bytes 786440 | tf_op jit(solution)/shard_map/ppermute | solution.py:357
  74.1 1.9 %collective-permute-start.1 = (bf16[256,512]{1,0:T(8,128)(2,1)S(1)}, bf16[256,512]{1,0:T(8,128)(2,1)S(1)}, u32[]{:S(2)}, u32[]{:S(2)}) collective-permute-start(bf16[256,512]{1,0:T(8,128)(2,1)S(1)} %get-tuple-element.42), channel_id=1, source_target_pairs={{0,1},{1,0},{2,3},{3,2},{4,5},{5,4},{6,7},{7,6},{8,9},{9,8},{10,11... | collective-permute-start | bytes 786440 | tf_op jit(solution)/shard_map/ppermute | solution.py:358
  76.0 20.8 %near_kernel.1 = (bf16[256,512]{1,0:T(8,128)(2,1)S(1)}, bf16[256,512]{1,0:T(8,128)(2,1)S(1)}) custom-call(bf16[512,512]{1,0:T(8,128)(2,1)S(1)} %get-tuple-element.43.seq_ref, f32[512,128]{1,0:T(8,128)S(1)} %get-tuple-element.37.columns_ref, bf16[512,512]{1,0:T(8,128)(2,1)S(1)} %copy-done.12, bf16[512,256]{1,0:T(8,128)(2,1)S(1)} %copy-done.14, ...), custom_call_target="tpu_custom_call" | custom-call | flops 6000000000 | bytes 4194304 | tf_op jit(solution)/shard_map/near_kernel/pallas_call | solution.py:360
  96.9 22.0 %far_kernel.1 = bf16[1024,512]{1,0:T(8,128)(2,1)} custom-call(bf16[256,512]{1,0:T(8,128)(2,1)S(1)} %collective-permute-done.cross_ref, bf16[256,512]{1,0:T(8,128)(2,1)S(1)} %collective-permute-done.1.core_ref, bf16[256,512]{1,0:T(8,128)(2,1)S(1)} %get-tuple-element.47.near_ref, bf16[256,512]{1,0:T(8,128)(2,1)S(1)} %get-tuple-element.48.far_query_ref, ...), custom_call_target="tpu_custom_call" | custom-call | flops 6000000000 | bytes 4194304 | tf_op jit(solution)/shard_map/far_kernel/pallas_call | solution.py:363
  118.9 8.0 %all-to-all-start.2 = ((bf16[128,8,512]{2,1,0:T(8,128)(2,1)}), bf16[128,8,512]{2,1,0:T(8,128)(2,1)S(1)}, u32[]{:S(2)}, u32[]{:S(2)}) async-start(bf16[128,8,512]{2,1,0:T(8,128)(2,1)} %bitcast.10), calls=%async_computation.2 | async-start | bytes 2097152 | tf_op jit(solution)/shard_map/all_to_all | solution.py:376
  127.5 29.8 %all-to-all-done.2 = bf16[128,8,512]{2,1,0:T(8,128)(2,1)S(1)} async-done(((bf16[128,8,512]{2,1,0:T(8,128)(2,1)}), bf16[128,8,512]{2,1,0:T(8,128)(2,1)S(1)}, u32[]{:S(2)}, u32[]{:S(2)}) %all-to-all-start.2) | async-done | bytes 1048608 | tf_op jit(solution)/shard_map/all_to_all | solution.py:376
  157.3 1.4 place_kernel.1
  (32 shorter events, 1.1 us)
Async XLA Ops:
  1.8 29.9 %all-to-all-start = ((s32[128,1,128]{2,1,0:T(1,128)}), s32[128,1,128]{2,1,0:T(1,128)S(1)}, u32[]{:S(2)}, u32[]{:S(2)}) async-start(s32[128,1,128]{2,1,0:T(1,128)} %bitcast.21), calls=%async_computation | async-start | bytes 131072 | tf_op jit(solution)/shard_map/all_to_all | solution.py:322
  20.2 1.0 copy-start.2
  21.3 0.7 copy-start.4
  21.9 0.7 copy-start.5
  23.0 15.9 %copy-start.17 = (f32[1536]{0:T(1024)S(1)}, f32[1536]{0:T(1024)}, u32[]{:S(2)}) copy-start(f32[1536]{0:T(1024)} %param.13) | copy-start | bytes 18436
  23.1 15.9 %copy-start = (s32[512]{0:T(512)S(1)}, s32[512]{0:T(512)}, u32[]{:S(2)}) copy-start(s32[512]{0:T(512)} %param.9) | copy-start | bytes 6148
  23.1 15.9 %copy-start.3 = (bf16[512,512]{1,0:T(8,128)(2,1)S(1)}, bf16[512,512]{1,0:T(8,128)(2,1)}, u32[]{:S(2)}) copy-start(bf16[512,512]{1,0:T(8,128)(2,1)} %proj_weight_ref) | copy-start | bytes 1572868
  23.1 15.9 %copy-start.6 = (f32[512]{0:T(512)S(1)}, f32[512]{0:T(512)}, u32[]{:S(2)}) copy-start(f32[512]{0:T(512)} %param.15) | copy-start | bytes 6148
  33.2 36.2 %all-to-all-start.1 = ((bf16[128,8,512]{2,1,0:T(8,128)(2,1)}), bf16[128,8,512]{2,1,0:T(8,128)(2,1)S(1)}, u32[]{:S(2)}, u32[]{:S(2)}) async-start(bf16[128,8,512]{2,1,0:T(8,128)(2,1)} %bitcast.5), calls=%async_computation.1 | async-start | bytes 2097152 | tf_op jit(solution)/shard_map/all_to_all | solution.py:338
  39.0 1.4 copy-start.1
  41.8 1.0 copy-start.7
  42.8 0.8 copy-start.9
  43.6 0.8 copy-start.11
  44.4 0.7 copy-start.13
  45.1 0.7 copy-start.15
  69.3 6.7 %copy-start.12 = (bf16[512,512]{1,0:T(8,128)(2,1)S(1)}, bf16[512,512]{1,0:T(8,128)(2,1)}, u32[]{:S(2)}) copy-start(bf16[512,512]{1,0:T(8,128)(2,1)} %copy-done.11) | copy-start | bytes 1572868
  69.3 6.7 %copy-start.14 = (bf16[512,256]{1,0:T(8,128)(2,1)S(1)}, bf16[512,256]{1,0:T(8,128)(2,1)}, u32[]{:S(2)}) copy-start(bf16[512,256]{1,0:T(8,128)(2,1)} %copy-done.13) | copy-start | bytes 786436
  69.3 6.7 %copy-start.16 = (bf16[256,512]{1,0:T(8,128)(2,1)S(1)}, bf16[256,512]{1,0:T(8,128)(2,1)}, u32[]{:S(2)}) copy-start(bf16[256,512]{1,0:T(8,128)(2,1)} %copy-done.15) | copy-start | bytes 786436
  70.4 26.5 %collective-permute-start = (bf16[256,512]{1,0:T(8,128)(2,1)S(1)}, bf16[256,512]{1,0:T(8,128)(2,1)S(1)}, u32[]{:S(2)}, u32[]{:S(2)}) collective-permute-start(bf16[256,512]{1,0:T(8,128)(2,1)S(1)} %get-tuple-element.41), channel_id=1, source_target_pairs={{0,127},{1,2},{2,1},{3,4},{4,3},{5,6},{6,5},{7,8},{8,7},{9,10},{10... | collective-permute-start | bytes 786440 | tf_op jit(solution)/shard_map/ppermute | solution.py:357
  74.1 22.8 %collective-permute-start.1 = (bf16[256,512]{1,0:T(8,128)(2,1)S(1)}, bf16[256,512]{1,0:T(8,128)(2,1)S(1)}, u32[]{:S(2)}, u32[]{:S(2)}) collective-permute-start(bf16[256,512]{1,0:T(8,128)(2,1)S(1)} %get-tuple-element.42), channel_id=1, source_target_pairs={{0,1},{1,0},{2,3},{3,2},{4,5},{5,4},{6,7},{7,6},{8,9},{9,8},{10,11... | collective-permute-start | bytes 786440 | tf_op jit(solution)/shard_map/ppermute | solution.py:358
  76.0 20.9 %copy-start.8 = (bf16[1024,512]{1,0:T(8,128)(2,1)S(1)}, bf16[1024,512]{1,0:T(8,128)(2,1)}, u32[]{:S(2)}) copy-start(bf16[1024,512]{1,0:T(8,128)(2,1)} %copy-done.7) | copy-start | bytes 3145732
  76.0 20.9 %copy-start.10 = (bf16[512,512]{1,0:T(8,128)(2,1)S(1)}, bf16[512,512]{1,0:T(8,128)(2,1)}, u32[]{:S(2)}) copy-start(bf16[512,512]{1,0:T(8,128)(2,1)} %copy-done.9) | copy-start | bytes 1572868
  118.9 38.4 %all-to-all-start.2 = ((bf16[128,8,512]{2,1,0:T(8,128)(2,1)}), bf16[128,8,512]{2,1,0:T(8,128)(2,1)S(1)}, u32[]{:S(2)}, u32[]{:S(2)}) async-start(bf16[128,8,512]{2,1,0:T(8,128)(2,1)} %bitcast.10), calls=%async_computation.2 | async-start | bytes 2097152 | tf_op jit(solution)/shard_map/all_to_all | solution.py:376
